TPU v7x, 32 devices: a whole 2x2x4 slice. The times are simulated.
32 devices in a mesh: dp: 16 (over z, y, core), fsdp: 2 (over x).
Axes of the slice: x: 2, y: 2, z: 4, core: 2. Of those that a mesh axis runs over, the one named last changes fastest.
Arguments:
- inputs: bfloat16 [32, 512, 768], P('dp', 'fsdp'), may hold values from -6 to 6
- box_coords: int32 [32, 512, 4], P('dp'), may hold values from 0 to 999
- mlm_mask: int32 [32, 512], P('dp', 'fsdp'), may hold values from 0 to 1, as said below
- cotangent: bfloat16 [32, 512, 768], P('dp', 'fsdp'), may hold values from -6 to 6
- params: float32 [7208960], P('fsdp')
- first_moment: float32 [7208960], P('fsdp'), may hold values from -0.15625 to 0.15625
- second_moment: float32 [7208960], P('fsdp'), may hold values from 1e-06 to 0.001
Outputs:
- layer_out: bfloat16 [32, 512, 768], P('dp', 'fsdp')
- input_grad: bfloat16 [32, 512, 768], P('dp', 'fsdp')
- weight_grad: float32 [7208960], P('fsdp')
- grad_norm: float32 [], replicated
- param_update: float32 [7208960], P('fsdp')
- new_first: float32 [7208960], P('fsdp')
Inputs may be any that keep to these rules, and one draw needn't show every extreme that they name: `mlm_mask`: the first token of every document is masked.
All inputs are finite; a program needn't handle non-finite values.
Results may differ from a plain program's by a relative error of at most 0.015.
The roundings to bfloat16 on the way count: a program that leaves them out, or rounds other values in their place, can miss the bound.
Values may be sent and summed in bfloat16 or wider, within the bound.
A program may use at most 256 MiB of HBM per device.

v0:
```python
import functools
import math

import jax
import jax.numpy as jnp
from jax import lax
from jax.sharding import PartitionSpec as P

D = 768
HEADS = 12
HDIM = 64
FF = 3072
BUCKETS = 32
FEAT = 128
LEN = 512
PADDED = 7208960


norm_eps = 1e-05
adam_one = 0.9
adam_two = 0.999
adam_eps = 1e-08
adam_steps = 100.0
decay_rate = 0.01
table_factor = 5.0


def layout_plan():
    return (
        ("w_qkv", (D, 3 * D)),
        ("qv_bias", (2 * D,)),
        ("w_out", (D, D)),
        ("out_bias", (D,)),
        ("gain_one", (D,)),
        ("shift_one", (D,)),
        ("w_up", (D, FF)),
        ("up_bias", (FF,)),
        ("w_down", (FF, D)),
        ("down_bias", (D,)),
        ("gain_two", (D,)),
        ("shift_two", (D,)),
        ("w_layout", (FEAT, D)),
        ("tables", (3, BUCKETS, HEADS)),
    )


def element_count(entry_shape):
    return functools.reduce(lambda running, extent: running * extent, entry_shape, 1)


def unpack(flat_vector):
    segments = {}
    offset = 0
    for entry_name, entry_shape in layout_plan():
        length = element_count(entry_shape)
        segments[entry_name] = flat_vector[offset : offset + length].reshape(entry_shape)
        offset = offset + length
    return segments


def pack(segments):
    flat_parts = [segments[entry_name].reshape(-1) for entry_name, entry_shape in layout_plan()]
    used_count = sum((element_count(entry_shape) for entry_name, entry_shape in layout_plan()))
    flat_parts.append(jnp.zeros((PADDED - used_count,), jnp.float32))
    return jnp.concatenate(flat_parts)


def special_start():
    offset = 0
    for entry_name, entry_shape in layout_plan():
        if entry_name == "w_layout":
            return offset
        offset = offset + element_count(entry_shape)
    return offset


def bucket_of(offsets):
    half_count = BUCKETS // 2
    quarter_count = half_count // 2
    spread = jnp.abs(offsets)
    result = half_count * (offsets > 0).astype(jnp.int32)
    for level_index in range(1, half_count):
        threshold = (
            level_index
            if level_index <= quarter_count
            else quarter_count * 2 ** (level_index - quarter_count)
        )
        result = result + (spread >= threshold).astype(jnp.int32)
    return result


def layout_features(coords):
    freq_count = FEAT // 8
    factors = (jnp.arange(freq_count, dtype=jnp.int32) + 1) ** 2
    phases = coords[..., :, None] * factors % 4096
    angles = phases.astype(jnp.float32) * (2.0 * math.pi / 4096.0)
    wave_parts = jnp.concatenate([jnp.sin(angles), jnp.cos(angles)], axis=-1)
    return wave_parts.reshape(coords.shape[:-1] + (FEAT,))


def adamw(weights_in, grads_in, first_in, second_in, positions):
    rate_scale = jnp.where(positions >= special_start(), table_factor, 1.0)
    first_new = adam_one * first_in + (1.0 - adam_one) * grads_in
    second_new = adam_two * second_in + (1.0 - adam_two) * grads_in * grads_in
    corrected = (
        first_new
        / (1.0 - adam_one**adam_steps)
        / (jnp.sqrt(second_new / (1.0 - adam_two**adam_steps)) + adam_eps)
    )
    return (rate_scale * (corrected + decay_rate * weights_in), first_new)


def standardize(values):
    centered = values - jnp.mean(values, -1, keepdims=True)
    inverse = lax.rsqrt(jnp.mean(centered * centered, -1, keepdims=True) + norm_eps)
    return (centered * inverse, inverse)


def norm_back(normed, inverse, gain_row, grad_rows):
    scaled_grad = grad_rows * gain_row
    result = inverse * (
        scaled_grad
        - jnp.mean(scaled_grad, -1, keepdims=True)
        - normed * jnp.mean(scaled_grad * normed, -1, keepdims=True)
    )
    return (result, jnp.sum(grad_rows * normed, 0), jnp.sum(grad_rows, 0))


def planar_ones(near_pos, far_pos):
    bucket_ids = bucket_of(far_pos[:, None, :] - near_pos[:, :, None])
    levels = jnp.arange(BUCKETS, dtype=jnp.int32)
    return (bucket_ids[:, None] == levels[None, :, None, None]).astype(jnp.bfloat16)


def block_scores(query_part, key_part, ones_x, ones_y, base_bias, tables):
    scores = jnp.einsum(
        "bqhd,bkhd->bhqk", query_part, key_part, preferred_element_type=jnp.float32
    ) * HDIM ** (-0.5)
    scores = scores + base_bias[None]
    scores = scores + jnp.einsum(
        "bnqk,nh->bhqk", ones_x, tables[1], preferred_element_type=jnp.float32
    )
    return scores + jnp.einsum(
        "bnqk,nh->bhqk", ones_y, tables[2], preferred_element_type=jnp.float32
    )


def layer(
    inputs, masked, total_masked, query_boxes, key_boxes, start_pos, weights, fetch, send_back
):
    doc_count, row_count = (inputs.shape[0], inputs.shape[1])
    token_count = doc_count * row_count
    per_block = LEN // row_count
    block_count = doc_count // per_block
    features = layout_features(query_boxes).reshape(token_count, FEAT).astype(jnp.bfloat16)
    start_rows = inputs.reshape(token_count, D).astype(jnp.float32) + jnp.dot(
        features, weights["w_layout"], preferred_element_type=jnp.float32
    )
    rounded = start_rows.astype(jnp.bfloat16)
    qkv_weight = weights["w_qkv"]
    bias_pair = weights["qv_bias"].astype(jnp.float32)
    query_rows = (
        jnp.dot(rounded, qkv_weight[:, :D], preferred_element_type=jnp.float32) + bias_pair[:D]
    ).astype(jnp.bfloat16)
    key_rows, value_rows = fetch(rounded.reshape(doc_count, row_count, D))
    tables = weights["tables"]
    query_pos = start_pos + jnp.arange(row_count, dtype=jnp.int32)
    key_pos = jnp.arange(LEN, dtype=jnp.int32)
    line_ids = bucket_of(key_pos[None, :] - query_pos[:, None])
    line_ones = (line_ids[None] == jnp.arange(BUCKETS, dtype=jnp.int32)[:, None, None]).astype(
        jnp.bfloat16
    )
    base_bias = jnp.einsum("nqk,nh->hqk", line_ones, tables[0], preferred_element_type=jnp.float32)
    query_b = query_rows.reshape(block_count, per_block, row_count, HEADS, HDIM)
    key_b = key_rows.reshape(block_count, per_block, LEN, HEADS, HDIM)
    value_b = value_rows.reshape(block_count, per_block, LEN, HEADS, HDIM)
    near_x = (query_boxes[..., 0] + query_boxes[..., 2]).reshape(block_count, per_block, row_count)
    near_y = (query_boxes[..., 1] + query_boxes[..., 3]).reshape(block_count, per_block, row_count)
    far_x = (key_boxes[..., 0] + key_boxes[..., 2]).reshape(block_count, per_block, LEN)
    far_y = (key_boxes[..., 1] + key_boxes[..., 3]).reshape(block_count, per_block, LEN)

    def forward_block(block_args):
        query_part, key_part, value_part, qx_part, kx_part, qy_part, ky_part = block_args
        scores = block_scores(
            query_part,
            key_part,
            planar_ones(qx_part, kx_part),
            planar_ones(qy_part, ky_part),
            base_bias,
            tables,
        )
        row_peak = jnp.max(scores, -1, keepdims=True)
        exponent = jnp.exp(scores - row_peak)
        row_mass = jnp.sum(exponent, -1, keepdims=True)
        soft_weights = (exponent / row_mass).astype(jnp.bfloat16)
        mixed_part = jnp.einsum(
            "bhqk,bkhd->bqhd", soft_weights, value_part, preferred_element_type=jnp.float32
        )
        return (mixed_part.astype(jnp.bfloat16), row_peak[..., 0] + jnp.log(row_mass[..., 0]))

    mixed_b, log_mass = lax.map(
        forward_block, (query_b, key_b, value_b, near_x, far_x, near_y, far_y)
    )
    mixed_rows = mixed_b.reshape(token_count, D)
    branch_one = jnp.dot(
        mixed_rows, weights["w_out"], preferred_element_type=jnp.float32
    ) + weights["out_bias"].astype(jnp.float32)
    normed_one, inverse_one = standardize(start_rows + branch_one)
    gain_one = weights["gain_one"].astype(jnp.float32)
    first_rows = normed_one * gain_one + weights["shift_one"].astype(jnp.float32)
    first_low = first_rows.astype(jnp.bfloat16)
    up_rows = jnp.dot(first_low, weights["w_up"], preferred_element_type=jnp.float32) + weights[
        "up_bias"
    ].astype(jnp.float32)
    gelu_value, gelu_back = jax.vjp(functools.partial(jax.nn.gelu, approximate=False), up_rows)
    hidden = gelu_value.astype(jnp.bfloat16)
    branch_two = jnp.dot(hidden, weights["w_down"], preferred_element_type=jnp.float32) + weights[
        "down_bias"
    ].astype(jnp.float32)
    normed_two, inverse_two = standardize(first_rows + branch_two)
    gain_two = weights["gain_two"].astype(jnp.float32)
    layer_out = (normed_two * gain_two + weights["shift_two"].astype(jnp.float32)).astype(
        jnp.bfloat16
    )
    grad_out = masked.reshape(token_count, D).astype(jnp.float32) / total_masked
    grad_second, grad_gain_two, grad_shift_two = norm_back(
        normed_two, inverse_two, gain_two, grad_out
    )
    grad_branch = grad_second.astype(jnp.bfloat16)
    grad_hidden = jnp.einsum(
        "td,fd->tf", grad_branch, weights["w_down"], preferred_element_type=jnp.float32
    )
    grad_up = gelu_back(grad_hidden)[0].astype(jnp.bfloat16)
    grad_first_in = grad_second + jnp.einsum(
        "tf,df->td", grad_up, weights["w_up"], preferred_element_type=jnp.float32
    )
    grad_first, grad_gain_one, grad_shift_one = norm_back(
        normed_one, inverse_one, gain_one, grad_first_in
    )
    grad_attn = grad_first.astype(jnp.bfloat16)
    grad_mixed = jnp.einsum(
        "te,de->td", grad_attn, weights["w_out"], preferred_element_type=jnp.float32
    ).astype(jnp.bfloat16)
    grad_mixed_b = grad_mixed.reshape(block_count, per_block, row_count, HEADS, HDIM)

    def backward_block(block_args):
        (
            query_part,
            key_part,
            value_part,
            qx_part,
            kx_part,
            qy_part,
            ky_part,
            mass_part,
            grad_part,
        ) = block_args
        ones_x = planar_ones(qx_part, kx_part)
        ones_y = planar_ones(qy_part, ky_part)
        scores = block_scores(query_part, key_part, ones_x, ones_y, base_bias, tables)
        soft_full = jnp.exp(scores - mass_part[..., None])
        grad_soft = jnp.einsum(
            "bqhd,bkhd->bhqk", grad_part, value_part, preferred_element_type=jnp.float32
        )
        row_inner = jnp.sum(soft_full * grad_soft, -1, keepdims=True)
        grad_scores = (soft_full * (grad_soft - row_inner)).astype(jnp.bfloat16)
        scale_factor = HDIM ** (-0.5)
        grad_query = (
            jnp.einsum("bhqk,bkhd->bqhd", grad_scores, key_part, preferred_element_type=jnp.float32)
            * scale_factor
        ).astype(jnp.bfloat16)
        grad_key = (
            jnp.einsum(
                "bhqk,bqhd->bkhd", grad_scores, query_part, preferred_element_type=jnp.float32
            )
            * scale_factor
        )
        grad_value = jnp.einsum(
            "bhqk,bqhd->bkhd",
            soft_full.astype(jnp.bfloat16),
            grad_part,
            preferred_element_type=jnp.float32,
        )
        table_x = jnp.einsum(
            "bnqk,bhqk->nh", ones_x, grad_scores, preferred_element_type=jnp.float32
        )
        table_y = jnp.einsum(
            "bnqk,bhqk->nh", ones_y, grad_scores, preferred_element_type=jnp.float32
        )
        line_sum = jnp.sum(grad_scores.astype(jnp.float32), 0)
        return (grad_query, grad_key, grad_value, table_x, table_y, line_sum)

    grad_query, grad_key, grad_value, table_x, table_y, line_sum = lax.map(
        backward_block,
        (query_b, key_b, value_b, near_x, far_x, near_y, far_y, log_mass, grad_mixed_b),
    )
    grad_key, grad_value = send_back(
        (grad_key.reshape(doc_count, LEN, D), grad_value.reshape(doc_count, LEN, D))
    )
    query_low = grad_query.reshape(token_count, D)
    key_low = grad_key.astype(jnp.bfloat16).reshape(token_count, D)
    value_low = grad_value.astype(jnp.bfloat16).reshape(token_count, D)
    grad_qkv = jnp.concatenate([query_low, key_low, value_low], -1)
    grad_start = (
        grad_first
        + jnp.einsum("te,de->td", grad_qkv, qkv_weight, preferred_element_type=jnp.float32)
    ).astype(jnp.bfloat16)
    table_line = jnp.einsum(
        "nqk,hqk->nh",
        line_ones.astype(jnp.float32),
        jnp.sum(line_sum, 0),
        precision=lax.Precision.HIGHEST,
        preferred_element_type=jnp.float32,
    )
    grads = {
        "w_qkv": jnp.einsum("td,te->de", rounded, grad_qkv, preferred_element_type=jnp.float32),
        "qv_bias": jnp.concatenate(
            [jnp.sum(query_low.astype(jnp.float32), 0), jnp.sum(value_low.astype(jnp.float32), 0)]
        ),
        "w_out": jnp.einsum("td,te->de", mixed_rows, grad_attn, preferred_element_type=jnp.float32),
        "out_bias": jnp.sum(grad_attn.astype(jnp.float32), 0),
        "gain_one": grad_gain_one,
        "shift_one": grad_shift_one,
        "w_up": jnp.einsum("td,tf->df", first_low, grad_up, preferred_element_type=jnp.float32),
        "up_bias": jnp.sum(grad_up.astype(jnp.float32), 0),
        "w_down": jnp.einsum("tf,td->fd", hidden, grad_branch, preferred_element_type=jnp.float32),
        "down_bias": jnp.sum(grad_branch.astype(jnp.float32), 0),
        "gain_two": grad_gain_two,
        "shift_two": grad_shift_two,
        "w_layout": jnp.einsum(
            "tf,td->fd", features, grad_start, preferred_element_type=jnp.float32
        ),
        "tables": jnp.stack([table_line, jnp.sum(table_x, 0), jnp.sum(table_y, 0)]),
    }
    return (
        layer_out.reshape(doc_count, row_count, D),
        grad_start.reshape(doc_count, row_count, D),
        pack(grads),
    )


def local(inputs, box_coords, mlm_mask, cotangent, params, first_moment, second_moment):
    fold_index = lax.axis_index("fsdp")
    doc_count, row_count = (inputs.shape[0], inputs.shape[1])
    total_masked = lax.psum(jnp.sum(mlm_mask.astype(jnp.float32)), ("dp", "fsdp"))
    weights = unpack(lax.all_gather(params.astype(jnp.bfloat16), "fsdp", axis=0, tiled=True))
    masked = cotangent * mlm_mask.astype(jnp.bfloat16)[..., None]

    def project(rows_in):
        both_rows = jnp.einsum(
            "trd,de->tre", rows_in, weights["w_qkv"][:, D:], preferred_element_type=jnp.float32
        )
        value_bias = weights["qv_bias"][D:].astype(jnp.float32)
        return (
            both_rows[..., :D].astype(jnp.bfloat16),
            (both_rows[..., D:] + value_bias).astype(jnp.bfloat16),
        )

    query_boxes = lax.dynamic_slice_in_dim(box_coords, fold_index * row_count, row_count, 1)

    def fetch(rows_in):
        own_keys, own_values = project(rows_in)
        return (
            lax.all_gather(own_keys, "fsdp", axis=1, tiled=True),
            lax.all_gather(own_values, "fsdp", axis=1, tiled=True),
        )

    def send_back(grad_pair):
        return (
            lax.psum_scatter(grad_pair[0], "fsdp", scatter_dimension=1, tiled=True),
            lax.psum_scatter(grad_pair[1], "fsdp", scatter_dimension=1, tiled=True),
        )

    layer_out, input_grad, grads = layer(
        inputs,
        masked,
        total_masked,
        query_boxes,
        box_coords,
        fold_index * row_count,
        weights,
        fetch,
        send_back,
    )
    grad_shard = lax.psum_scatter(
        grads.astype(jnp.bfloat16), "fsdp", scatter_dimension=0, tiled=True
    ).astype(jnp.float32)
    summed_piece = lax.psum_scatter(grad_shard, "dp", scatter_dimension=0, tiled=True)
    grad_shard = lax.all_gather(summed_piece.astype(jnp.bfloat16), "dp", axis=0, tiled=True).astype(
        summed_piece.dtype
    )
    squares = lax.psum(jnp.sum(grad_shard * grad_shard), "fsdp")
    shard_len = grad_shard.shape[0]
    positions = fold_index * shard_len + jnp.arange(shard_len, dtype=jnp.int32)
    update, new_first = adamw(params, grad_shard, first_moment, second_moment, positions)
    return (layer_out, input_grad, grad_shard, jnp.sqrt(squares), update, new_first)


def solution(mesh):
    in_specs = (
        P("dp", "fsdp", None),
        P("dp", None, None),
        P("dp", "fsdp"),
        P("dp", "fsdp", None),
        P("fsdp"),
        P("fsdp"),
        P("fsdp"),
    )
    out_specs = (P("dp", "fsdp", None), P("dp", "fsdp", None), P("fsdp"), P(), P("fsdp"), P("fsdp"))
    return jax.shard_map(local, mesh=mesh, in_specs=in_specs, out_specs=out_specs, check_vma=False)
```

profile of v0, /device:TPU:0, one launch (start us, length us, event | category | flops | bytes accessed | tf_op | source)
XLA Modules:
  0.0 1474.6 jit_solution(8162286649208587358)
XLA Ops:
  16.4 42.5 %psum.14 = f32[]{:T(128)} all-reduce(f32[]{:T(128)} %convert_reduce_fusion.1), channel_id=1, replica_groups=mesh['dp'=16,'fsdp'=2] {'dp','fsdp'}, use_global_device_ids=true, to_apply=%region_7.8 | all-reduce | flops 1 | bytes 8 | tf_op jit(solution)/shard_map/psum | solution.py:345
  63.6 24.4 %copy.88 = pred[32,256,512]{2,0,1:T(32,128)(4,1)} copy(pred[32,256,512]{1,0,2:T(32,128)(4,1)S(1)} %iota_compare_fusion.6) | data formatting | bytes 8388608 | tf_op jit(solution)/shard_map/eq | solution.py:170
  93.8 97.6 %all-gather.5.cloned.1.call-done = bf16[7208960]{0:T(1024)(128)(2,1)} async-done(((bf16[3604480]{0:T(1024)(128)(2,1)}), bf16[7208960]{0:T(1024)(128)(2,1)}) %all-gather.5.cloned.1.call-update) | async-done | bytes 14417936 | tf_op jit(solution)/shard_map/all_gather | solution.py:346
  210.2 9.5 fusion.3
  219.7 9.3 fusion.1
  237.2 17.5 %copy.92 = f32[2,256,512,12]{2,1,3,0:T(8,128)} copy(f32[2,256,512,12]{1,3,2,0:T(8,128)} %fusion.3) | data formatting | bytes 25165824 | tf_op jit(solution)/shard_map/while/body/eval_jaxpr/bnqk,nh->bhqk/dot_general | solution.py:140
  254.7 17.9 %copy.94 = f32[2,256,512,12]{2,1,3,0:T(8,128)} copy(f32[2,256,512,12]{1,3,2,0:T(8,128)} %fusion.1) | data formatting | bytes 25165824 | tf_op jit(solution)/shard_map/while/body/eval_jaxpr/bnqk,nh->bhqk/dot_general | solution.py:143
  295.0 9.3 reshape.399
  311.0 18.8 %fusion.122 = (f32[2,12,256]{2,1,0:T(8,128)S(1)}, f32[2,12,256,512]{3,2,1,0:T(8,128)}) fusion(f32[2,256,512,12]{2,1,3,0:T(8,128)} %copy.94, f32[2,256,512,12]{2,1,3,0:T(8,128)} %copy.92, f32[12,256,512]{2,1,0:T(8,128)} %copy.90, bf16[2,512,12,64]{1,3,2,0:T(8,128)(2,1)S(1)} %bitcast.145, bf16[2,256,12,64]{1,0,3,2:T(2,128)(2,1)} %squeeze.63), kind=kOutput, calls=%fused_computation.229 | convolution fusion | flops 418375680 | bytes 46424064 | tf_op jit(solution)/shard_map/while/body/eval_jaxpr/bqhd,bkhd->bhqk/dot_general | solution.py:136
  348.0 18.5 %multiply_convert_fusion.1 = (bf16[512,3072]{1,0:T(8,128)(2,1)S(1)}, f32[512,3072]{1,0:T(8,128)}, f32[512,3072]{1,0:T(8,128)}) fusion(f32[3072]{0:T(1024)S(1)} %slice_convert_fusion.1, bf16[768,3072]{1,0:T(8,128)(2,1)S(1)} %bitcast.152, f32[512,768]{1,0:T(8,128)S(1)} %get-tuple-element.143, f32[768]{0:T(1024)S(1)} %get-tuple-element.120, ...), kind=kOutput, calls=%fused_computation.38 | convolution fusion | flops 2521694208 | bytes 22042624 | tf_op jit(solution)/shard_map/dot_general | solution.py:212
  371.8 8.8 fusion.126
  395.4 9.8 convert_reduce_fusion
  421.2 14.3 copy.106
  435.5 9.7 copy.105
  445.1 11.2 fusion.73
  494.5 9.4 reshape.410
  530.2 19.3 %dynamic-update-slice.3 = bf16[7208960]{0:T(1024)(128)(2,1)} dynamic-update-slice(bf16[7208960]{0:T(1024)(128)(2,1)} %dynamic-update-slice.2, bf16[589824]{0:T(1024)(128)(2,1)} %reshape.408, s32[]{} %constant.303) | dynamic-update-slice | bytes 2359300
  553.8 72.9 %dynamic-update-slice.7 = bf16[7208960]{0:T(1024)(128)(2,1)} dynamic-update-slice(bf16[7208960]{0:T(1024)(128)(2,1)} %dynamic-update-slice.6, bf16[2359296]{0:T(1024)(128)(2,1)} %bitcast.142, s32[]{} %constant.307) | dynamic-update-slice | bytes 9437188
  628.2 72.9 %dynamic-update-slice.9 = bf16[7208960]{0:T(1024)(128)(2,1)} dynamic-update-slice(bf16[7208960]{0:T(1024)(128)(2,1)} %dynamic-update-slice.8, bf16[2359296]{0:T(1024)(128)(2,1)} %reshape.410, s32[]{} %constant.309) | dynamic-update-slice | bytes 9437188
  712.2 324.7 %all-reduce.5.cloned.1.call-done = bf16[7208960]{0:T(1024)(128)(2,1)} async-done(((bf16[7208960]{0:T(1024)(128)(2,1)}), bf16[7208960]{0:T(1024)(128)(2,1)}) %all-reduce.5.cloned.1.call-update) | async-done | bytes 14417936
  1036.9 8.6 dynamic-slice_convert_fusion
  1045.5 301.5 %all-reduce.6 = bf16[3604480]{0:T(1024)(128)(2,1)} all-reduce(f32[3604480]{0:T(1024)} %dynamic-slice_convert_fusion), channel_id=5, replica_groups=mesh['dp'=16,'fsdp'=2] {'dp'}, use_global_device_ids=true, to_apply=%region_26.27.clone | all-reduce | flops 3604480 | bytes 21626880
  1348.8 71.0 %all-gather.11.cloned.1.call-done = bf16[3604480]{0:T(1024)(128)(2,1)} async-done(((bf16[225280]{0:T(1024)(128)(2,1)}), bf16[3604480]{0:T(1024)(128)(2,1)}) %all-gather.11.cloned.1.call-update) | async-done | bytes 7208976 | tf_op jit(solution)/shard_map/all_gather | solution.py:389
  1419.9 32.2 %fusion.14 = (f32[3604480]{0:T(1024)}, f32[3604480]{0:T(1024)}, f32[3604480]{0:T(1024)}) fusion(f32[3604480]{0:T(1024)} %param.11, f32[3604480]{0:T(1024)} %param.13, s32[]{:T(128)S(6)} %mul.291, f32[3604480]{0:T(1024)} %param.12, bf16[3604480]{0:T(1024)(128)(2,1)} %all-gather.11.cloned.1.call-done), kind=kLoop, calls=%fused_computation.18 | loop fusion | flops 64880640 | bytes 93716480 | tf_op jit(solution)/shard_map/mul | solution.py:110
  (230 shorter events, 224.4 us)
Async XLA Ops:
  7.2 184.2 %all-gather.5.cloned.1.call-start = ((), (), s32[]{:S(2)}) async-start(), calls=%async_computation.2 | async-start | bytes 21626880 | tf_op jit(solution)/shard_map/all_gather | solution.py:346
  15.2 43.8 %copy-start.30 = (s32[2,512,4]{1,2,0:T(4,128)S(1)}, s32[2,512,4]{1,2,0:T(4,128)}, u32[]{:S(2)}) copy-start(s32[2,512,4]{1,2,0:T(4,128)} %param.8) | copy-start | bytes 49156
  15.2 294.0 %all-gather.9.cloned.1.call-start = ((), (), s32[]{:S(2)}) async-start(), calls=%async_computation.4 | async-start | bytes 2359296 | tf_op jit(solution)/shard_map/all_gather | solution.py:364
  61.3 26.8 %copy-start.14 = (s32[256,512]{0,1:T(8,128)}, s32[256,512]{0,1:T(8,128)S(1)}, u32[]{:S(2)}) copy-start(s32[256,512]{0,1:T(8,128)S(1)} %convert_add_fusion.3) | copy-start | bytes 1572868
  200.1 10.1 copy-start.5
  203.0 30.8 %copy-start.29 = (bf16[512,768]{1,0:T(8,128)(2,1)}, bf16[512,768]{1,0:T(8,128)(2,1)S(1)}, u32[]{:S(2)}) copy-start(bf16[512,768]{1,0:T(8,128)(2,1)S(1)} %get-tuple-element.138) | copy-start | bytes 2359300
  209.1 127.1 %all-gather.7.cloned.1.call-start = ((), (), s32[]{:S(2)}) async-start(), calls=%async_computation.3 | async-start | bytes 2359296 | tf_op jit(solution)/shard_map/all_gather | solution.py:365
  210.2 18.8 %slice-start = ((s8[14417920]{0:T(1024)(128)(4,1)}), s8[4194304]{0:T(1024)(128)(4,1)S(1)}, s32[]{:S(2)}) async-start(s8[14417920]{0:T(1024)(128)(4,1)} %bitcast.143), calls=%async_computation.9 | async-start | bytes 8388608
  210.2 18.8 %slice-start.1 = ((s8[14417920]{0:T(1024)(128)(4,1)}), s8[4194304]{0:T(1024)(128)(4,1)S(1)}, s32[]{:S(2)}) async-start(s8[14417920]{0:T(1024)(128)(4,1)} %bitcast.143), calls=%async_computation.10 | async-start | bytes 8388608
  308.4 195.5 %reduce-scatter.3.cloned.1.call-start = ((), (), s32[]{:S(2)}) async-start(), calls=%async_computation.5 | async-start | bytes 4718592 | tf_op jit(solution)/shard_map/reduce_scatter | solution.py:370
  311.0 18.8 %copy-start.1 = (bf16[2,512,768]{1,2,0:T(8,128)(2,1)}, bf16[2,512,768]{1,2,0:T(8,128)(2,1)S(1)}, u32[]{:S(2)}) copy-start(bf16[2,512,768]{1,2,0:T(8,128)(2,1)S(1)} %copy.86) | copy-start | bytes 4718596
  338.0 10.0 slice-start.5
  338.0 10.0 slice-start.6
  346.7 19.8 %slice-start.7 = ((s8[4718592]{0:T(1024)(128)(4,1)}), s8[4194304]{0:T(1024)(128)(4,1)S(1)}, s32[]{:S(2)}) async-start(s8[4718592]{0:T(1024)(128)(4,1)} %bitcast.153), calls=%async_computation.16 | async-start | bytes 8388608
  347.7 36.5 %copy-start.11 = (f32[512,768]{1,0:T(8,128)}, f32[512,768]{1,0:T(8,128)S(1)}, u32[]{:S(2)}) copy-start(f32[512,768]{1,0:T(8,128)S(1)} %get-tuple-element.143) | copy-start | bytes 4718596
  348.0 18.5 %slice-start.8 = ((s8[4718592]{0:T(1024)(128)(4,1)}), s8[524288]{0:T(1024)(128)(4,1)S(1)}, s32[]{:S(2)}) async-start(s8[4718592]{0:T(1024)(128)(4,1)} %bitcast.153), calls=%async_computation.17 | async-start | bytes 1048576
  412.5 94.1 %reduce-scatter.5.cloned.1.call-start = ((), (), s32[]{:S(2)}) async-start(), calls=%async_computation.6 | async-start | bytes 4718592 | tf_op jit(solution)/shard_map/reduce_scatter | solution.py:371
  421.1 615.8 %all-reduce.5.cloned.1.call-start = ((), (), s32[]{:S(2)}) async-start(), calls=%async_computation.8 | async-start | bytes 28835840
  435.5 9.7 copy-start.15
  435.5 20.9 %copy-start.6 = (s32[2,256,512]{1,2,0:T(8,128)S(1)}, s32[2,256,512]{1,2,0:T(8,128)}, u32[]{:S(2)}) copy-start(s32[2,256,512]{1,2,0:T(8,128)} %convert_add_fusion.2) | copy-start | bytes 3145732
  445.1 11.3 copy-start.3
  527.1 99.6 %copy-start.33 = (bf16[3072]{0:T(1024)(128)(2,1)S(1)}, bf16[3072]{0:T(1024)(128)(2,1)}, u32[]{:S(2)}) copy-start(bf16[3072]{0:T(1024)(128)(2,1)} %get-tuple-element.152) | copy-start | bytes 18436
  626.8 77.2 %copy-start.31 = (bf16[768]{0:T(1024)(128)(2,1)S(1)}, bf16[768]{0:T(1024)(128)(2,1)}, u32[]{:S(2)}) copy-start(bf16[768]{0:T(1024)(128)(2,1)} %get-tuple-element.84) | copy-start | bytes 4612
  709.1 710.7 %all-gather.11.cloned.1.call-start = ((), (), s32[]{:S(2)}) async-start(), calls=%async_computation.7 | async-start | bytes 7659520 | tf_op jit(solution)/shard_map/all_gather | solution.py:389
  (30 other events, 150.1 us)
Sparse Core Ops, SparseCore 0:
  15.3 176.0 all-gather.4
  209.2 27.2 all-gather.8
  308.5 27.2 all-gather.6
  412.7 43.3 reduce-scatter.2
  458.2 43.3 reduce-scatter.4
  709.2 327.6 all-reduce.4
  1348.9 70.8 all-gather.10
where the time goes:
time: 1500 us; the launch traced here: 1470 us
  waiting for transfers between devices  494 us (33%)
  local copies, waits for them, and re-layouts  360 us (24%)
  blocking collectives  350 us (23%)
  matrix products  158 us (11%)
  other arithmetic  94.5 us (6%)
  between operations  18.5 us (1%)
    unnamed x8, waiting for transfers between devices  325 us
    unnamed x1, blocking collectives  301 us
    unnamed x117, local copies, waits for them, and re-layouts  197 us
    all_gather x1, waiting for transfers between devices, local(): lax.all_gather(params.astype(jnp.bfloat16), 'fsdp', axis=0, tiled=True)  97.6 us
    all_gather x1, waiting for transfers between devices, local(): lax.all_gather(summed_piece.astype(jnp.bfloat16), 'dp', axis=0, tiled=True)  71 us
    psum x1, blocking collectives, local(): lax.psum(jnp.sum(mlm_mask.astype(jnp.float32)), ('dp', 'fsdp'))  42.5 us
    mul x1, other arithmetic, adamw(): return (rate_scale * (corrected + decay_rate * weights_in), first_new)  32.2 us
  transfers between devices with their start and end apart: 7, of which 3 were waited for; matrix products, arithmetic and copies ran while one was open for 17% of the time, Pallas kernels for 0%

commit v1 on v0

v1 whole, which is shorter than its diff:
```python
import functools
import math

import jax
import jax.numpy as jnp
import numpy as np
from jax import lax
from jax.experimental import pallas as pl
from jax.experimental.pallas import tpu as pltpu
from jax.sharding import PartitionSpec as P

D = 768
HEADS = 12
HDIM = 64
FF = 3072
BUCKETS = 32
FEAT = 128
LEN = 512
PADDED = 7208960
SHARD = PADDED // 2
FLAT = SHARD // 128
PAIRS = HEADS // 2
QROWS = 128

norm_eps = 1e-05
adam_one = 0.9
adam_two = 0.999
adam_eps = 1e-08
adam_steps = 100.0
decay_rate = 0.01
table_factor = 5.0

MESH = pl.DeviceIdType.MESH
F32 = jnp.float32
BF16 = jnp.bfloat16
VMEM = pl.BlockSpec(memory_space=pltpu.VMEM)
ANY = pl.BlockSpec(memory_space=pl.ANY)

ROWS = 28672
CHUNK = 2048
CHUNKS = ROWS // CHUNK
CUT = 404
UP_A, UP_B = 416, 368
OUT0 = 18 * D
UP0 = OUT0 + 6 * D
SM0 = UP0 + 24 * UP_A
UP1 = 0
DOWN1 = 24 * UP_B
LAY1 = DOWN1 + 6 * FF
SM1 = LAY1 + 6 * FEAT
F_OUT = 13836
F_UP = 18462
F_UPB1 = 8734
F_DOWN1 = 8758
F_SM1 = 27190
F_LAY1 = 27208
F_TAB1 = 27976
LEAD = 104


def nt(a, b):
    return lax.dot_general(a, b, (((1,), (1,)), ((), ())), preferred_element_type=F32)


def nn(a, b):
    return lax.dot_general(a, b, (((1,), (0,)), ((), ())), preferred_element_type=F32)


def tn(a, b):
    return lax.dot_general(a, b, (((0,), (0,)), ((), ())), preferred_element_type=F32)


def radices(replicas):
    stages, stride, left = [], 2, replicas // 2
    if left % 2 == 0:
        stages.append((2, stride))
        stride, left = stride * 2, left // 2
    while left > 1:
        radix = left if left <= 8 else 4
        stages.append((radix, stride))
        stride, left = stride * radix, left // radix
    return stages


def place():
    return lax.axis_index("dp"), lax.axis_index("fsdp")


def member(dp, radix, stride, digit):
    return dp + (digit - (dp // stride) % radix) * stride


def peers(stages):
    dp, fs = place()
    found = [(dp + 1 - 2 * (dp % 2), fs), (dp, 1 - fs)]
    for radix, stride in stages:
        mine = (dp // stride) % radix
        for step in range(1, radix):
            found.append((member(dp, radix, stride, (mine + step) % radix), fs))
    return found


def greet(stages):
    barrier = pltpu.get_barrier_semaphore()
    all_peers = peers(stages)
    for peer in all_peers:
        pl.semaphore_signal(barrier, inc=1, device_id=peer, device_id_type=MESH)
    pl.semaphore_wait(barrier, len(all_peers))


def remote(src, dst, send, recv, peer):
    return pltpu.make_async_remote_copy(
        src_ref=src, dst_ref=dst, send_sem=send, recv_sem=recv, device_id=peer, device_id_type=MESH
    )


def rows_at(start, size):
    return pl.ds(pl.multiple_of(start, 16), size)


def offsets(dp, stages, extent):
    size = extent // 2
    start = (dp % 2) * size
    found = [(start, size)]
    for radix, stride in stages:
        size = size // radix
        start = start + ((dp // stride) % radix) * size
        found.append((start, size))
    return found


def row_of(ref_rows, start, count):
    return jnp.concatenate([ref_rows[start + i : start + i + 1, :] for i in range(count)], axis=1)


def relayout_tasks(plane, flat, out):
    tasks = []

    def block(dst, src, count, stride):
        def run():
            out[plane, pl.ds(dst, count), :] = flat[pl.ds(LEAD + src, count, stride=stride), :].astype(BF16)

        tasks.append((dst + count, run))

    def window(dst, src, count):
        def run():
            out[plane, pl.ds(dst, count), :] = flat[pl.ds(LEAD + src, count), :].astype(BF16)

        tasks.append((dst + count, run))

    if plane == 0:
        for pos in range(18):
            block(pos * D, (pos % 3) * 6 + pos // 3, D, 18)
        for c in range(6):
            block(OUT0 + c * D, F_OUT + c, D, 6)
        for c in range(24):
            block(UP0 + c * UP_A, F_UP + c, UP_A, 24)
        window(SM0, 13824, 16)
        window(SM0 + 16, 18440, 32)
        used = SM0 + 48
    else:
        for c in range(24):
            block(UP1 + c * UP_B, c - 98, UP_B, 24)
        for c in range(6):
            block(DOWN1 + c * FF, F_DOWN1 + c, FF, 6)
        for c in range(6):
            block(LAY1 + c * FEAT, F_LAY1 + c, FEAT, 6)
        window(SM1, 8728, 32)
        window(SM1 + 32, 27184, 32)
        window(SM1 + 64, 27976, 16)
        used = SM1 + 80

    def clear():
        out[plane, pl.ds(used, ROWS - used), :] = jnp.zeros((ROWS - used, 128), BF16)

    tasks.append((ROWS, clear))
    return tasks


def direct_type(position):
    return position % 4 == 1


def gather_kernel(
    stages, p_hbm, xin, cot, cnt, wall, xdoc, cdoc, total,
    flat, zall, xs, cs, cnt_slots, in_sem, x_send, x_recv, c_send, c_recv, act_send, act_recv,
    n_send, n_recv, out_sem, *stage_sems,
):
    dp, fs = place()
    other = 1 - fs
    pieces = 8
    span = FLAT // pieces
    loads = [
        pltpu.make_async_copy(
            p_hbm.at[pl.ds(i * span, span)], flat.at[pl.ds(LEAD + i * span, span)], in_sem.at[i]
        )
        for i in range(pieces)
    ]
    for load in loads:
        load.start()
    flat[pl.ds(0, LEAD), :] = jnp.zeros((LEAD, 128), F32)
    flat[pl.ds(LEAD + FLAT, 288), :] = jnp.zeros((288, 128), F32)
    greet(stages)
    x_peer = (dp, other)
    core_peer = (dp + 1 - 2 * (dp % 2), fs)
    half = LEN // 2

    def act_copies(send):
        where = rows_at((fs if send else other) * half, half)
        return [
            remote(xin.at[other], xs.at[where], act_send.at[0], act_recv.at[0], x_peer),
            remote(cot.at[other], cs.at[where], act_send.at[1], act_recv.at[1], x_peer),
        ]

    for copy in act_copies(True):
        copy.start()
    for load in loads:
        load.wait()

    order = [(CHUNKS - 1 + i) % CHUNKS for i in range(CHUNKS)]
    parts = offsets(dp, stages, CHUNK)

    def x_copy(position, plane):
        start, size = parts[0] if direct_type(position) else parts[-1]
        where = zall.at[plane, rows_at(order[position] * CHUNK + start, size)]
        return remote(where, where, x_send.at[position], x_recv.at[position], x_peer)

    def stage_copies(level, position, receive):
        radix, stride = stages[level]
        start, size = parts[level + 1]
        mine = (dp // stride) % radix
        send_sem, recv_sem = stage_sems[2 * level], stage_sems[2 * level + 1]
        copies = []
        for step in range(1, radix):
            peer = (member(dp, radix, stride, (mine + step) % radix), fs)
            shift = ((mine - step + radix) % radix - mine) * size if receive else 0
            where = zall.at[other, rows_at(order[position] * CHUNK + start + shift, size)]
            copies.append(
                remote(where, where, send_sem.at[position, step - 1], recv_sem.at[position, step - 1], peer)
            )
        return copies

    def core_copy(position, receive):
        size = CHUNK // 2
        start = (1 - dp % 2 if receive else dp % 2) * size
        where = zall.at[other, rows_at(order[position] * CHUNK + start, size)]
        return remote(where, where, c_send.at[position], c_recv.at[position], core_peer)

    levels = len(stages)

    def advance(position, stage):
        if direct_type(position):
            if stage == 0:
                x_copy(position, other).wait_recv()
                core_copy(position, False).start()
            return
        if stage == 0:
            x_copy(position, other).wait_recv()
        else:
            for copy in stage_copies(levels - stage, position, True):
                copy.wait_recv()
        if stage < levels:
            for copy in stage_copies(levels - 1 - stage, position, False):
                copy.start()
        else:
            core_copy(position, False).start()

    rounds = [[core_peer], [x_peer]] + [
        [
            (member(dp, radix, stride, ((dp // stride) % radix + step) % radix), fs)
            for step in range(1, radix)
        ]
        for radix, stride in stages
    ]

    def count_copies(number):
        base = sum(len(r) for r in rounds[:number])
        return [
            remote(total.at[...], cnt_slots.at[base + i], n_send.at[base + i], n_recv.at[base + i], peer)
            for i, peer in enumerate(rounds[number])
        ]

    def count_round(number):
        if number > 0:
            for copy in count_copies(number - 1):
                copy.wait()
            base = sum(len(r) for r in rounds[: number - 1])
            gathered = total[...]
            for i in range(len(rounds[number - 1])):
                gathered = gathered + cnt_slots[base + i]
            total[...] = gathered
        if number < len(rounds):
            for copy in count_copies(number):
                copy.start()

    total[...] = cnt[...]
    count_round(0)

    tasks = [relayout_tasks(0, flat, zall), relayout_tasks(1, flat, zall)]
    done = [set(), set()]
    for position in range(CHUNKS + levels + 1):
        if position < CHUNKS:
            low, high = order[position] * CHUNK, (order[position] + 1) * CHUNK
            for plane in range(2):
                run, start = [], 0
                for number, (end, task) in enumerate(tasks[plane]):
                    if start < high and end > low and number not in done[plane]:
                        done[plane].add(number)
                        run.append(task)
                    start = end

                @pl.when(fs == plane)
                def _(run=run):
                    for task in run:
                        task()

            x_copy(position, fs).start()
        for stage in range(levels + 1):
            if 0 <= position - 1 - stage < CHUNKS:
                advance(position - 1 - stage, stage)
        if 2 <= position and (position - 2) % 2 == 0 and (position - 2) // 2 + 1 <= len(rounds):
            count_round((position - 2) // 2 + 1)
    xdoc[pl.ds(fs * half, half), :] = xin[fs]
    cdoc[pl.ds(fs * half, half), :] = cot[fs]
    outs = [
        pltpu.make_async_copy(zall.at[fs], wall.at[fs], out_sem.at[0]),
    ]
    outs[0].start()
    for copy in act_copies(False):
        copy.wait_recv()
    xdoc[pl.ds(other * half, half), :] = xs[pl.ds(other * half, half), :]
    cdoc[pl.ds(other * half, half), :] = cs[pl.ds(other * half, half), :]
    for copy in act_copies(True):
        copy.wait_send()
    for position in range(CHUNKS):
        core_copy(position, True).wait_recv()
        core_copy(position, False).wait_send()
        x_copy(position, fs).wait_send()
        if not direct_type(position):
            for level in range(levels):
                for copy in stage_copies(level, position, False):
                    copy.wait_send()
    outs.append(pltpu.make_async_copy(zall.at[other], wall.at[other], out_sem.at[1]))
    outs[1].start()
    for copy in outs:
        copy.wait()


def gather_weights(stages, p2, xin, cot, cnt):
    count_peers = 2 + sum(radix - 1 for radix, _ in stages)
    sems = []
    for radix, _ in stages:
        sems += [pltpu.SemaphoreType.DMA((CHUNKS, radix - 1))] * 2
    half = LEN // 2
    return pl.pallas_call(
        functools.partial(gather_kernel, stages),
        name="gather_weights",
        out_shape=(
            jax.ShapeDtypeStruct((2, ROWS, 128), BF16),
            jax.ShapeDtypeStruct((LEN, D), BF16),
            jax.ShapeDtypeStruct((LEN, D), BF16),
            jax.ShapeDtypeStruct((8, 128), F32),
        ),
        in_specs=[ANY, VMEM, VMEM, VMEM],
        out_specs=(ANY, VMEM, VMEM, VMEM),
        scratch_shapes=[
            pltpu.VMEM((LEAD + FLAT + 288, 128), F32),
            pltpu.VMEM((2, ROWS, 128), BF16),
            pltpu.VMEM((LEN, D), BF16),
            pltpu.VMEM((LEN, D), BF16),
            pltpu.VMEM((count_peers, 8, 128), F32),
            pltpu.SemaphoreType.DMA((8,)),
            pltpu.SemaphoreType.DMA((CHUNKS,)),
            pltpu.SemaphoreType.DMA((CHUNKS,)),
            pltpu.SemaphoreType.DMA((CHUNKS,)),
            pltpu.SemaphoreType.DMA((CHUNKS,)),
            pltpu.SemaphoreType.DMA((2,)),
            pltpu.SemaphoreType.DMA((2,)),
            pltpu.SemaphoreType.DMA((count_peers,)),
            pltpu.SemaphoreType.DMA((count_peers,)),
            pltpu.SemaphoreType.DMA((2,)),
        ]
        + sems,
        compiler_params=pltpu.CompilerParams(
            collective_id=1, has_side_effects=True, vmem_limit_bytes=60 * 2**20
        ),
    )(p2, xin, cot, cnt)


def table_constants():
    width = BUCKETS * HEADS
    lane = np.arange(width)
    pick = np.zeros((3, width, 128), np.float32)
    for table in range(3):
        pick[table, lane, 32 * table + lane // HEADS] = 1.0
    keep = (lane[None, :] % HEADS == np.arange(16)[:, None]).astype(np.float32)
    return pick.astype(jnp.bfloat16), keep


def bucket_of(offset):
    spread = jnp.abs(offset)
    result = jnp.minimum(spread, 8) + jnp.where(offset > 0, 16, 0)
    for level in range(9, 16):
        result = result + jnp.where(spread >= 8 * 2 ** (level - 8), 1, 0)
    return result


def up_block(wall, j):
    columns = []
    for c in (2 * j, 2 * j + 1):
        first = wall[0, rows_at(UP0 + c * UP_A, UP_A), :]
        second = wall[1, rows_at(UP1 + c * UP_B + 16, UP_B - 16), :]
        columns.append(jnp.concatenate([first, second], axis=0))
    return jnp.concatenate(columns, axis=1)


def down_rows(wall, j):
    return jnp.concatenate(
        [wall[1, rows_at(DOWN1 + c * FF + j * 256, 256), :] for c in range(6)], axis=1
    )


def merge_up(wall):
    row = lax.broadcasted_iota(jnp.int32, (16, 128), 0)

    def one(c, carry):
        low_at = rows_at(UP0 + c * UP_A + UP_A - 16, 16)
        low = wall[0, low_at, :].astype(F32)
        high = wall[1, rows_at(UP1 + c * UP_B, 16), :].astype(F32)
        cut = jnp.where(c < 2, CUT + 1 - 400, CUT - 400)
        wall[0, low_at, :] = jnp.where(row < cut, low, high).astype(BF16)
        return carry

    lax.fori_loop(0, 24, one, 0)


def stats(values):
    mean = jnp.mean(values, axis=1, keepdims=True)
    centered = values - mean
    inverse = lax.rsqrt(jnp.mean(centered * centered, axis=1, keepdims=True) + norm_eps)
    return centered * inverse, inverse


def forward_kernel(
    wall_hbm, xdoc, features, coord_row, coord_col, pick, keep,
    layer_out, rounded, qkv, probs, mixed, normed_one, inverse_one, first_low, hidden, slope,
    normed_two, inverse_two,
    wall, start, up_bias, acc, bias, sem,
):
    load = pltpu.make_async_copy(wall_hbm, wall, sem.at[0])
    load.start()
    load.wait()
    merge_up(wall)
    small0 = wall[0, pl.ds(SM0, 48), :].astype(F32)
    small1 = wall[1, pl.ds(SM1, 80), :].astype(F32)
    qv_bias = row_of(small0, 0, 12)
    out_bias, gain_one, shift_one = (row_of(small0, 20 + 6 * i, 6) for i in range(3))
    down_bias, gain_two, shift_two = (row_of(small1, 38 + 6 * i, 6) for i in range(3))

    w_layout = jnp.concatenate([wall[1, pl.ds(LAY1 + c * FEAT, FEAT), :] for c in range(6)], axis=1)
    start[...] = xdoc[...].astype(F32) + nn(features[...], w_layout)
    rounded[...] = start[...].astype(BF16)

    heads_by_lane = jnp.zeros((16, 128), F32)
    for table in range(3):
        flat_row = row_of(small1, 64 + 3 * table, 3)
        spread = (jnp.broadcast_to(flat_row, (16, 384)) * keep[...]).astype(BF16)
        heads_by_lane = heads_by_lane + nn(spread, pick[table])
    rows_by_head = [jnp.broadcast_to(heads_by_lane[h : h + 1, :], (8, 128)) for h in range(HEADS)]

    def bias_rows(a, carry):
        at = pl.ds(pl.multiple_of(a * 8, 8), 8)
        for j in range(4):
            lanes = pl.ds(j * 128, 128)
            sums = [None] * HEADS
            for table in range(3):
                far = coord_row[table : table + 1, j * 128 : (j + 1) * 128]
                near = coord_col[at, table : table + 1]
                index = bucket_of(jnp.broadcast_to(far, (8, 128)) - near) + 32 * table
                for h in range(HEADS):
                    found = jnp.take_along_axis(rows_by_head[h], index, axis=1)
                    sums[h] = found if sums[h] is None else sums[h] + found
            for h in range(HEADS):
                bias[h, at, lanes] = sums[h]
        return carry

    lax.fori_loop(0, LEN // 8, bias_rows, 0)

    left = lax.broadcasted_iota(jnp.int32, (LEN, 128), 1) < HDIM
    for pair in range(PAIRS):
        weight = jnp.concatenate(
            [wall[0, pl.ds((3 * pair + i) * D, D), :] for i in range(3)], axis=1
        )
        part = nn(rounded[...], weight)
        lanes = slice(pair * 128, (pair + 1) * 128)
        query = (part[:, :128] + qv_bias[:, lanes]).astype(BF16)
        qkv[3 * pair] = query * HDIM**-0.5
        qkv[3 * pair + 1] = part[:, 128:256].astype(BF16)
        value_bias = qv_bias[:, D + pair * 128 : D + (pair + 1) * 128]
        qkv[3 * pair + 2] = (part[:, 256:] + value_bias).astype(BF16)

    def attend(pair, carry):
        query, key, value = qkv[3 * pair], qkv[3 * pair + 1], qkv[3 * pair + 2]
        found = []
        for side in range(2):
            head = 2 * pair + side
            mine = left if side == 0 else jnp.logical_not(left)
            for at in (slice(r, r + QROWS) for r in range(0, LEN, QROWS)):
                part = query[at]
                scores = nt(jnp.where(mine[at], part, jnp.zeros_like(part)), key) + bias[head, at, :]
                scores = jnp.exp(scores - jnp.max(scores, axis=1, keepdims=True))
                soft = scores * (1.0 / jnp.sum(scores, axis=1, keepdims=True))
                probs[head, at, :] = soft.astype(BF16)
            found.append(nn(probs[head], value))
        mixed[:, pl.ds(pl.multiple_of(pair * 128, 128), 128)] = jnp.where(left, found[0], found[1]).astype(BF16)
        return carry

    lax.fori_loop(0, PAIRS, attend, 0)

    w_out = jnp.concatenate([wall[0, pl.ds(OUT0 + c * D, D), :] for c in range(6)], axis=1)

    def first_rows(r, carry):
        at = pl.ds(pl.multiple_of(r * QROWS, QROWS), QROWS)
        normed, inverse = stats(start[at, :] + nn(mixed[at, :], w_out) + out_bias)
        normed_one[at, :] = normed
        inverse_one[at, :] = inverse
        result = normed * gain_one + shift_one
        first_low[at, :] = result.astype(BF16)
        acc[at, :] = result + down_bias
        return carry

    lax.fori_loop(0, LEN // QROWS, first_rows, 0)
    for j in range(12):
        up_bias[:, j * 256 : (j + 1) * 256] = row_of(small1, 6 + 2 * j, 2)

    def feed_step(j, carry):
        lanes = pl.ds(pl.multiple_of(j * 256, 256), 256)
        up = nn(first_low[...], up_block(wall, j)) + up_bias[:, lanes]
        half_up = 0.5 + 0.5 * lax.erf(up * math.sqrt(0.5))
        bell = jnp.exp(-0.5 * up * up) * (1.0 / math.sqrt(2.0 * math.pi))
        slope[:, lanes] = (half_up + up * bell).astype(BF16)
        part = (up * half_up).astype(BF16)
        hidden[:, lanes] = part
        acc[...] += nn(part, down_rows(wall, j))
        return carry

    lax.fori_loop(0, 12, feed_step, 0)

    def second_rows(r, carry):
        at = pl.ds(pl.multiple_of(r * QROWS, QROWS), QROWS)
        normed, inverse = stats(acc[at, :])
        normed_two[at, :] = normed
        inverse_two[at, :] = inverse
        layer_out[at, :] = (normed * gain_two + shift_two).astype(BF16)
        return carry

    lax.fori_loop(0, LEN // QROWS, second_rows, 0)


def forward_pass(wall, xdoc, features, coord_row, coord_col):
    pick, keep = table_constants()
    sds = jax.ShapeDtypeStruct
    return pl.pallas_call(
        forward_kernel,
        name="forward",
        out_shape=(
            sds((LEN, D), BF16),
            sds((LEN, D), BF16),
            sds((18, LEN, 128), BF16),
            sds((HEADS, LEN, LEN), BF16),
            sds((LEN, D), BF16),
            sds((LEN, D), F32),
            sds((LEN, 1), F32),
            sds((LEN, D), BF16),
            sds((LEN, FF), BF16),
            sds((LEN, FF), BF16),
            sds((LEN, D), F32),
            sds((LEN, 1), F32),
        ),
        in_specs=[ANY] + [VMEM] * 6,
        out_specs=(VMEM,) * 12,
        scratch_shapes=[
            pltpu.VMEM((2, ROWS, 128), BF16),
            pltpu.VMEM((LEN, D), F32),
            pltpu.VMEM((1, FF), F32),
            pltpu.VMEM((LEN, D), F32),
            pltpu.VMEM((HEADS, LEN, LEN), F32),
            pltpu.SemaphoreType.DMA((1,)),
        ],
        compiler_params=pltpu.CompilerParams(vmem_limit_bytes=62 * 2**20),
    )(wall, xdoc, features, coord_row, coord_col, jnp.asarray(pick), jnp.asarray(keep))


G_SMALL = (("qv_bias", 0, 0, 12), ("out_bias", 0, 12, 6), ("gain_one", 0, 18, 6), ("shift_one", 0, 24, 6),
           ("up_bias", 1, 0, 24), ("down_bias", 1, 24, 6), ("gain_two", 1, 30, 6), ("shift_two", 1, 36, 6),
           ("tables", 1, 42, 9))


def spread_norm(normed, inverse, gain, grad):
    scaled = grad * gain
    return inverse * (
        scaled
        - jnp.mean(scaled, axis=1, keepdims=True)
        - normed * jnp.mean(scaled * normed, axis=1, keepdims=True)
    )


def total_rows(values):
    return jnp.sum(values.astype(F32), axis=0, keepdims=True)


def backward_kernel(
    wall_hbm, cdoc, total, rounded, qkv, probs_hbm, mixed, normed_one, inverse_one, first_low, hidden_hbm,
    slope_hbm, normed_two, inverse_two, features, coord_row, coord_col, pick, keep,
    input_grad, grads,
    wall, gstack, acc, branch, hidden, d_up, probs, d_mixed, d_scores, less, prefix, small, lut, places,
    sem, out_sem, probs_sem,
):
    loads = [
        pltpu.make_async_copy(wall_hbm, wall, sem.at[0]),
        pltpu.make_async_copy(hidden_hbm, hidden, sem.at[1]),
        pltpu.make_async_copy(slope_hbm, d_up, sem.at[2]),
    ]
    for load in loads:
        load.start()

    def probs_copy(pair, slot):
        return pltpu.make_async_copy(
            probs_hbm.at[pl.ds(2 * pair, 2)], probs.at[pl.ds(2 * slot, 2)], probs_sem.at[slot]
        )

    probs_copy(0, 0).start()
    for load in loads:
        load.wait()
    merge_up(wall)
    small0 = wall[0, pl.ds(SM0, 48), :].astype(F32)
    small1 = wall[1, pl.ds(SM1, 80), :].astype(F32)
    gain_one = row_of(small0, 26, 6)
    gain_two = row_of(small1, 44, 6)
    small[...] = jnp.zeros_like(small)
    spots = {name: (plane, first_row) for name, plane, first_row, _ in G_SMALL}

    def keep_small(name, vector):
        plane, at = spots[name]
        for i in range(vector.shape[1] // 128):
            small[plane, at + i : at + i + 1, :] = vector[:, i * 128 : (i + 1) * 128]

    count = total[0:1, 0:1]
    none = jnp.zeros((1, D), F32)

    def second_rows(r, sums):
        at = pl.ds(pl.multiple_of(r * QROWS, QROWS), QROWS)
        grad_out = cdoc[at, :].astype(F32) / count
        normed = normed_two[at, :]
        result = spread_norm(normed, inverse_two[at, :], gain_two, grad_out)
        acc[at, :] = result
        low = result.astype(BF16)
        branch[at, :] = low
        return sums[0] + total_rows(grad_out * normed), sums[1] + total_rows(grad_out), sums[2] + total_rows(low)

    sums = lax.fori_loop(0, LEN // QROWS, second_rows, (none, none, none))
    for name, vector in zip(("gain_two", "shift_two", "down_bias"), sums):
        keep_small(name, vector)
    plane_up, at_up = spots["up_bias"]

    def down_step(j, carry):
        lanes = pl.ds(pl.multiple_of(j * 256, 256), 256)
        grad = nt(branch[...], down_rows(wall, j))
        part = (grad * d_up[:, lanes].astype(F32)).astype(BF16)
        d_up[:, lanes] = part
        sums = total_rows(part)
        small[plane_up, pl.ds(at_up + 2 * j, 1), :] = sums[:, :128]
        small[plane_up, pl.ds(at_up + 2 * j + 1, 1), :] = sums[:, 128:]
        down = tn(hidden[:, lanes], branch[...]).astype(BF16)
        for c in range(6):
            gstack[1, rows_at(DOWN1 + c * FF + j * 256, 256), :] = down[:, c * 128 : (c + 1) * 128]
        return carry

    lax.fori_loop(0, 12, down_step, 0)

    def up_step(j, carry):
        lanes = pl.ds(pl.multiple_of(j * 256, 256), 256)
        part = d_up[:, lanes]
        up = tn(first_low[...], part).astype(BF16)
        for i in range(2):
            c = 2 * j + i
            gstack[0, rows_at(UP0 + c * UP_A, UP_A), :] = up[:UP_A, i * 128 : (i + 1) * 128]
            gstack[1, rows_at(UP1 + c * UP_B, UP_B), :] = up[D - UP_B :, i * 128 : (i + 1) * 128]
        acc[...] += nt(part, up_block(wall, j))
        return carry

    lax.fori_loop(0, 12, up_step, 0)

    w_out = jnp.concatenate([wall[0, pl.ds(OUT0 + c * D, D), :] for c in range(6)], axis=1)

    def first_rows(r, sums):
        at = pl.ds(pl.multiple_of(r * QROWS, QROWS), QROWS)
        grad, normed = acc[at, :], normed_one[at, :]
        result = spread_norm(normed, inverse_one[at, :], gain_one, grad)
        acc[at, :] = result
        low = result.astype(BF16)
        branch[at, :] = low
        d_mixed[at, :] = nt(low, w_out).astype(BF16)
        return sums[0] + total_rows(grad * normed), sums[1] + total_rows(grad), sums[2] + total_rows(low)

    sums = lax.fori_loop(0, LEN // QROWS, first_rows, (none, none, none))
    for name, vector in zip(("gain_one", "shift_one", "out_bias"), sums):
        keep_small(name, vector)

    def out_step(j, carry):
        lanes = pl.ds(pl.multiple_of(j * 256, 256), 256)
        part = tn(mixed[...], branch[:, lanes]).astype(BF16)
        for i in range(2):
            gstack[0, rows_at(OUT0 + (2 * j + i) * D, D), :] = part[:, i * 128 : (i + 1) * 128]
        return carry

    lax.fori_loop(0, 3, out_step, 0)

    left = lax.broadcasted_iota(jnp.int32, (LEN, 128), 1) < HDIM

    def attend(pair, carry):
        query, key, value = qkv[3 * pair], qkv[3 * pair + 1], qkv[3 * pair + 2]
        slot = pair % 2

        @pl.when(pair + 1 < PAIRS)
        def _():
            probs_copy(pair + 1, 1 - slot).start()

        probs_copy(pair, slot).wait()
        grad = d_mixed[:, pl.ds(pl.multiple_of(pair * 128, 128), 128)]
        found = []
        for side in range(2):
            head = 2 * pair + side
            mine = left if side == 0 else jnp.logical_not(left)
            for at in (slice(r, r + QROWS) for r in range(0, LEN, QROWS)):
                part = grad[at]
                d_probs = nt(jnp.where(mine[at], part, jnp.zeros_like(part)), value)
                soft = probs[2 * slot + side, at, :].astype(F32)
                inner = jnp.sum(soft * d_probs, axis=1, keepdims=True)
                d_scores[head, at, :] = (soft * (d_probs - inner)).astype(BF16)
            scores = d_scores[head]
            found.append((nn(scores, key), tn(scores, query), tn(probs[2 * slot + side], grad)))
        d_query = (jnp.where(left, found[0][0], found[1][0]) * HDIM**-0.5).astype(BF16)
        d_key = jnp.where(left, found[0][1], found[1][1]).astype(BF16)
        d_value = jnp.where(left, found[0][2], found[1][2]).astype(BF16)
        both = jnp.concatenate([d_query, d_key, d_value], axis=1)
        plane, spot = spots["qv_bias"]
        small[plane, pl.ds(spot + pair, 1), :] = total_rows(d_query)
        small[plane, pl.ds(spot + 6 + pair, 1), :] = total_rows(d_value)
        at = pl.multiple_of(3 * pair * D, 16)
        weight = jnp.concatenate([wall[0, rows_at(at + i * D, D), :] for i in range(3)], axis=1)
        acc[...] += nt(both, weight)
        part = tn(rounded[...], both).astype(BF16)
        for i in range(3):
            gstack[0, rows_at(at + i * D, D), :] = part[:, i * 128 : (i + 1) * 128]
        return carry

    lax.fori_loop(0, PAIRS, attend, 0)
    result = acc[...].astype(BF16)
    input_grad[...] = result
    layout = tn(features[...], result).astype(BF16)
    for c in range(6):
        gstack[1, pl.ds(LAY1 + c * FEAT, FEAT), :] = layout[:, c * 128 : (c + 1) * 128]

    table_grads(d_scores, coord_row, coord_col, pick, keep, less, prefix, small, lut, places, spots)

    gstack[0, pl.ds(SM0, ROWS - SM0), :] = jnp.zeros((ROWS - SM0, 128), BF16)
    gstack[1, pl.ds(SM1, ROWS - SM1), :] = jnp.zeros((ROWS - SM1, 128), BF16)
    gstack[0, pl.ds(SM0, 64), :] = small[0].astype(BF16)
    gstack[1, pl.ds(SM1, 64), :] = small[1].astype(BF16)
    store = pltpu.make_async_copy(gstack, grads, out_sem.at[0])
    store.start()
    store.wait()


def table_grads(d_scores, coord_row, coord_col, pick, keep, less, prefix, small, lut, places, spots):
    lane = lax.broadcasted_iota(jnp.int32, (8, 128), 1)
    step = lane % 16
    level = jnp.where(step <= 8, step, lax.shift_left(jnp.full_like(step, 8), jnp.maximum(step - 8, 0)))
    edge = jnp.where(lane < 16, 1 - level, jnp.where(lane == 16, 1 << 12, level))
    rows = []
    for table in range(3):
        key_row = coord_row[table : table + 1, :]
        key_col = coord_col[:, table : table + 1]
        less[...] = jnp.where(
            jnp.broadcast_to(key_col, (LEN, LEN)) <= jnp.broadcast_to(key_row, (LEN, LEN)), 1.0, 0.0
        ).astype(BF16)
        code = key_col * LEN + lax.broadcasted_iota(jnp.int32, (LEN, 1), 0)
        for group in range(16):
            value = lax.broadcasted_iota(jnp.int32, (LEN, 128), 1) + group * 128
            best = jnp.max(
                jnp.where(jnp.broadcast_to(key_col, (LEN, 128)) < value, jnp.broadcast_to(code, (LEN, 128)), -1),
                axis=0, keepdims=True,
            )
            lut[group : group + 1, :] = jnp.where(best < 0, LEN, best & (LEN - 1))

        def find(a, carry):
            at = pl.ds(pl.multiple_of(a * 8, 8), 8)
            value = jnp.clip(coord_col[at, table : table + 1] + edge, 0, 2047)
            low, high = value & 127, value >> 7
            found = jnp.full((8, 128), LEN, jnp.int32)
            for group in range(16):
                row = jnp.broadcast_to(lut[group : group + 1, :], (8, 128))
                found = jnp.where(high == group, jnp.take_along_axis(row, low, axis=1), found)
            places[at, :] = found
            return carry

        lax.fori_loop(0, LEN // 8, find, 0)

        sums = []
        for batch in range(3):
            for h in range(4):
                prefix[h] = nn(d_scores[batch * 4 + h], less[...])

            def pick_up(a, carry):
                at = pl.ds(pl.multiple_of(a * 8, 8), 8)
                place_of = places[at, :]
                low, high = place_of & 127, place_of >> 7
                result = []
                for h in range(4):
                    value = jnp.zeros((8, 128), F32)
                    for j in range(4):
                        part = jnp.take_along_axis(prefix[h, at, j * 128 : (j + 1) * 128], low, axis=1)
                        value = jnp.where(high == j, part, value)
                    result.append(carry[h] + value)
                return tuple(result)

            sums += lax.fori_loop(
                0, LEN // 8, pick_up, tuple(jnp.zeros((8, 128), F32) for _ in range(4)), unroll=4
            )
        heads = jnp.concatenate(
            [jnp.sum(s, axis=0, keepdims=True) for s in sums] + [jnp.zeros((4, 128), F32)], axis=0
        )
        after = pltpu.roll(heads, 127, 1)
        whole = pltpu.roll(heads, 15, 1)
        lanes = lax.broadcasted_iota(jnp.int32, (16, 128), 1)
        buckets = jnp.where(lanes < 16, heads - after, after - heads)
        buckets = jnp.where(lanes == 15, heads, buckets)
        buckets = jnp.where(lanes == 16, 0.0, buckets)
        buckets = jnp.where(lanes == 31, whole - heads, buckets)
        buckets = jnp.where(lanes < 32, buckets, 0.0)
        placed = buckets if table == 0 else pltpu.roll(buckets, 32 * table, 1)
        flat_row = jnp.sum(nt(placed.astype(BF16), pick[table]) * keep[...], axis=0, keepdims=True)
        plane, at = spots["tables"]
        for i in range(3):
            row_at = at + 3 * table + i
            small[plane, row_at : row_at + 1, :] = flat_row[:, i * 128 : (i + 1) * 128]


def backward_pass(wall, cdoc, total, saved, features, coord_row, coord_col):
    pick, keep = table_constants()
    sds = jax.ShapeDtypeStruct
    return pl.pallas_call(
        backward_kernel,
        name="backward",
        out_shape=(sds((LEN, D), BF16), sds((2, ROWS, 128), BF16)),
        in_specs=[ANY] + [VMEM] * 4 + [ANY] + [VMEM] * 4 + [ANY] * 2 + [VMEM] * 7,
        out_specs=(VMEM, ANY),
        scratch_shapes=[
            pltpu.VMEM((2, ROWS, 128), BF16),
            pltpu.VMEM((2, ROWS, 128), BF16),
            pltpu.VMEM((LEN, D), F32),
            pltpu.VMEM((LEN, D), BF16),
            pltpu.VMEM((LEN, FF), BF16),
            pltpu.VMEM((LEN, FF), BF16),
            pltpu.VMEM((4, LEN, LEN), BF16),
            pltpu.VMEM((LEN, D), BF16),
            pltpu.VMEM((HEADS, LEN, LEN), BF16),
            pltpu.VMEM((LEN, LEN), BF16),
            pltpu.VMEM((4, LEN, LEN), F32),
            pltpu.VMEM((2, 64, 128), F32),
            pltpu.VMEM((16, 128), jnp.int32),
            pltpu.VMEM((LEN, 128), jnp.int32),
            pltpu.SemaphoreType.DMA((3,)),
            pltpu.SemaphoreType.DMA((1,)),
            pltpu.SemaphoreType.DMA((2,)),
        ],
        compiler_params=pltpu.CompilerParams(vmem_limit_bytes=64 * 2**20 - 2**18),
    )(wall, cdoc, total, *saved, features, coord_row, coord_col, jnp.asarray(pick), jnp.asarray(keep))


def reduce_kernel(stages, grads, pair_grad, out, pair_out, gstack, core_slots, x_slots, final, in_sem, fin_sem,
                  act_send, act_recv, c_send, c_recv, x_send, x_recv, b_send, b_recv, *rest):
    levels = len(stages)
    slots, sems = rest[:levels], rest[levels:]
    dp, fs = place()
    other = 1 - fs
    x_peer = (dp, other)
    core_peer = (dp + 1 - 2 * (dp % 2), fs)
    half = LEN // 2
    loads = [
        pltpu.make_async_copy(
            grads.at[:, pl.ds(i * CHUNK, CHUNK)], gstack.at[:, pl.ds(i * CHUNK, CHUNK)], in_sem.at[i]
        )
        for i in range(CHUNKS)
    ]
    order = [(2 * CHUNKS - 2 - i) % CHUNKS for i in range(CHUNKS)]
    for i in order:
        loads[i].start()
    greet(stages)

    sent = remote(pair_grad.at[rows_at(other * half, half)], pair_out, act_send.at[0], act_recv.at[0], x_peer)
    sent.start()

    parts = offsets(dp, stages, CHUNK)
    core_size = CHUNK // 2

    def core_copy(position, plane):
        base = order[position] * CHUNK
        return remote(
            gstack.at[plane, rows_at(base + (1 - dp % 2) * core_size, core_size)],
            core_slots.at[plane, position], c_send.at[position, plane], c_recv.at[position, plane], core_peer,
        )

    def x_copy(position):
        where = rows_at(order[position] * CHUNK + parts[0][0], core_size)
        return remote(gstack.at[other, where], x_slots.at[position], x_send.at[position], x_recv.at[position], x_peer)

    def scatter_copies(level, position):
        radix, stride = stages[level]
        start, size = parts[level]
        size = size // radix
        mine = (dp // stride) % radix
        copies = []
        for step in range(1, radix):
            target = (mine + step) % radix
            where = rows_at(order[position] * CHUNK + start + target * size, size)
            copies.append(
                remote(
                    gstack.at[fs, where], slots[level].at[position, step - 1],
                    sems[4 * level].at[position, step - 1], sems[4 * level + 1].at[position, step - 1],
                    (member(dp, radix, stride, target), fs),
                )
            )
        return copies

    def spread_copies(level, position, receive):
        radix, stride = stages[level]
        start, size = parts[level + 1]
        mine = (dp // stride) % radix
        copies = []
        for step in range(1, radix):
            shift = ((mine - step + radix) % radix - mine) * size if receive else 0
            where = final.at[rows_at(order[position] * CHUNK + start + shift, size)]
            copies.append(
                remote(
                    where, where, sems[4 * level + 2].at[position, step - 1], sems[4 * level + 3].at[position, step - 1],
                    (member(dp, radix, stride, (mine + step) % radix), fs),
                )
            )
        return copies

    def back_copy(position, receive):
        start = (1 - dp % 2 if receive else dp % 2) * core_size
        where = final.at[rows_at(order[position] * CHUNK + start, core_size)]
        return remote(where, where, b_send.at[position], b_recv.at[position], core_peer)

    def write_copy(position):
        where = pl.ds(order[position] * CHUNK, CHUNK)
        return pltpu.make_async_copy(final.at[where], out.at[where], fin_sem.at[position])

    def add_rows(plane, start, size, terms, target=None):
        where = rows_at(start, size)
        value = gstack[plane, where, :].astype(F32)
        for term in terms:
            value = value + term.astype(F32)
        if target is None:
            gstack[plane, where, :] = value.astype(BF16)
        else:
            target[where, :] = value.astype(BF16)

    def step_of(position, stage):
        base = order[position] * CHUNK
        if stage == 0:
            loads[order[position]].wait()
            for plane in range(2):
                core_copy(position, plane).start()
        elif stage == 1:
            for plane in range(2):
                core_copy(position, plane).wait_recv()
            add_rows(other, base + parts[0][0], core_size, [core_slots[other, position]])
            x_copy(position).start()
        elif stage <= levels + 2:
            level = stage - 2
            start, size = parts[level]
            if level == 0:
                x_copy(position).wait_recv()
                terms = [core_slots[fs, position], x_slots[position]]
            else:
                for copy in scatter_copies(level - 1, position):
                    copy.wait_recv()
                radix = stages[level - 1][0]
                terms = [slots[level - 1][position, i] for i in range(radix - 1)]
            if level < levels:
                add_rows(fs, base + start, size, terms)
                for copy in scatter_copies(level, position):
                    copy.start()
            else:
                add_rows(fs, base + start, size, terms, final)
                for copy in spread_copies(levels - 1, position, False):
                    copy.start()
        elif stage <= 2 * levels + 2:
            level = 2 * levels + 2 - stage
            for copy in spread_copies(level, position, True):
                copy.wait_recv()
            if level > 0:
                for copy in spread_copies(level - 1, position, False):
                    copy.start()
            else:
                back_copy(position, False).start()
        else:
            back_copy(position, True).wait_recv()
            write_copy(position).start()

    last = 2 * levels + 3
    for step in range(CHUNKS + last):
        for stage in range(last + 1):
            if 0 <= step - stage < CHUNKS:
                step_of(step - stage, stage)
    sent.wait()
    for position in range(CHUNKS):
        write_copy(position).wait()
        back_copy(position, False).wait_send()
        x_copy(position).wait_send()
        for plane in range(2):
            core_copy(position, plane).wait_send()
        for level in range(levels):
            for copy in scatter_copies(level, position) + spread_copies(level, position, False):
                copy.wait_send()


def reduce_grads(stages, grads, pair_grad):
    slots, sems = [], []
    size = CHUNK // 2
    for radix, _ in stages:
        size = size // radix
        slots.append(pltpu.VMEM((CHUNKS, radix - 1, size, 128), BF16))
        sems += [pltpu.SemaphoreType.DMA((CHUNKS, radix - 1))] * 4
    dma = pltpu.SemaphoreType.DMA
    return pl.pallas_call(
        functools.partial(reduce_kernel, stages),
        name="reduce_grads",
        out_shape=(jax.ShapeDtypeStruct((ROWS, 128), BF16), jax.ShapeDtypeStruct((LEN // 2, D), BF16)),
        in_specs=[ANY, VMEM],
        out_specs=(ANY, VMEM),
        scratch_shapes=[
            pltpu.VMEM((2, ROWS, 128), BF16),
            pltpu.VMEM((2, CHUNKS, CHUNK // 2, 128), BF16),
            pltpu.VMEM((CHUNKS, CHUNK // 2, 128), BF16),
            pltpu.VMEM((ROWS, 128), BF16),
            dma((CHUNKS,)), dma((CHUNKS,)), dma((1,)), dma((1,)),
            dma((CHUNKS, 2)), dma((CHUNKS, 2)), dma((CHUNKS,)), dma((CHUNKS,)), dma((CHUNKS,)), dma((CHUNKS,)),
        ]
        + slots
        + sems,
        compiler_params=pltpu.CompilerParams(
            collective_id=2, has_side_effects=True, vmem_limit_bytes=60 * 2**20
        ),
    )(grads, pair_grad)


BLOCK = 1760


def flatten_rows(plane, source, flat):
    def block(src, dst, count, stride):
        flat[pl.ds(LEAD + dst, count, stride=stride), :] = source[pl.ds(src, count), :].astype(F32)

    if plane == 0:
        for c in range(24):
            block(UP0 + c * UP_A, F_UP + c, UP_A, 24)
        for pos in range(18):
            block(pos * D, (pos % 3) * 6 + pos // 3, D, 18)
        for c in range(6):
            block(OUT0 + c * D, F_OUT + c, D, 6)
        small = source[pl.ds(SM0, 64), :].astype(F32)
        flat[pl.ds(LEAD + 13824, 12), :] = small[0:12]
        flat[pl.ds(LEAD + 18444, 18), :] = small[12:30]
    else:
        for c in range(24):
            block(UP1 + c * UP_B, c - 98, UP_B, 24)
        for c in range(6):
            block(DOWN1 + c * FF, F_DOWN1 + c, FF, 6)
        for c in range(6):
            block(LAY1 + c * FEAT, F_LAY1 + c, FEAT, 6)
        small = source[pl.ds(SM1, 64), :].astype(F32)
        flat[pl.ds(LEAD + F_UPB1, 24), :] = small[0:24]
        flat[pl.ds(LEAD + F_SM1, 18), :] = small[24:42]
        flat[pl.ds(LEAD + F_TAB1, 9), :] = small[42:51]
        rest = FLAT - F_TAB1 - 9
        flat[pl.ds(LEAD + F_TAB1 + 9, rest), :] = jnp.zeros((rest, 128), F32)


def adam_kernel(source, weights, first, second, grad_out, update_out, first_out, square, flat):
    step = pl.program_id(0)
    fs = lax.axis_index("fsdp")

    @pl.when(step == 0)
    def _():
        square[...] = jnp.zeros_like(square)

        @pl.when(fs == 0)
        def _():
            flatten_rows(0, source, flat)

        @pl.when(fs == 1)
        def _():
            flatten_rows(1, source, flat)

    part = 160
    row = lax.broadcasted_iota(jnp.int32, (part, 128), 0)

    def some(i, carry):
        at = pl.ds(pl.multiple_of(i * part, 8), part)
        begin = pl.multiple_of(step * BLOCK + i * part, 8)
        grad = flat[pl.ds(LEAD + begin, part), :]
        grad_out[at, :] = grad
        new_first = adam_one * first[at, :] + (1.0 - adam_one) * grad
        new_second = adam_two * second[at, :] + (1.0 - adam_two) * grad * grad
        corrected = (
            new_first
            / (1.0 - adam_one**adam_steps)
            / (jnp.sqrt(new_second / (1.0 - adam_two**adam_steps)) + adam_eps)
        )
        rate = jnp.where((fs == 1) & (row + begin >= F_LAY1), table_factor, 1.0)
        update_out[at, :] = rate * (corrected + decay_rate * weights[at, :])
        first_out[at, :] = new_first
        squares = grad * grad
        return carry + jnp.sum(squares.reshape(part // 8, 8, 128), axis=0)

    square[...] += lax.fori_loop(0, BLOCK // part, some, jnp.zeros((8, 128), F32))


def adam(source, weights, first, second):
    block = pl.BlockSpec((BLOCK, 128), lambda i: (i, 0))
    vector = jax.ShapeDtypeStruct((FLAT, 128), F32)
    return pl.pallas_call(
        adam_kernel,
        name="adamw",
        grid=(FLAT // BLOCK,),
        out_shape=(vector, vector, vector, jax.ShapeDtypeStruct((8, 128), F32)),
        in_specs=[VMEM, block, block, block],
        out_specs=(block, block, block, pl.BlockSpec((8, 128), lambda i: (0, 0))),
        scratch_shapes=[pltpu.VMEM((LEAD + FLAT + 288, 128), F32)],
        compiler_params=pltpu.CompilerParams(vmem_limit_bytes=60 * 2**20),
    )(source, weights, first, second)


def layout_features(coords):
    freq_count = FEAT // 8
    factors = (jnp.arange(freq_count, dtype=jnp.int32) + 1) ** 2
    phases = coords[..., :, None] * factors % 4096
    angles = phases.astype(F32) * (2.0 * math.pi / 4096.0)
    wave_parts = jnp.concatenate([jnp.sin(angles), jnp.cos(angles)], axis=-1)
    return wave_parts.reshape(coords.shape[:-1] + (FEAT,))


def local(stages, inputs, box_coords, mlm_mask, cotangent, params, first_moment, second_moment):
    fs = lax.axis_index("fsdp")
    half = LEN // 2
    masked = cotangent * mlm_mask.astype(BF16)[..., None]
    count = jnp.full((8, 128), jnp.sum(mlm_mask.astype(F32)))
    boxes = lax.dynamic_index_in_dim(box_coords, fs, 0, keepdims=False)
    features = layout_features(boxes).astype(BF16)
    coord_col = jnp.stack(
        [jnp.arange(LEN, dtype=jnp.int32), boxes[:, 0] + boxes[:, 2], boxes[:, 1] + boxes[:, 3]], axis=1
    )
    coord_row = coord_col.T
    flat = [v.reshape(FLAT, 128) for v in (params, first_moment, second_moment)]
    wall, xdoc, cdoc, total = gather_weights(stages, flat[0], inputs, masked, count)
    out_doc, *saved = forward_pass(wall, xdoc, features, coord_row, coord_col)
    grad_doc, grads = backward_pass(wall, cdoc, total, saved, features, coord_row, coord_col)
    reduced, grad_other = reduce_grads(stages, grads, grad_doc)
    out_other = lax.ppermute(
        lax.dynamic_slice_in_dim(out_doc, (1 - fs) * half, half, 0), "fsdp", [(0, 1), (1, 0)]
    )

    def owned(doc, moved):
        mine = lax.dynamic_slice_in_dim(doc, fs * half, half, 0)
        return jnp.where(fs == 0, jnp.stack([mine, moved]), jnp.stack([moved, mine]))

    grad, update, new_first, square = adam(reduced, *flat)
    norm = jnp.sqrt(lax.psum(jnp.sum(square), "fsdp"))
    return (
        owned(out_doc, out_other),
        owned(grad_doc, grad_other),
        grad.reshape(-1),
        norm,
        update.reshape(-1),
        new_first.reshape(-1),
    )


def solution(mesh):
    in_specs = (
        P("dp", "fsdp", None),
        P("dp", None, None),
        P("dp", "fsdp"),
        P("dp", "fsdp", None),
        P("fsdp"),
        P("fsdp"),
        P("fsdp"),
    )
    out_specs = (P("dp", "fsdp", None), P("dp", "fsdp", None), P("fsdp"), P(), P("fsdp"), P("fsdp"))
    stages = radices(mesh.shape["dp"])
    return jax.shard_map(
        functools.partial(local, stages), mesh=mesh, in_specs=in_specs, out_specs=out_specs, check_vma=False
    )
```

time: 1500 us -> 476 us (0.32); the launches traced: 1470 us -> 471 us
  waiting for transfers between devices: 494 us -> 0.01 us
  Pallas kernels: 0 us -> 448 us
  local copies, waits for them, and re-layouts: 360 us -> 5.01 us
  blocking collectives: 350 us -> 5.55 us
  matrix products: 158 us -> 0 us
  other arithmetic: 94.5 us -> 9.8 us
  between operations: 18.5 us -> 3.03 us
    pallas_call x0 -> x5, Pallas kernels: none -> 448 us  [the longest x1 121 us: backward_pass(): pl.pallas_call(backward_kernel, name='backward', out_shape=(sds((LEN, D),...]
    unnamed x8 -> x0, waiting for transfers between devices: 325 us -> none
    unnamed x1 -> x0, blocking collectives: 301 us -> none
    unnamed x117 -> x10, local copies, waits for them, and re-layouts: 197 us -> 0.03 us
    all_gather x4 -> x0, waiting for transfers between devices: 169 us -> none  [the longest x1 97.6 us: local(): lax.all_gather(params.astype(jnp.bfloat16), 'fsdp', axis=0, tiled=True)]
    dot_general x27 -> x0, matrix products: 158 us -> none  [the longest x1 18.8 us: block_scores(): jnp.einsum('bqhd,bkhd->bhqk', query_part, key_part, preferred_element_typ...]
    reshape x14 -> x0, local copies, waits for them, and re-layouts: 53 us -> none  [the longest x5 26.4 us: unpack(): flat_vector[offset:offset + length].reshape(entry_shape)]
    psum x2 -> x1, blocking collectives: 48 us -> 5.55 us  [local(): norm = jnp.sqrt(lax.psum(jnp.sum(square), 'fsdp'))]
  transfers between devices with their start and end apart: 7 -> 1, of which waited for: 3 -> 0; matrix products, arithmetic and copies ran while one was open for 17% -> 0% of each run, Pallas kernels for 0% -> 60%
where the time goes in v1:
time: 476 us; the launch traced here: 471 us
  Pallas kernels  448 us (94%)
  other arithmetic  9.8 us (2%)
  blocking collectives  5.55 us (1%)
  local copies, waits for them, and re-layouts  5.01 us (1%)
    pallas_call x1, Pallas kernels, backward_pass(): pl.pallas_call(backward_kernel, name='backward', out_shape=(sds((LEN, D),...  121 us
    pallas_call x1, Pallas kernels, reduce_grads(): pl.pallas_call(functools.partial(reduce_kernel, stages), name='reduce_gra...  118 us
    pallas_call x1, Pallas kernels, forward_pass(): pl.pallas_call(forward_kernel, name='forward', out_shape=(sds((LEN, D), B...  83.4 us
    pallas_call x1, Pallas kernels, gather_weights(): pl.pallas_call(functools.partial(gather_kernel, stages), name='gather_wei...  81.5 us
    pallas_call x1, Pallas kernels, adam(): pl.pallas_call(adam_kernel, name='adamw', grid=(FLAT // BLOCK,), out_shap...  43.7 us
  transfers between devices with their start and end apart: 1, of which 0 were waited for; matrix products, arithmetic and copies ran while one was open for 0% of the time, Pallas kernels for 60%

profile of v1, /device:TPU:0, one launch (start us, length us, event | category | flops | bytes accessed | tf_op | source)
XLA Modules:
  0.0 471.1 jit_solution(12009825452684915809)
XLA Ops:
  0.6 0.0 copy-start
  0.7 0.7 convert_element_type.12
  1.4 1.3 convert_reduce_fusion
  2.6 0.0 copy-done
  2.7 0.6 pad_add_fusion
  3.3 0.9 copy.27.coord_col
  4.2 0.6 sine_convert_fusion
  4.8 0.7 copy.26.features
  5.5 2.1 broadcast_multiply_fusion.cot
  7.7 1.2 broadcast_in_dim.2.cnt
  8.9 81.5 %gather_weights.1 = (bf16[2,28672,128]{2,1,0:T(8,128)(2,1)}, bf16[512,768]{1,0:T(8,128)(2,1)}, bf16[512,768]{1,0:T(8,128)(2,1)}, f32[8,128]{1,0:T(8,128)}) custom-call(f32[28160,128]{1,0:T(8,128)} %bitcast.17, bf16[2,256,768]{2,1,0:T(8,128)(2,1)} %xin.1, bf16[2,256,768]{2,1,0:T(8,128)(2,1)} %broadcast_multiply_fusion.cot, f32[8,128]{1,0:T(8,128)} %broadcast_in_dim.2.cnt), custom_call_target="tpu_custom_call" | custom-call | tf_op jit(solution)/shard_map/gather_weights/pallas_call | solution.py:355
  90.4 83.4 %forward.1 = (bf16[512,768]{1,0:T(8,128)(2,1)}, bf16[512,768]{1,0:T(8,128)(2,1)}, bf16[18,512,128]{2,1,0:T(8,128)(2,1)}, bf16[12,512,512]{2,1,0:T(8,128)(2,1)}, ...) custom-call(bf16[2,28672,128]{2,1,0:T(8,128)(2,1)} %get-tuple-elemen, ...), custom_call_target="tpu_custom_call" | custom-call | tf_op jit(solution)/shard_map/forward/pallas_call | solution.py:563
  173.8 2.1 dynamic-slice_bitcast_fusion.1
  175.9 0.1 collective-permute-start
  176.0 120.9 %backward.1 = (bf16[512,768]{1,0:T(8,128)(2,1)}, bf16[2,28672,128]{2,1,0:T(8,128)(2,1)}) custom-call(bf16[2,28672,128]{2,1,0:T(8,128)(2,1)} %get-tuple-element.30.wall_hbm, bf16[512,768]{1,0:T(8,128)(2,1)} %get-tuple-element.33.cdoc, f32[8,128]{1,0:T(8,128)} %get-tuple-element.34.total, bf16[512,768]{1,0:T(8,128)(2,1)} %get-tuple-element.35.rounded, ...), custom_call_target="tpu_custom_call" | custom-call | tf_op jit(solution)/shard_map/backward/pallas_call | solution.py:853
  296.8 118.2 %reduce_grads.1 = (bf16[28672,128]{1,0:T(8,128)(2,1)}, bf16[256,768]{1,0:T(8,128)(2,1)}) custom-call(bf16[2,28672,128]{2,1,0:T(8,128)(2,1)} %get-tuple-element.47.grads, bf16[512,768]{1,0:T(8,128)(2,1)} %get-tuple-element.46.pair_grad), custom_call_target="tpu_custom_call" | custom-call | tf_op jit(solution)/shard_map/reduce_grads/pallas_call | solution.py:1040
  415.0 0.0 copy-start.2
  415.0 0.0 copy-start.1
  415.0 43.7 %adamw.1 = (f32[28160,128]{1,0:T(8,128)}, f32[28160,128]{1,0:T(8,128)}, f32[28160,128]{1,0:T(8,128)}, f32[8,128]{1,0:T(8,128)}) custom-call(bf16[28672,128]{1,0:T(8,128)(2,1)} %get-tuple-element.49.source, f32[28160,128]{1,0:T(8,128)} %bitcast.18, f32[28160,128]{1,0:T(8,128)} %bitcast.19, f32[28160,128]{1,0:T(8,128)} %bitcast.20), custom_call_target="tpu_custom_call" | custom-call | tf_op jit(solution)/shard_map/adamw/pallas_call | solution.py:1137
  458.8 1.3 reduce_sum.19
  460.0 5.5 %psum.7 = f32[]{:T(128)} all-reduce(f32[]{:T(128)} %reduce_sum.19), channel_id=1, replica_groups=mesh['dp'=16,'fsdp'=2] {'fsdp'}, use_global_device_ids=true, to_apply=%region_2.3 | all-reduce | flops 1 | bytes 8 | tf_op jit(solution)/shard_map/psum | solution.py:1183
  466.4 1.0 maximum_select_fusion.1
  467.4 0.0 collective-permute-done
  467.4 2.2 maximum_select_fusion
  (12 shorter events, 0.1 us)
Async XLA Ops:
  0.6 2.0 copy-start
  175.9 291.5 %collective-permute-start = (bf16[256,768]{1,0:T(8,128)(2,1)}, bf16[256,768]{1,0:T(8,128)(2,1)}, u32[]{:S(2)}, u32[]{:S(2)}) collective-permute-start(bf16[256,768]{1,0:T(8,128)(2,1)} %get-tuple-element.55), channel_id=1, source_target_pairs={{0,1},{1,0},{2,3},{3,2},{4,5},{5,4},{6,7},{7,6},{8,9},{9,8},{10,11... | collective-permute-start | bytes 1179656 | tf_op jit(solution)/shard_map/ppermute | solution.py:1174
  415.0 51.3 %copy-start.2 = (bf16[512,768]{1,0:T(8,128)(2,1)S(1)}, bf16[512,768]{1,0:T(8,128)(2,1)}, u32[]{:S(2)}) copy-start(bf16[512,768]{1,0:T(8,128)(2,1)} %get-tuple-element.46.pair_grad) | copy-start | bytes 2359300
  415.0 51.3 %copy-start.4 = (bf16[256,768]{1,0:T(8,128)(2,1)S(1)}, bf16[256,768]{1,0:T(8,128)(2,1)}, u32[]{:S(2)}) copy-start(bf16[256,768]{1,0:T(8,128)(2,1)} %get-tuple-element.48) | copy-start | bytes 1179652
  415.0 52.3 %copy-start.3 = (bf16[1,256,768]{2,1,0:T(8,128)(2,1)S(1)}, bf16[1,256,768]{2,1,0:T(8,128)(2,1)}, u32[]{:S(2)}) copy-start(bf16[1,256,768]{2,1,0:T(8,128)(2,1)} %get-tuple-element.54) | copy-start | bytes 1179652
  415.0 54.5 %copy-start.1 = (s32[2,512,4]{1,2,0:T(4,128)S(1)}, s32[2,512,4]{1,2,0:T(4,128)}, u32[]{:S(2)}) copy-start(s32[2,512,4]{1,2,0:T(4,128)} %param.12) | copy-start | bytes 49156

commit v2 on v1

--- a/solution.py
+++ b/solution.py
@@ -46,7 +46,8 @@
 SM0 = UP0 + 24 * UP_A
 UP1 = 0
 DOWN1 = 24 * UP_B
-LAY1 = DOWN1 + 6 * FF
+DOWN_END = DOWN1 + 6 * FF
+LAY1 = 27648
 SM1 = LAY1 + 6 * FEAT
 F_OUT = 13836
 F_UP = 18462
@@ -147,6 +148,12 @@
             out[plane, pl.ds(dst, count), :] = flat[pl.ds(LEAD + src, count), :].astype(BF16)
 
         tasks.append((dst + count, run))
+
+    def clear(low, high):
+        def run():
+            out[plane, pl.ds(low, high - low), :] = jnp.zeros((high - low, 128), BF16)
+
+        tasks.append((high, run))
 
     if plane == 0:
         for pos in range(18):
@@ -161,8 +168,10 @@
     else:
         for c in range(24):
             block(UP1 + c * UP_B, c - 98, UP_B, 24)
-        for c in range(6):
-            block(DOWN1 + c * FF, F_DOWN1 + c, FF, 6)
+        for j in range(12):
+            for c in range(6):
+                block(DOWN1 + j * 1536 + c * 256, F_DOWN1 + j * 1536 + c, 256, 6)
+        clear(DOWN_END, LAY1)
         for c in range(6):
             block(LAY1 + c * FEAT, F_LAY1 + c, FEAT, 6)
         window(SM1, 8728, 32)
@@ -170,10 +179,7 @@
         window(SM1 + 64, 27976, 16)
         used = SM1 + 80
 
-    def clear():
-        out[plane, pl.ds(used, ROWS - used), :] = jnp.zeros((ROWS - used, 128), BF16)
-
-    tasks.append((ROWS, clear))
+    clear(used, ROWS)
     return tasks
 
 
@@ -416,7 +422,7 @@
 
 def down_rows(wall, j):
     return jnp.concatenate(
-        [wall[1, rows_at(DOWN1 + c * FF + j * 256, 256), :] for c in range(6)], axis=1
+        [wall[1, rows_at(DOWN1 + j * 1536 + c * 256, 256), :] for c in range(6)], axis=1
     )
 
 
@@ -441,16 +447,61 @@
     return centered * inverse, inverse
 
 
+def find_places(coord_col, lut, places):
+    lane = lax.broadcasted_iota(jnp.int32, (8, 128), 1)
+    step = lane % 16
+    level = jnp.where(step <= 8, step, lax.shift_left(jnp.full_like(step, 8), jnp.maximum(step - 8, 0)))
+    edge = jnp.where(lane < 16, 1 - level, jnp.where(lane == 16, 1 << 12, level))
+
+    def line_rows(a, carry):
+        at = pl.ds(pl.multiple_of(a * 8, 8), 8)
+        value = coord_col[at, 0:1] + edge
+        places[0, at, :] = jnp.where(value <= 0, LEN, jnp.minimum(value, LEN) - 1)
+        return carry
+
+    lax.fori_loop(0, LEN // 8, line_rows, 0, unroll=4)
+    for table in (1, 2):
+        def look(a, best):
+            at = pl.ds(pl.multiple_of(a * 8, 8), 8)
+            near = jnp.broadcast_to(coord_col[at, table : table + 1], (8, 128))
+            code = near * LEN + (lax.broadcasted_iota(jnp.int32, (8, 128), 0) + a * 8)
+            return tuple(
+                jnp.maximum(best[g], jnp.where(near < lane + 128 * g, code, -1)) for g in range(16)
+            )
+
+        best = lax.fori_loop(
+            0, LEN // 8, look, tuple(jnp.full((8, 128), -1, jnp.int32) for _ in range(16)), unroll=2
+        )
+        for g in range(16):
+            most = jnp.max(best[g], axis=0, keepdims=True)
+            lut[g : g + 1, :] = jnp.where(most < 0, LEN, most & (LEN - 1))
+        luts = [jnp.broadcast_to(lut[g : g + 1, :], (8, 128)) for g in range(16)]
+
+        def find(a, carry):
+            at = pl.ds(pl.multiple_of(a * 8, 8), 8)
+            value = jnp.clip(coord_col[at, table : table + 1] + edge, 0, 2047)
+            low, high = value & 127, value >> 7
+            found = jnp.full((8, 128), LEN, jnp.int32)
+            for g in range(16):
+                found = jnp.where(high == g, jnp.take_along_axis(luts[g], low, axis=1), found)
+            places[table, at, :] = found
+            return carry
+
+        lax.fori_loop(0, LEN // 8, find, 0, unroll=4)
+
+
 def forward_kernel(
     wall_hbm, xdoc, features, coord_row, coord_col, pick, keep,
     layer_out, rounded, qkv, probs, mixed, normed_one, inverse_one, first_low, hidden, slope,
-    normed_two, inverse_two,
-    wall, start, up_bias, acc, bias, sem,
+    normed_two, inverse_two, places, wall_out,
+    wall, start, up_bias, acc, bias, indices, lut, sem,
 ):
     load = pltpu.make_async_copy(wall_hbm, wall, sem.at[0])
     load.start()
     load.wait()
     merge_up(wall)
+    store = pltpu.make_async_copy(wall, wall_out, sem.at[0])
+    store.start()
     small0 = wall[0, pl.ds(SM0, 48), :].astype(F32)
     small1 = wall[1, pl.ds(SM1, 80), :].astype(F32)
     qv_bias = row_of(small0, 0, 12)
@@ -468,15 +519,26 @@
         heads_by_lane = heads_by_lane + nn(spread, pick[table])
     rows_by_head = [jnp.broadcast_to(heads_by_lane[h : h + 1, :], (8, 128)) for h in range(HEADS)]
 
+    def index_rows(a, carry):
+        at = pl.ds(pl.multiple_of(a * 8, 8), 8)
+        for table in range(3):
+            near = jnp.broadcast_to(coord_col[at, table : table + 1], (8, 128))
+            for j in range(4):
+                far = coord_row[table : table + 1, j * 128 : (j + 1) * 128]
+                indices[table, at, j * 128 : (j + 1) * 128] = (
+                    bucket_of(jnp.broadcast_to(far, (8, 128)) - near) + 32 * table
+                )
+        return carry
+
+    lax.fori_loop(0, LEN // 8, index_rows, 0, unroll=4)
+
     def bias_rows(a, carry):
         at = pl.ds(pl.multiple_of(a * 8, 8), 8)
         for j in range(4):
             lanes = pl.ds(j * 128, 128)
             sums = [None] * HEADS
             for table in range(3):
-                far = coord_row[table : table + 1, j * 128 : (j + 1) * 128]
-                near = coord_col[at, table : table + 1]
-                index = bucket_of(jnp.broadcast_to(far, (8, 128)) - near) + 32 * table
+                index = indices[table, at, lanes]
                 for h in range(HEADS):
                     found = jnp.take_along_axis(rows_by_head[h], index, axis=1)
                     sums[h] = found if sums[h] is None else sums[h] + found
@@ -484,7 +546,8 @@
                 bias[h, at, lanes] = sums[h]
         return carry
 
-    lax.fori_loop(0, LEN // 8, bias_rows, 0)
+    lax.fori_loop(0, LEN // 8, bias_rows, 0, unroll=4)
+    find_places(coord_col, lut, places)
 
     left = lax.broadcasted_iota(jnp.int32, (LEN, 128), 1) < HDIM
     for pair in range(PAIRS):
@@ -501,18 +564,22 @@
 
     def attend(pair, carry):
         query, key, value = qkv[3 * pair], qkv[3 * pair + 1], qkv[3 * pair + 2]
-        found = []
+        found = [[], []]
         for side in range(2):
             head = 2 * pair + side
             mine = left if side == 0 else jnp.logical_not(left)
-            for at in (slice(r, r + QROWS) for r in range(0, LEN, QROWS)):
+            for r in range(0, LEN, QROWS):
+                at = slice(r, r + QROWS)
                 part = query[at]
                 scores = nt(jnp.where(mine[at], part, jnp.zeros_like(part)), key) + bias[head, at, :]
                 scores = jnp.exp(scores - jnp.max(scores, axis=1, keepdims=True))
-                soft = scores * (1.0 / jnp.sum(scores, axis=1, keepdims=True))
-                probs[head, at, :] = soft.astype(BF16)
-            found.append(nn(probs[head], value))
-        mixed[:, pl.ds(pl.multiple_of(pair * 128, 128), 128)] = jnp.where(left, found[0], found[1]).astype(BF16)
+                soft = (scores * (1.0 / jnp.sum(scores, axis=1, keepdims=True))).astype(BF16)
+                for j in range(4):
+                    probs[rows_at((4 * head + j) * LEN + r, QROWS), :] = soft[:, j * 128 : (j + 1) * 128]
+                found[side].append(nn(soft, value))
+        mixed[:, pl.ds(pl.multiple_of(pair * 128, 128), 128)] = jnp.where(
+            left, jnp.concatenate(found[0], axis=0), jnp.concatenate(found[1], axis=0)
+        ).astype(BF16)
         return carry
 
     lax.fori_loop(0, PAIRS, attend, 0)
@@ -555,6 +622,7 @@
         return carry
 
     lax.fori_loop(0, LEN // QROWS, second_rows, 0)
+    store.wait()
 
 
 def forward_pass(wall, xdoc, features, coord_row, coord_col):
@@ -567,7 +635,7 @@
             sds((LEN, D), BF16),
             sds((LEN, D), BF16),
             sds((18, LEN, 128), BF16),
-            sds((HEADS, LEN, LEN), BF16),
+            sds((HEADS * 4 * LEN, 128), BF16),
             sds((LEN, D), BF16),
             sds((LEN, D), F32),
             sds((LEN, 1), F32),
@@ -576,15 +644,19 @@
             sds((LEN, FF), BF16),
             sds((LEN, D), F32),
             sds((LEN, 1), F32),
+            sds((3, LEN, 128), jnp.int32),
+            sds((2, ROWS, 128), BF16),
         ),
         in_specs=[ANY] + [VMEM] * 6,
-        out_specs=(VMEM,) * 12,
+        out_specs=(VMEM,) * 13 + (ANY,),
         scratch_shapes=[
             pltpu.VMEM((2, ROWS, 128), BF16),
             pltpu.VMEM((LEN, D), F32),
             pltpu.VMEM((1, FF), F32),
             pltpu.VMEM((LEN, D), F32),
             pltpu.VMEM((HEADS, LEN, LEN), F32),
+            pltpu.VMEM((3, LEN, LEN), jnp.int32),
+            pltpu.VMEM((16, 128), jnp.int32),
             pltpu.SemaphoreType.DMA((1,)),
         ],
         compiler_params=pltpu.CompilerParams(vmem_limit_bytes=62 * 2**20),
@@ -609,35 +681,264 @@
     return jnp.sum(values.astype(F32), axis=0, keepdims=True)
 
 
+def reduce_chunk(stages):
+    replicas = 2
+    for radix, _ in stages:
+        replicas *= radix
+    return max(1024, 16 * replicas)
+
+
+SKEW = 2
+
+
+class Reduction:
+    def __init__(self, stages, gstack, out, core_slots, x_slots, pieces, slots, sems):
+        self.stages, self.gstack, self.out = stages, gstack, out
+        self.core_slots, self.x_slots, self.pieces, self.slots = core_slots, x_slots, pieces, slots
+        (self.c_send, self.c_recv, self.x_send, self.x_recv, self.b_send, self.b_recv, self.own_sem) = sems[:7]
+        self.sems = sems[7:]
+        self.dp, self.fs = place()
+        self.other = 1 - self.fs
+        self.size = reduce_chunk(stages)
+        self.count = ROWS // self.size
+        self.levels = len(stages)
+        self.parts = offsets(self.dp, stages, self.size)
+        self.half = self.size // 2
+        self.x_peer = (self.dp, self.other)
+        self.core_peer = (self.dp + 1 - 2 * (self.dp % 2), self.fs)
+
+    def base(self, position):
+        return lax.rem(2 * self.count - 2 - position, self.count) * self.size
+
+    def ready(self, row):
+        return jnp.maximum(self.count - 1 - (row + self.size - 1) // self.size, 0)
+
+    def core_copy(self, position, plane):
+        where = rows_at(self.base(position) + (1 - self.dp % 2) * self.half, self.half)
+        return remote(
+            self.gstack.at[plane, where], self.core_slots.at[plane, position],
+            self.c_send.at[plane, position], self.c_recv.at[plane, position], self.core_peer,
+        )
+
+    def x_copy(self, position):
+        where = rows_at(self.base(position) + self.parts[0][0], self.half)
+        return remote(
+            self.gstack.at[self.other, where], self.x_slots.at[position],
+            self.x_send.at[position], self.x_recv.at[position], self.x_peer,
+        )
+
+    def scatter_copies(self, level, position):
+        radix, stride = self.stages[level]
+        start, size = self.parts[level]
+        size = size // radix
+        mine = (self.dp // stride) % radix
+        copies = []
+        for step in range(1, radix):
+            target = (mine + step) % radix
+            where = rows_at(self.base(position) + start + target * size, size)
+            copies.append(
+                remote(
+                    self.gstack.at[self.fs, where], self.slots[level].at[position, step - 1],
+                    self.sems[4 * level].at[position, step - 1], self.sems[4 * level + 1].at[position, step - 1],
+                    (member(self.dp, radix, stride, target), self.fs),
+                )
+            )
+        return copies
+
+    def spread_copies(self, level, position, receive):
+        radix, stride = self.stages[level]
+        start, size = self.parts[level + 1]
+        mine = (self.dp // stride) % radix
+        copies = []
+        for step in range(1, radix):
+            shift = ((mine - step + radix) % radix - mine) * size if receive else 0
+            where = self.out.at[rows_at(self.base(position) + start + shift, size)]
+            source = self.pieces.at[position] if level == self.levels - 1 and not receive else where
+            copies.append(
+                remote(
+                    source, where,
+                    self.sems[4 * level + 2].at[position, step - 1], self.sems[4 * level + 3].at[position, step - 1],
+                    (member(self.dp, radix, stride, (mine + step) % radix), self.fs),
+                )
+            )
+        return copies
+
+    def own_copy(self, position):
+        start, size = self.parts[-1]
+        return pltpu.make_async_copy(
+            self.pieces.at[position], self.out.at[rows_at(self.base(position) + start, size)],
+            self.own_sem.at[position],
+        )
+
+    def back_copy(self, position, receive):
+        start = (1 - self.dp % 2 if receive else self.dp % 2) * self.half
+        where = self.out.at[rows_at(self.base(position) + start, self.half)]
+        return remote(where, where, self.b_send.at[position], self.b_recv.at[position], self.core_peer)
+
+    def feed(self, plane, low, high):
+        def one(position, carry):
+            self.core_copy(position, plane).start()
+            return carry
+
+        lax.fori_loop(low, high, one, 0)
+
+    def push(self, low, high):
+        def one(position, carry):
+            self.core_copy(position, self.other).wait_recv()
+            where = rows_at(self.base(position) + self.parts[0][0], self.half)
+            value = self.gstack[self.other, where, :].astype(F32) + self.core_slots[self.other, position].astype(F32)
+            self.gstack[self.other, where, :] = value.astype(BF16)
+            self.x_copy(position).start()
+            return carry
+
+        lax.fori_loop(low, high, one, 0)
+
+    def work(self, position, step):
+        levels = self.levels
+        base = self.base(position)
+        if step <= levels:
+            start, size = self.parts[step]
+            where = rows_at(base + start, size)
+            if step == 0:
+                self.core_copy(position, self.fs).wait_recv()
+                self.x_copy(position).wait_recv()
+                terms = [self.core_slots[self.fs, position], self.x_slots[position]]
+            else:
+                for copy in self.scatter_copies(step - 1, position):
+                    copy.wait()
+                terms = [self.slots[step - 1][position, i] for i in range(self.stages[step - 1][0] - 1)]
+            value = self.gstack[self.fs, where, :].astype(F32)
+            for term in terms:
+                value = value + term.astype(F32)
+            if step < levels:
+                self.gstack[self.fs, where, :] = value.astype(BF16)
+                for copy in self.scatter_copies(step, position):
+                    copy.start()
+            else:
+                self.pieces[position] = value.astype(BF16)
+                self.own_copy(position).start()
+                for copy in self.spread_copies(levels - 1, position, False):
+                    copy.start()
+        else:
+            level = 2 * levels - step
+            for copy in self.spread_copies(level, position, True):
+                copy.wait_recv()
+            for copy in self.spread_copies(level, position, False):
+                copy.wait_send()
+            if level == levels - 1:
+                self.own_copy(position).wait()
+                self.x_copy(position).wait_send()
+                for plane in range(2):
+                    self.core_copy(position, plane).wait_send()
+            if level > 0:
+                for copy in self.spread_copies(level - 1, position, False):
+                    copy.start()
+            else:
+                self.back_copy(position, False).start()
+
+    def tick(self, number):
+        for step in range(2 * self.levels, -1, -1):
+            position = number - SKEW * step
+
+            @pl.when((position >= 0) & (position < self.count))
+            def _(position=position, step=step):
+                self.work(position, step)
+
+    def ticks(self):
+        return self.count + 2 * SKEW * self.levels
+
+    def finish(self):
+        def one(position, carry):
+            self.back_copy(position, True).wait_recv()
+            self.back_copy(position, False).wait_send()
+            return carry
+
+        lax.fori_loop(0, self.count, one, 0)
+
+
+def reduction_scratch(stages):
+    size = reduce_chunk(stages)
+    count, half = ROWS // size, size // 2
+    dma = pltpu.SemaphoreType.DMA
+    slots, sems = [], []
+    for radix, _ in stages:
+        half = half // radix
+        slots.append(pltpu.VMEM((count, radix - 1, half, 128), BF16))
+        sems += [dma((count, radix - 1))] * 4
+    return (
+        [
+            pltpu.VMEM((2, count, size // 2, 128), BF16),
+            pltpu.VMEM((count, size // 2, 128), BF16),
+            pltpu.VMEM((count, half, 128), BF16),
+        ]
+        + slots,
+        [dma((2, count)), dma((2, count))] + [dma((count,))] * 5 + sems,
+    )
+
+
 def backward_kernel(
-    wall_hbm, cdoc, total, rounded, qkv, probs_hbm, mixed, normed_one, inverse_one, first_low, hidden_hbm,
-    slope_hbm, normed_two, inverse_two, features, coord_row, coord_col, pick, keep,
-    input_grad, grads,
-    wall, gstack, acc, branch, hidden, d_up, probs, d_mixed, d_scores, less, prefix, small, lut, places,
-    sem, out_sem, probs_sem,
+    stages,
+    wall_hbm, cdoc_hbm, total, rounded_hbm, qkv_hbm, probs_hbm, mixed_hbm, one_hbm, inverse_one, low_hbm, hidden_hbm,
+    slope_hbm, two_hbm, inverse_two, places_hbm, features, coord_row, coord_col, pick, keep,
+    input_grad, reduced, norm,
+    wall, gstack, acc, branch, hidden, d_up, low, rounded, qkv, mixed, normed_one, less, places, prefix, small,
+    square_slots, load_sem, step_sem, probs_sem, act_send, act_recv, act_sem, n_send, n_recv, *rest,
 ):
-    loads = [
-        pltpu.make_async_copy(wall_hbm, wall, sem.at[0]),
-        pltpu.make_async_copy(hidden_hbm, hidden, sem.at[1]),
-        pltpu.make_async_copy(slope_hbm, d_up, sem.at[2]),
+    levels = len(stages)
+    parts_vmem, sems = rest[: 3 + levels], rest[3 + levels :]
+    red = Reduction(stages, gstack, reduced, parts_vmem[0], parts_vmem[1], parts_vmem[2], parts_vmem[3:], sems)
+    dp, fs, other = red.dp, red.fs, red.other
+    half = LEN // 2
+
+    early = [
+        pltpu.make_async_copy(wall_hbm.at[:, pl.ds(SM0, 256)], wall.at[:, pl.ds(SM0, 256)], load_sem.at[0]),
+        pltpu.make_async_copy(cdoc_hbm, branch, load_sem.at[1]),
+        pltpu.make_async_copy(two_hbm, acc, load_sem.at[2]),
     ]
-    for load in loads:
+    lows = [pltpu.make_async_copy(low_hbm, low, load_sem.at[3])]
+    rest_loads = [
+        pltpu.make_async_copy(one_hbm, normed_one, load_sem.at[4]),
+        pltpu.make_async_copy(wall_hbm.at[0, pl.ds(0, UP0)], wall.at[0, pl.ds(0, UP0)], load_sem.at[5]),
+        pltpu.make_async_copy(mixed_hbm, mixed, load_sem.at[6]),
+        pltpu.make_async_copy(qkv_hbm, qkv, load_sem.at[7]),
+        pltpu.make_async_copy(rounded_hbm, rounded, load_sem.at[8]),
+        pltpu.make_async_copy(places_hbm, places, load_sem.at[9]),
+    ]
+
+    def step_loads(j):
+        lanes = pl.ds(pl.multiple_of(j * 256, 256), 256)
+        areas = [(1, DOWN1 + 1536 * j, 1536), (0, UP0 + 2 * UP_A * j, 2 * UP_A), (1, UP1 + 2 * UP_B * j, 2 * UP_B)]
+        copies = [
+            pltpu.make_async_copy(
+                wall_hbm.at[plane, rows_at(start, size)], wall.at[plane, rows_at(start, size)], step_sem.at[i, j]
+            )
+            for i, (plane, start, size) in enumerate(areas)
+        ]
+        copies.append(pltpu.make_async_copy(hidden_hbm.at[:, lanes], hidden.at[:, lanes], step_sem.at[3, j]))
+        copies.append(pltpu.make_async_copy(slope_hbm.at[:, lanes], d_up.at[:, lanes], step_sem.at[4, j]))
+        return copies
+
+    for load in early + lows:
         load.start()
 
-    def probs_copy(pair, slot):
-        return pltpu.make_async_copy(
-            probs_hbm.at[pl.ds(2 * pair, 2)], probs.at[pl.ds(2 * slot, 2)], probs_sem.at[slot]
-        )
-
-    probs_copy(0, 0).start()
-    for load in loads:
+    def start_loads(it, carry):
+        for load in step_loads(11 - it):
+            load.start()
+        return carry
+
+    lax.fori_loop(0, 12, start_loads, 0)
+    for load in rest_loads:
+        load.start()
+    greet(stages)
+    small[...] = jnp.zeros_like(small)
+    gstack[1, pl.ds(DOWN_END, LAY1 - DOWN_END), :] = jnp.zeros((LAY1 - DOWN_END, 128), BF16)
+    for load in early:
         load.wait()
-    merge_up(wall)
+
     small0 = wall[0, pl.ds(SM0, 48), :].astype(F32)
     small1 = wall[1, pl.ds(SM1, 80), :].astype(F32)
     gain_one = row_of(small0, 26, 6)
     gain_two = row_of(small1, 44, 6)
-    small[...] = jnp.zeros_like(small)
     spots = {name: (plane, first_row) for name, plane, first_row, _ in G_SMALL}
 
     def keep_small(name, vector):
@@ -650,20 +951,37 @@
 
     def second_rows(r, sums):
         at = pl.ds(pl.multiple_of(r * QROWS, QROWS), QROWS)
-        grad_out = cdoc[at, :].astype(F32) / count
-        normed = normed_two[at, :]
+        grad_out = branch[at, :].astype(F32) / count
+        normed = acc[at, :]
         result = spread_norm(normed, inverse_two[at, :], gain_two, grad_out)
         acc[at, :] = result
-        low = result.astype(BF16)
-        branch[at, :] = low
-        return sums[0] + total_rows(grad_out * normed), sums[1] + total_rows(grad_out), sums[2] + total_rows(low)
+        lower = result.astype(BF16)
+        branch[at, :] = lower
+        return sums[0] + total_rows(grad_out * normed), sums[1] + total_rows(grad_out), sums[2] + total_rows(lower)
 
     sums = lax.fori_loop(0, LEN // QROWS, second_rows, (none, none, none))
     for name, vector in zip(("gain_two", "shift_two", "down_bias"), sums):
         keep_small(name, vector)
     plane_up, at_up = spots["up_bias"]
-
-    def down_step(j, carry):
+    lows[0].wait()
+
+    def fed(plane, it):
+        row = UP0 + 2 * UP_A * (11 - it) if plane == 0 else DOWN1 + 1536 * (11 - it)
+        return red.ready(row)
+
+    def of_other(values):
+        return jnp.where(other == 0, values[0], values[1])
+
+    fine = red.count >= 28
+    tile_row = lax.broadcasted_iota(jnp.int32, (16, 128), 0)
+
+    def feed_step(it, carry):
+        j = 11 - it
+        for load in step_loads(j):
+            load.wait()
+        for plane in range(2):
+            red.feed(plane, fed(plane, it - 2), fed(plane, it - 1))
+        red.push(of_other([fed(p, it - 3) for p in range(2)]), of_other([fed(p, it - 2) for p in range(2)]))
         lanes = pl.ds(pl.multiple_of(j * 256, 256), 256)
         grad = nt(branch[...], down_rows(wall, j))
         part = (grad * d_up[:, lanes].astype(F32)).astype(BF16)
@@ -673,23 +991,35 @@
         small[plane_up, pl.ds(at_up + 2 * j + 1, 1), :] = sums[:, 128:]
         down = tn(hidden[:, lanes], branch[...]).astype(BF16)
         for c in range(6):
-            gstack[1, rows_at(DOWN1 + c * FF + j * 256, 256), :] = down[:, c * 128 : (c + 1) * 128]
-        return carry
-
-    lax.fori_loop(0, 12, down_step, 0)
-
-    def up_step(j, carry):
-        lanes = pl.ds(pl.multiple_of(j * 256, 256), 256)
-        part = d_up[:, lanes]
-        up = tn(first_low[...], part).astype(BF16)
+            gstack[1, rows_at(DOWN1 + j * 1536 + c * 256, 256), :] = down[:, c * 128 : (c + 1) * 128]
+        up = tn(low[...], part)
         for i in range(2):
             c = 2 * j + i
-            gstack[0, rows_at(UP0 + c * UP_A, UP_A), :] = up[:UP_A, i * 128 : (i + 1) * 128]
-            gstack[1, rows_at(UP1 + c * UP_B, UP_B), :] = up[D - UP_B :, i * 128 : (i + 1) * 128]
+            cut = jnp.where(c < 2, CUT + 1 - 400, CUT - 400)
+            columns = up[:, i * 128 : (i + 1) * 128]
+            tile = columns[400:416]
+            gstack[0, rows_at(UP0 + c * UP_A, 400), :] = columns[:400].astype(BF16)
+            gstack[0, rows_at(UP0 + c * UP_A + 400, 16), :] = jnp.where(tile_row < cut, tile, 0.0).astype(BF16)
+            gstack[1, rows_at(UP1 + c * UP_B, 16), :] = jnp.where(tile_row < cut, 0.0, tile).astype(BF16)
+            gstack[1, rows_at(UP1 + c * UP_B + 16, UP_B - 16), :] = columns[416:].astype(BF16)
         acc[...] += nt(part, up_block(wall, j))
         return carry
 
-    lax.fori_loop(0, 12, up_step, 0)
+    lax.fori_loop(0, 12, feed_step, 0)
+
+    def probs_copy(pair, slot):
+        size = 8 * LEN
+        return pltpu.make_async_copy(
+            probs_hbm.at[rows_at(pair * size, size)], wall.at[0, rows_at(UP0 + slot * size, size)], probs_sem.at[slot]
+        )
+
+    probs_copy(PAIRS - 1, 0).start()
+    last = red.count - 1
+    red.feed(0, fed(0, 10), fed(0, 11))
+    red.feed(1, fed(1, 10), last)
+    red.push(of_other([fed(p, 9) for p in range(2)]), of_other([fed(p, 10) for p in range(2)]))
+    for load in rest_loads:
+        load.wait()
 
     w_out = jnp.concatenate([wall[0, pl.ds(OUT0 + c * D, D), :] for c in range(6)], axis=1)
 
@@ -698,14 +1028,21 @@
         grad, normed = acc[at, :], normed_one[at, :]
         result = spread_norm(normed, inverse_one[at, :], gain_one, grad)
         acc[at, :] = result
-        low = result.astype(BF16)
-        branch[at, :] = low
-        d_mixed[at, :] = nt(low, w_out).astype(BF16)
-        return sums[0] + total_rows(grad * normed), sums[1] + total_rows(grad), sums[2] + total_rows(low)
+        lower = result.astype(BF16)
+        branch[at, :] = lower
+        low[at, :] = nt(lower, w_out).astype(BF16)
+        return sums[0] + total_rows(grad * normed), sums[1] + total_rows(grad), sums[2] + total_rows(lower)
 
     sums = lax.fori_loop(0, LEN // QROWS, first_rows, (none, none, none))
     for name, vector in zip(("gain_one", "shift_one", "out_bias"), sums):
         keep_small(name, vector)
+    red.push(of_other([fed(p, 10) for p in range(2)]), jnp.where(other == 0, fed(0, 11), last))
+
+    def drain(number, carry):
+        red.tick(number)
+        return carry
+
+    per_pair = 2 if fine else 1
 
     def out_step(j, carry):
         lanes = pl.ds(pl.multiple_of(j * 256, 256), 256)
@@ -715,31 +1052,53 @@
         return carry
 
     lax.fori_loop(0, 3, out_step, 0)
+    drain(0, 0)
+    drain(1, 0)
 
     left = lax.broadcasted_iota(jnp.int32, (LEN, 128), 1) < HDIM
 
-    def attend(pair, carry):
+    def sent(it):
+        return red.ready(jnp.where(it <= -2, UP0, 2304 * (5 - it)))
+
+    def score_rows(head, j, start, size):
+        return rows_at((4 * head + j) * LEN + start, size)
+
+    def attend(it, carry):
+        pair = PAIRS - 1 - it
+        slot = lax.rem(it, 2)
+
+        @pl.when(it + 1 < PAIRS)
+        def _():
+            probs_copy(pair - 1, 1 - slot).start()
+
+        red.feed(0, sent(it - 2), sent(it - 1))
+
+        @pl.when(other == 0)
+        def _():
+            red.push(sent(it - 3), sent(it - 2))
+
+        lax.fori_loop(2 + per_pair * it, 2 + per_pair * (it + 1), drain, 0)
+        probs_copy(pair, slot).wait()
         query, key, value = qkv[3 * pair], qkv[3 * pair + 1], qkv[3 * pair + 2]
-        slot = pair % 2
-
-        @pl.when(pair + 1 < PAIRS)
-        def _():
-            probs_copy(pair + 1, 1 - slot).start()
-
-        probs_copy(pair, slot).wait()
-        grad = d_mixed[:, pl.ds(pl.multiple_of(pair * 128, 128), 128)]
+        grad = low[:, pl.ds(pl.multiple_of(pair * 128, 128), 128)]
         found = []
         for side in range(2):
             head = 2 * pair + side
             mine = left if side == 0 else jnp.logical_not(left)
-            for at in (slice(r, r + QROWS) for r in range(0, LEN, QROWS)):
-                part = grad[at]
-                d_probs = nt(jnp.where(mine[at], part, jnp.zeros_like(part)), value)
-                soft = probs[2 * slot + side, at, :].astype(F32)
+            base = UP0 + slot * 8 * LEN + side * 4 * LEN
+            for r in range(0, LEN, QROWS):
+                part = grad[r : r + QROWS]
+                d_probs = nt(jnp.where(mine[r : r + QROWS], part, jnp.zeros_like(part)), value)
+                soft = jnp.concatenate(
+                    [wall[0, rows_at(base + j * LEN + r, QROWS), :] for j in range(4)], axis=1
+                ).astype(F32)
                 inner = jnp.sum(soft * d_probs, axis=1, keepdims=True)
-                d_scores[head, at, :] = (soft * (d_probs - inner)).astype(BF16)
-            scores = d_scores[head]
-            found.append((nn(scores, key), tn(scores, query), tn(probs[2 * slot + side], grad)))
+                scores = (soft * (d_probs - inner)).astype(BF16)
+                for j in range(4):
+                    wall[1, score_rows(head, j, r, QROWS), :] = scores[:, j * 128 : (j + 1) * 128]
+            scores = jnp.concatenate([wall[1, score_rows(head, j, 0, LEN), :] for j in range(4)], axis=1)
+            chances = jnp.concatenate([wall[0, rows_at(base + j * LEN, LEN), :] for j in range(4)], axis=1)
+            found.append((nn(scores, key), tn(scores, query), tn(chances, grad)))
         d_query = (jnp.where(left, found[0][0], found[1][0]) * HDIM**-0.5).astype(BF16)
         d_key = jnp.where(left, found[0][1], found[1][1]).astype(BF16)
         d_value = jnp.where(left, found[0][2], found[1][2]).astype(BF16)
@@ -756,68 +1115,119 @@
         return carry
 
     lax.fori_loop(0, PAIRS, attend, 0)
-    result = acc[...].astype(BF16)
-    input_grad[...] = result
-    layout = tn(features[...], result).astype(BF16)
+    red.feed(0, sent(4), sent(5))
+
+    @pl.when(other == 0)
+    def _():
+        red.push(sent(3), sent(4))
+
+    branch[...] = acc[...].astype(BF16)
+    act_out = remote(branch.at[rows_at(other * half, half)], input_grad.at[fs], act_send.at[0], act_recv.at[0], red.x_peer)
+    act_in = remote(branch.at[rows_at(other * half, half)], input_grad.at[other], act_send.at[0], act_recv.at[0], red.x_peer)
+    act_own = pltpu.make_async_copy(branch.at[rows_at(fs * half, half)], input_grad.at[fs], act_sem.at[0])
+    act_out.start()
+    act_own.start()
+    layout = tn(features[...], branch[...]).astype(BF16)
     for c in range(6):
         gstack[1, pl.ds(LAY1 + c * FEAT, FEAT), :] = layout[:, c * 128 : (c + 1) * 128]
 
-    table_grads(d_scores, coord_row, coord_col, pick, keep, less, prefix, small, lut, places, spots)
-
-    gstack[0, pl.ds(SM0, ROWS - SM0), :] = jnp.zeros((ROWS - SM0, 128), BF16)
-    gstack[1, pl.ds(SM1, ROWS - SM1), :] = jnp.zeros((ROWS - SM1, 128), BF16)
-    gstack[0, pl.ds(SM0, 64), :] = small[0].astype(BF16)
-    gstack[1, pl.ds(SM1, 64), :] = small[1].astype(BF16)
-    store = pltpu.make_async_copy(gstack, grads, out_sem.at[0])
-    store.start()
-    store.wait()
-
-
-def table_grads(d_scores, coord_row, coord_col, pick, keep, less, prefix, small, lut, places, spots):
-    lane = lax.broadcasted_iota(jnp.int32, (8, 128), 1)
-    step = lane % 16
-    level = jnp.where(step <= 8, step, lax.shift_left(jnp.full_like(step, 8), jnp.maximum(step - 8, 0)))
-    edge = jnp.where(lane < 16, 1 - level, jnp.where(lane == 16, 1 << 12, level))
-    rows = []
+    @pl.when(other == 0)
+    def _():
+        red.push(sent(4), sent(5))
+
+    late = 2 + per_pair * PAIRS
+    pace = 2 if fine else 5
+    table_grads(wall, coord_row, coord_col, pick, keep, less, places, prefix, small, spots, red, late, pace)
+    late += (23 + pace) // pace
+
+    for plane in range(2):
+        gstack[plane, pl.ds(SM0, 64), :] = small[plane].astype(BF16)
+        gstack[plane, pl.ds(SM0 + 64, ROWS - SM0 - 64), :] = jnp.zeros((ROWS - SM0 - 64, 128), BF16)
+        red.feed(plane, last, last + 1)
+    red.push(last, last + 1)
+
+    summed = red.count + SKEW * levels
+    lax.fori_loop(late, summed, drain, 0)
+
+    def squares(position, carry):
+        piece = red.pieces[position].astype(F32)
+        return carry + jnp.sum((piece * piece).reshape(-1, 8, 128), axis=0)
+
+    value = lax.fori_loop(0, red.count, squares, jnp.zeros((8, 128), F32))
+    value = jnp.sum(jnp.sum(value, axis=0, keepdims=True), axis=1, keepdims=True)
+    norm[...] = jnp.broadcast_to(value, (8, 128))
+    rounds = [
+        [
+            (member(dp, radix, stride, ((dp // stride) % radix + step) % radix), fs)
+            for step in range(1, radix)
+        ]
+        for radix, stride in stages
+    ] + [[red.core_peer], [red.x_peer]]
+
+    def square_copies(number):
+        base = sum(len(r) for r in rounds[:number])
+        return [
+            remote(norm.at[...], square_slots.at[base + i], n_send.at[base + i], n_recv.at[base + i], peer)
+            for i, peer in enumerate(rounds[number])
+        ]
+
+    for number in range(max(red.ticks() - summed, len(rounds)) + 1):
+        if number < len(rounds):
+            for copy in square_copies(number):
+                copy.start()
+        if summed + number < red.ticks():
+            red.tick(summed + number)
+        if number < len(rounds):
+            gathered = norm[...]
+            base = sum(len(r) for r in rounds[:number])
+            for i, copy in enumerate(square_copies(number)):
+                copy.wait()
+                gathered = gathered + square_slots[base + i]
+            norm[...] = gathered
+    norm[...] = jnp.sqrt(norm[...])
+
+    red.finish()
+    act_own.wait()
+    act_out.wait_send()
+    act_in.wait_recv()
+
+
+def table_grads(wall, coord_row, coord_col, pick, keep, less, places, prefix, small, spots, red, late, pace):
+    block = 64
     for table in range(3):
-        key_row = coord_row[table : table + 1, :]
-        key_col = coord_col[:, table : table + 1]
-        less[...] = jnp.where(
-            jnp.broadcast_to(key_col, (LEN, LEN)) <= jnp.broadcast_to(key_row, (LEN, LEN)), 1.0, 0.0
-        ).astype(BF16)
-        code = key_col * LEN + lax.broadcasted_iota(jnp.int32, (LEN, 1), 0)
-        for group in range(16):
-            value = lax.broadcasted_iota(jnp.int32, (LEN, 128), 1) + group * 128
-            best = jnp.max(
-                jnp.where(jnp.broadcast_to(key_col, (LEN, 128)) < value, jnp.broadcast_to(code, (LEN, 128)), -1),
-                axis=0, keepdims=True,
+        key_row = jnp.broadcast_to(coord_row[table : table + 1, :], (16, LEN))
+
+        def less_rows(a, carry):
+            at = pl.ds(pl.multiple_of(a * 16, 16), 16)
+            near = jnp.broadcast_to(coord_col[at, table : table + 1], (16, LEN))
+            less[at, :] = jnp.where(near <= key_row, 1.0, 0.0).astype(BF16)
+            return carry
+
+        lax.fori_loop(0, LEN // 16, less_rows, 0, unroll=4)
+
+        def query_rows(b, sums):
+            @pl.when(lax.rem(table * 8 + b, pace) == 0)
+            def _():
+                red.tick(late + (table * 8 + b) // pace)
+
+            start = b * block
+            scores = jnp.concatenate(
+                [
+                    jnp.concatenate(
+                        [wall[1, rows_at((4 * h + j) * LEN + start, block), :] for j in range(4)], axis=1
+                    )
+                    for h in range(HEADS)
+                ],
+                axis=0,
             )
-            lut[group : group + 1, :] = jnp.where(best < 0, LEN, best & (LEN - 1))
-
-        def find(a, carry):
-            at = pl.ds(pl.multiple_of(a * 8, 8), 8)
-            value = jnp.clip(coord_col[at, table : table + 1] + edge, 0, 2047)
-            low, high = value & 127, value >> 7
-            found = jnp.full((8, 128), LEN, jnp.int32)
-            for group in range(16):
-                row = jnp.broadcast_to(lut[group : group + 1, :], (8, 128))
-                found = jnp.where(high == group, jnp.take_along_axis(row, low, axis=1), found)
-            places[at, :] = found
-            return carry
-
-        lax.fori_loop(0, LEN // 8, find, 0)
-
-        sums = []
-        for batch in range(3):
-            for h in range(4):
-                prefix[h] = nn(d_scores[batch * 4 + h], less[...])
+            prefix[...] = nn(scores, less[...]).reshape(HEADS, block, LEN)
 
             def pick_up(a, carry):
                 at = pl.ds(pl.multiple_of(a * 8, 8), 8)
-                place_of = places[at, :]
+                place_of = places[table, pl.ds(pl.multiple_of(start + a * 8, 8), 8), :]
                 low, high = place_of & 127, place_of >> 7
                 result = []
-                for h in range(4):
+                for h in range(HEADS):
                     value = jnp.zeros((8, 128), F32)
                     for j in range(4):
                         part = jnp.take_along_axis(prefix[h, at, j * 128 : (j + 1) * 128], low, axis=1)
@@ -825,9 +1235,11 @@
                     result.append(carry[h] + value)
                 return tuple(result)
 
-            sums += lax.fori_loop(
-                0, LEN // 8, pick_up, tuple(jnp.zeros((8, 128), F32) for _ in range(4)), unroll=4
-            )
+            return lax.fori_loop(0, block // 8, pick_up, sums, unroll=4)
+
+        sums = lax.fori_loop(
+            0, LEN // block, query_rows, tuple(jnp.zeros((8, 128), F32) for _ in range(HEADS))
+        )
         heads = jnp.concatenate(
             [jnp.sum(s, axis=0, keepdims=True) for s in sums] + [jnp.zeros((4, 128), F32)], axis=0
         )
@@ -847,15 +1259,18 @@
             small[plane, row_at : row_at + 1, :] = flat_row[:, i * 128 : (i + 1) * 128]
 
 
-def backward_pass(wall, cdoc, total, saved, features, coord_row, coord_col):
+def backward_pass(stages, wall, cdoc, total, saved, features, coord_row, coord_col):
     pick, keep = table_constants()
     sds = jax.ShapeDtypeStruct
+    count_peers = 2 + sum(radix - 1 for radix, _ in stages)
+    dma = pltpu.SemaphoreType.DMA
+    buffers, sems = reduction_scratch(stages)
     return pl.pallas_call(
-        backward_kernel,
-        name="backward",
-        out_shape=(sds((LEN, D), BF16), sds((2, ROWS, 128), BF16)),
-        in_specs=[ANY] + [VMEM] * 4 + [ANY] + [VMEM] * 4 + [ANY] * 2 + [VMEM] * 7,
-        out_specs=(VMEM, ANY),
+        functools.partial(backward_kernel, stages),
+        name="backward_reduce",
+        out_shape=(sds((2, LEN // 2, D), BF16), sds((ROWS, 128), BF16), sds((8, 128), F32)),
+        in_specs=[ANY, ANY, VMEM, ANY, ANY, ANY, ANY, ANY, VMEM, ANY, ANY, ANY, ANY, VMEM, ANY] + [VMEM] * 5,
+        out_specs=(ANY, ANY, VMEM),
         scratch_shapes=[
             pltpu.VMEM((2, ROWS, 128), BF16),
             pltpu.VMEM((2, ROWS, 128), BF16),
@@ -863,200 +1278,24 @@
             pltpu.VMEM((LEN, D), BF16),
             pltpu.VMEM((LEN, FF), BF16),
             pltpu.VMEM((LEN, FF), BF16),
-            pltpu.VMEM((4, LEN, LEN), BF16),
             pltpu.VMEM((LEN, D), BF16),
-            pltpu.VMEM((HEADS, LEN, LEN), BF16),
+            pltpu.VMEM((LEN, D), BF16),
+            pltpu.VMEM((18, LEN, 128), BF16),
+            pltpu.VMEM((LEN, D), BF16),
+            pltpu.VMEM((LEN, D), F32),
             pltpu.VMEM((LEN, LEN), BF16),
-            pltpu.VMEM((4, LEN, LEN), F32),
+            pltpu.VMEM((3, LEN, 128), jnp.int32),
+            pltpu.VMEM((HEADS, 64, LEN), F32),
             pltpu.VMEM((2, 64, 128), F32),
-            pltpu.VMEM((16, 128), jnp.int32),
-            pltpu.VMEM((LEN, 128), jnp.int32),
-            pltpu.SemaphoreType.DMA((3,)),
-            pltpu.SemaphoreType.DMA((1,)),
-            pltpu.SemaphoreType.DMA((2,)),
-        ],
-        compiler_params=pltpu.CompilerParams(vmem_limit_bytes=64 * 2**20 - 2**18),
-    )(wall, cdoc, total, *saved, features, coord_row, coord_col, jnp.asarray(pick), jnp.asarray(keep))
-
-
-def reduce_kernel(stages, grads, pair_grad, out, pair_out, gstack, core_slots, x_slots, final, in_sem, fin_sem,
-                  act_send, act_recv, c_send, c_recv, x_send, x_recv, b_send, b_recv, *rest):
-    levels = len(stages)
-    slots, sems = rest[:levels], rest[levels:]
-    dp, fs = place()
-    other = 1 - fs
-    x_peer = (dp, other)
-    core_peer = (dp + 1 - 2 * (dp % 2), fs)
-    half = LEN // 2
-    loads = [
-        pltpu.make_async_copy(
-            grads.at[:, pl.ds(i * CHUNK, CHUNK)], gstack.at[:, pl.ds(i * CHUNK, CHUNK)], in_sem.at[i]
-        )
-        for i in range(CHUNKS)
-    ]
-    order = [(2 * CHUNKS - 2 - i) % CHUNKS for i in range(CHUNKS)]
-    for i in order:
-        loads[i].start()
-    greet(stages)
-
-    sent = remote(pair_grad.at[rows_at(other * half, half)], pair_out, act_send.at[0], act_recv.at[0], x_peer)
-    sent.start()
-
-    parts = offsets(dp, stages, CHUNK)
-    core_size = CHUNK // 2
-
-    def core_copy(position, plane):
-        base = order[position] * CHUNK
-        return remote(
-            gstack.at[plane, rows_at(base + (1 - dp % 2) * core_size, core_size)],
-            core_slots.at[plane, position], c_send.at[position, plane], c_recv.at[position, plane], core_peer,
-        )
-
-    def x_copy(position):
-        where = rows_at(order[position] * CHUNK + parts[0][0], core_size)
-        return remote(gstack.at[other, where], x_slots.at[position], x_send.at[position], x_recv.at[position], x_peer)
-
-    def scatter_copies(level, position):
-        radix, stride = stages[level]
-        start, size = parts[level]
-        size = size // radix
-        mine = (dp // stride) % radix
-        copies = []
-        for step in range(1, radix):
-            target = (mine + step) % radix
-            where = rows_at(order[position] * CHUNK + start + target * size, size)
-            copies.append(
-                remote(
-                    gstack.at[fs, where], slots[level].at[position, step - 1],
-                    sems[4 * level].at[position, step - 1], sems[4 * level + 1].at[position, step - 1],
-                    (member(dp, radix, stride, target), fs),
-                )
-            )
-        return copies
-
-    def spread_copies(level, position, receive):
-        radix, stride = stages[level]
-        start, size = parts[level + 1]
-        mine = (dp // stride) % radix
-        copies = []
-        for step in range(1, radix):
-            shift = ((mine - step + radix) % radix - mine) * size if receive else 0
-            where = final.at[rows_at(order[position] * CHUNK + start + shift, size)]
-            copies.append(
-                remote(
-                    where, where, sems[4 * level + 2].at[position, step - 1], sems[4 * level + 3].at[position, step - 1],
-                    (member(dp, radix, stride, (mine + step) % radix), fs),
-                )
-            )
-        return copies
-
-    def back_copy(position, receive):
-        start = (1 - dp % 2 if receive else dp % 2) * core_size
-        where = final.at[rows_at(order[position] * CHUNK + start, core_size)]
-        return remote(where, where, b_send.at[position], b_recv.at[position], core_peer)
-
-    def write_copy(position):
-        where = pl.ds(order[position] * CHUNK, CHUNK)
-        return pltpu.make_async_copy(final.at[where], out.at[where], fin_sem.at[position])
-
-    def add_rows(plane, start, size, terms, target=None):
-        where = rows_at(start, size)
-        value = gstack[plane, where, :].astype(F32)
-        for term in terms:
-            value = value + term.astype(F32)
-        if target is None:
-            gstack[plane, where, :] = value.astype(BF16)
-        else:
-            target[where, :] = value.astype(BF16)
-
-    def step_of(position, stage):
-        base = order[position] * CHUNK
-        if stage == 0:
-            loads[order[position]].wait()
-            for plane in range(2):
-                core_copy(position, plane).start()
-        elif stage == 1:
-            for plane in range(2):
-                core_copy(position, plane).wait_recv()
-            add_rows(other, base + parts[0][0], core_size, [core_slots[other, position]])
-            x_copy(position).start()
-        elif stage <= levels + 2:
-            level = stage - 2
-            start, size = parts[level]
-            if level == 0:
-                x_copy(position).wait_recv()
-                terms = [core_slots[fs, position], x_slots[position]]
-            else:
-                for copy in scatter_copies(level - 1, position):
-                    copy.wait_recv()
-                radix = stages[level - 1][0]
-                terms = [slots[level - 1][position, i] for i in range(radix - 1)]
-            if level < levels:
-                add_rows(fs, base + start, size, terms)
-                for copy in scatter_copies(level, position):
-                    copy.start()
-            else:
-                add_rows(fs, base + start, size, terms, final)
-                for copy in spread_copies(levels - 1, position, False):
-                    copy.start()
-        elif stage <= 2 * levels + 2:
-            level = 2 * levels + 2 - stage
-            for copy in spread_copies(level, position, True):
-                copy.wait_recv()
-            if level > 0:
-                for copy in spread_copies(level - 1, position, False):
-                    copy.start()
-            else:
-                back_copy(position, False).start()
-        else:
-            back_copy(position, True).wait_recv()
-            write_copy(position).start()
-
-    last = 2 * levels + 3
-    for step in range(CHUNKS + last):
-        for stage in range(last + 1):
-            if 0 <= step - stage < CHUNKS:
-                step_of(step - stage, stage)
-    sent.wait()
-    for position in range(CHUNKS):
-        write_copy(position).wait()
-        back_copy(position, False).wait_send()
-        x_copy(position).wait_send()
-        for plane in range(2):
-            core_copy(position, plane).wait_send()
-        for level in range(levels):
-            for copy in scatter_copies(level, position) + spread_copies(level, position, False):
-                copy.wait_send()
-
-
-def reduce_grads(stages, grads, pair_grad):
-    slots, sems = [], []
-    size = CHUNK // 2
-    for radix, _ in stages:
-        size = size // radix
-        slots.append(pltpu.VMEM((CHUNKS, radix - 1, size, 128), BF16))
-        sems += [pltpu.SemaphoreType.DMA((CHUNKS, radix - 1))] * 4
-    dma = pltpu.SemaphoreType.DMA
-    return pl.pallas_call(
-        functools.partial(reduce_kernel, stages),
-        name="reduce_grads",
-        out_shape=(jax.ShapeDtypeStruct((ROWS, 128), BF16), jax.ShapeDtypeStruct((LEN // 2, D), BF16)),
-        in_specs=[ANY, VMEM],
-        out_specs=(ANY, VMEM),
-        scratch_shapes=[
-            pltpu.VMEM((2, ROWS, 128), BF16),
-            pltpu.VMEM((2, CHUNKS, CHUNK // 2, 128), BF16),
-            pltpu.VMEM((CHUNKS, CHUNK // 2, 128), BF16),
-            pltpu.VMEM((ROWS, 128), BF16),
-            dma((CHUNKS,)), dma((CHUNKS,)), dma((1,)), dma((1,)),
-            dma((CHUNKS, 2)), dma((CHUNKS, 2)), dma((CHUNKS,)), dma((CHUNKS,)), dma((CHUNKS,)), dma((CHUNKS,)),
+            pltpu.VMEM((count_peers, 8, 128), F32),
+            dma((10,)), dma((5, 12)), dma((2,)), dma((1,)), dma((1,)), dma((1,)), dma((count_peers,)), dma((count_peers,)),
         ]
-        + slots
+        + buffers
         + sems,
         compiler_params=pltpu.CompilerParams(
-            collective_id=2, has_side_effects=True, vmem_limit_bytes=60 * 2**20
+            collective_id=2, has_side_effects=True, vmem_limit_bytes=64 * 2**20 - 2**16
         ),
-    )(grads, pair_grad)
+    )(wall, cdoc, total, *saved, features, coord_row, coord_col, jnp.asarray(pick), jnp.asarray(keep))
 
 
 BLOCK = 1760
@@ -1079,8 +1318,9 @@
     else:
         for c in range(24):
             block(UP1 + c * UP_B, c - 98, UP_B, 24)
-        for c in range(6):
-            block(DOWN1 + c * FF, F_DOWN1 + c, FF, 6)
+        for j in range(12):
+            for c in range(6):
+                block(DOWN1 + j * 1536 + c * 256, F_DOWN1 + j * 1536 + c, 256, 6)
         for c in range(6):
             block(LAY1 + c * FEAT, F_LAY1 + c, FEAT, 6)
         small = source[pl.ds(SM1, 64), :].astype(F32)
@@ -1091,14 +1331,12 @@
         flat[pl.ds(LEAD + F_TAB1 + 9, rest), :] = jnp.zeros((rest, 128), F32)
 
 
-def adam_kernel(source, weights, first, second, grad_out, update_out, first_out, square, flat):
+def adam_kernel(source, weights, first, second, grad_out, update_out, first_out, flat):
     step = pl.program_id(0)
     fs = lax.axis_index("fsdp")
 
     @pl.when(step == 0)
     def _():
-        square[...] = jnp.zeros_like(square)
-
         @pl.when(fs == 0)
         def _():
             flatten_rows(0, source, flat)
@@ -1125,10 +1363,9 @@
         rate = jnp.where((fs == 1) & (row + begin >= F_LAY1), table_factor, 1.0)
         update_out[at, :] = rate * (corrected + decay_rate * weights[at, :])
         first_out[at, :] = new_first
-        squares = grad * grad
-        return carry + jnp.sum(squares.reshape(part // 8, 8, 128), axis=0)
-
-    square[...] += lax.fori_loop(0, BLOCK // part, some, jnp.zeros((8, 128), F32))
+        return carry
+
+    lax.fori_loop(0, BLOCK // part, some, 0)
 
 
 def adam(source, weights, first, second):
@@ -1138,9 +1375,9 @@
         adam_kernel,
         name="adamw",
         grid=(FLAT // BLOCK,),
-        out_shape=(vector, vector, vector, jax.ShapeDtypeStruct((8, 128), F32)),
+        out_shape=(vector, vector, vector),
         in_specs=[VMEM, block, block, block],
-        out_specs=(block, block, block, pl.BlockSpec((8, 128), lambda i: (0, 0))),
+        out_specs=(block, block, block),
         scratch_shapes=[pltpu.VMEM((LEAD + FLAT + 288, 128), F32)],
         compiler_params=pltpu.CompilerParams(vmem_limit_bytes=60 * 2**20),
     )(source, weights, first, second)
@@ -1168,27 +1405,15 @@
     coord_row = coord_col.T
     flat = [v.reshape(FLAT, 128) for v in (params, first_moment, second_moment)]
     wall, xdoc, cdoc, total = gather_weights(stages, flat[0], inputs, masked, count)
-    out_doc, *saved = forward_pass(wall, xdoc, features, coord_row, coord_col)
-    grad_doc, grads = backward_pass(wall, cdoc, total, saved, features, coord_row, coord_col)
-    reduced, grad_other = reduce_grads(stages, grads, grad_doc)
+    out_doc, *saved, wall = forward_pass(wall, xdoc, features, coord_row, coord_col)
+    input_grad, reduced, norm = backward_pass(stages, wall, cdoc, total, saved, features, coord_row, coord_col)
     out_other = lax.ppermute(
         lax.dynamic_slice_in_dim(out_doc, (1 - fs) * half, half, 0), "fsdp", [(0, 1), (1, 0)]
     )
-
-    def owned(doc, moved):
-        mine = lax.dynamic_slice_in_dim(doc, fs * half, half, 0)
-        return jnp.where(fs == 0, jnp.stack([mine, moved]), jnp.stack([moved, mine]))
-
-    grad, update, new_first, square = adam(reduced, *flat)
-    norm = jnp.sqrt(lax.psum(jnp.sum(square), "fsdp"))
-    return (
-        owned(out_doc, out_other),
-        owned(grad_doc, grad_other),
-        grad.reshape(-1),
-        norm,
-        update.reshape(-1),
-        new_first.reshape(-1),
-    )
+    out_mine = lax.dynamic_slice_in_dim(out_doc, fs * half, half, 0)
+    layer_out = jnp.where(fs == 0, jnp.stack([out_mine, out_other]), jnp.stack([out_other, out_mine]))
+    grad, update, new_first = adam(reduced, *flat)
+    return (layer_out, input_grad, grad.reshape(-1), norm[0, 0], update.reshape(-1), new_first.reshape(-1))
 
 
 def solution(mesh):

time: 476 us -> 356 us (0.75)
  Pallas kernels: 448 us -> 339 us
  blocking collectives: 5.55 us -> 0 us
    pallas_call x2 -> x1, Pallas kernels: 239 us -> 131 us  [backward_pass(): pl.pallas_call(functools.partial(backward_kernel, stages), name='backward...]
    psum x1 -> x0, blocking collectives: 5.55 us -> none  [local(): norm = jnp.sqrt(lax.psum(jnp.sum(square), 'fsdp'))]
  transfers between devices with their start and end apart: 1 -> 1, of which waited for: 0 -> 0; matrix products, arithmetic and copies ran while one was open for 0% -> 0% of each run, Pallas kernels for 60% -> 49%
where the time goes in v2:
time: 356 us; the launch traced here: 355 us
  Pallas kernels  339 us (95%)
  local copies, waits for them, and re-layouts  7.69 us (2%)
  other arithmetic  7.47 us (2%)
    pallas_call x1, Pallas kernels, backward_pass(): pl.pallas_call(functools.partial(backward_kernel, stages), name='backward...  131 us
    pallas_call x1, Pallas kernels, forward_pass(): pl.pallas_call(forward_kernel, name='forward', out_shape=(sds((LEN, D), B...  82.9 us
    pallas_call x1, Pallas kernels, gather_weights(): pl.pallas_call(functools.partial(gather_kernel, stages), name='gather_wei...  81.6 us
    pallas_call x1, Pallas kernels, adam(): pl.pallas_call(adam_kernel, name='adamw', grid=(FLAT // BLOCK,), out_shap...  43.6 us
  transfers between devices with their start and end apart: 1, of which 0 were waited for; matrix products, arithmetic and copies ran while one was open for 0% of the time, Pallas kernels for 49%

profile of v2, /device:TPU:0, one launch (start us, length us, event | category | flops | bytes accessed | tf_op | source)
XLA Modules:
  0.0 355.0 jit_solution(13936577509590507990)
XLA Ops:
  0.6 0.7 convert_element_type.12
  1.3 1.3 convert_reduce_fusion
  2.6 0.7 dynamic-slice_bitcast_fusion.1
  3.3 0.6 pad_add_fusion
  4.0 0.9 copy.27.coord_col
  4.8 0.6 sine_convert_fusion
  5.4 0.8 copy.26.features
  6.2 2.1 broadcast_multiply_fusion.cot
  8.3 1.2 broadcast_in_dim.2.cnt
  9.6 81.6 %gather_weights.1 = (bf16[2,28672,128]{2,1,0:T(8,128)(2,1)}, bf16[512,768]{1,0:T(8,128)(2,1)}, bf16[512,768]{1,0:T(8,128)(2,1)}, f32[8,128]{1,0:T(8,128)}) custom-call(f32[28160,128]{1,0:T(8,128)} %bitcast.15, bf16[2,256,768]{2,1,0:T(8,128)(2,1)} %xin.1, bf16[2,256,768]{2,1,0:T(8,128)(2,1)} %broadcast_multiply_fusion.cot, f32[8,128]{1,0:T(8,128)} %broadcast_in_dim.2.cnt), custom_call_target="tpu_custom_call" | custom-call | tf_op jit(solution)/shard_map/gather_weights/pallas_call | solution.py:361
  91.2 82.9 %forward.1 = (bf16[512,768]{1,0:T(8,128)(2,1)}, bf16[512,768]{1,0:T(8,128)(2,1)}, bf16[18,512,128]{2,1,0:T(8,128)(2,1)}, bf16[24576,128]{1,0:T(8,128)(2,1)}, bf1...) custom-call(bf16[2,28672,128]{2,1,0:T(8,128)(2,1)} %get-tuple-elemen, ...), custom_call_target="tpu_custom_call" | custom-call | tf_op jit(solution)/shard_map/forward/pallas_call | solution.py:631
  174.1 2.1 dynamic-slice_bitcast_fusion
  176.1 0.2 collective-permute-start
  176.4 130.8 %backward_reduce.1 = (bf16[2,256,768]{2,1,0:T(8,128)(2,1)}, bf16[28672,128]{1,0:T(8,128)(2,1)}, f32[8,128]{1,0:T(8,128)}) custom-call(bf16[2,28672,128]{2,1,0:T(8,128)(2,1)} %get-tuple-element.33.wall_hbm, bf16[512,768]{1,0:T(8,128)(2,1)} %get-tuple-element.34.cdoc_hbm, f32[8,128]{1,0:T(8,128)} %get-tuple-element.35.total, ...), custom_call_target="tpu_custom_call" | custom-call | tf_op jit(solution)/shard_map/backward_reduce/pallas_call | solution.py:1268
  307.2 1.2 slice.19
  308.4 0.0 copy-start
  308.4 0.0 copy-start.1
  308.4 43.6 %adamw.1 = (f32[28160,128]{1,0:T(8,128)}, f32[28160,128]{1,0:T(8,128)}, f32[28160,128]{1,0:T(8,128)}) custom-call(bf16[28672,128]{1,0:T(8,128)(2,1)} %get-tuple-element.49.source, f32[28160,128]{1,0:T(8,128)} %bitcast.16, f32[28160,128]{1,0:T(8,128)} %bitcast.17, f32[28160,128]{1,0:T(8,128)} %bitcast.18), custom_call_target="tpu_custom_call" | custom-call | tf_op jit(solution)/shard_map/adamw/pallas_call | solution.py:1374
  352.0 0.0 collective-permute-done
  352.0 0.0 copy-done
  352.0 2.1 maximum_select_fusion
  354.1 0.0 copy-done.1
  354.1 0.9 copy.31
  (4 shorter events, 0.0 us)
Async XLA Ops:
  176.1 175.8 %collective-permute-start = (bf16[256,768]{1,0:T(8,128)(2,1)}, bf16[256,768]{1,0:T(8,128)(2,1)}, u32[]{:S(2)}, u32[]{:S(2)}) collective-permute-start(bf16[256,768]{1,0:T(8,128)(2,1)} %get-tuple-element.55), channel_id=1, source_target_pairs={{0,1},{1,0},{2,3},{3,2},{4,5},{5,4},{6,7},{7,6},{8,9},{9,8},{10,11... | collective-permute-start | bytes 1179656 | tf_op jit(solution)/shard_map/ppermute | solution.py:1410
  308.4 43.6 %copy-start = (bf16[1,256,768]{2,1,0:T(8,128)(2,1)S(1)}, bf16[1,256,768]{2,1,0:T(8,128)(2,1)}, u32[]{:S(2)}) copy-start(bf16[1,256,768]{2,1,0:T(8,128)(2,1)} %get-tuple-element.54) | copy-start | bytes 1179652
  308.4 45.7 %copy-start.1 = (bf16[2,256,768]{2,1,0:T(8,128)(2,1)S(1)}, bf16[2,256,768]{2,1,0:T(8,128)(2,1)}, u32[]{:S(2)}) copy-start(bf16[2,256,768]{2,1,0:T(8,128)(2,1)} %get-tuple-element.69) | copy-start | bytes 2359300

commit v3 on v2

--- a/solution.py
+++ b/solution.py
@@ -20,7 +20,10 @@
 SHARD = PADDED // 2
 FLAT = SHARD // 128
 PAIRS = HEADS // 2
-QROWS = 128
+QROWS = 256
+AROWS = 512
+BROWS = 256
+SKEW = 2
 
 norm_eps = 1e-05
 adam_one = 0.9
@@ -134,66 +137,265 @@
     return jnp.concatenate([ref_rows[start + i : start + i + 1, :] for i in range(count)], axis=1)
 
 
-def relayout_tasks(plane, flat, out):
-    tasks = []
-
-    def block(dst, src, count, stride):
-        def run():
-            out[plane, pl.ds(dst, count), :] = flat[pl.ds(LEAD + src, count, stride=stride), :].astype(BF16)
-
-        tasks.append((dst + count, run))
+def table_constants():
+    width = BUCKETS * HEADS
+    lane = np.arange(width)
+    pick = np.zeros((3, width, 128), np.float32)
+    for table in range(3):
+        pick[table, lane, 32 * table + lane // HEADS] = 1.0
+    keep = (lane[None, :] % HEADS == np.arange(16)[:, None]).astype(np.float32)
+    return pick.astype(jnp.bfloat16), keep
+
+
+def bucket_of(offset):
+    spread = jnp.abs(offset)
+    result = jnp.minimum(spread, 8) + jnp.where(offset > 0, 16, 0)
+    for level in range(9, 16):
+        result = result + jnp.where(spread >= 8 * 2 ** (level - 8), 1, 0)
+    return result
+
+
+def up_block(wall, j):
+    columns = []
+    for c in (2 * j, 2 * j + 1):
+        first = wall[0, rows_at(UP0 + c * UP_A, UP_A), :]
+        second = wall[1, rows_at(UP1 + c * UP_B + 16, UP_B - 16), :]
+        columns.append(jnp.concatenate([first, second], axis=0))
+    return jnp.concatenate(columns, axis=1)
+
+
+def down_rows(wall, j):
+    return jnp.concatenate(
+        [wall[1, rows_at(DOWN1 + j * 1536 + c * 256, 256), :] for c in range(6)], axis=1
+    )
+
+
+def merge_up(wall):
+    row = lax.broadcasted_iota(jnp.int32, (16, 128), 0)
+
+    def one(c, carry):
+        low_at = rows_at(UP0 + c * UP_A + UP_A - 16, 16)
+        low = wall[0, low_at, :].astype(F32)
+        high = wall[1, rows_at(UP1 + c * UP_B, 16), :].astype(F32)
+        cut = jnp.where(c < 2, CUT + 1 - 400, CUT - 400)
+        wall[0, low_at, :] = jnp.where(row < cut, low, high).astype(BF16)
+        return carry
+
+    lax.fori_loop(0, 24, one, 0)
+
+
+def stats(values):
+    mean = jnp.mean(values, axis=1, keepdims=True)
+    centered = values - mean
+    inverse = lax.rsqrt(jnp.mean(centered * centered, axis=1, keepdims=True) + norm_eps)
+    return centered * inverse, inverse
+
+
+def find_places(coord_col, lut, places, tick):
+    lane = lax.broadcasted_iota(jnp.int32, (8, 128), 1)
+    step = lane % 16
+    level = jnp.where(step <= 8, step, lax.shift_left(jnp.full_like(step, 8), jnp.maximum(step - 8, 0)))
+    edge = jnp.where(lane < 16, 1 - level, jnp.where(lane == 16, 1 << 12, level))
+
+    def line_rows(a, carry):
+        at = pl.ds(pl.multiple_of(a * 8, 8), 8)
+        value = coord_col[at, 0:1] + edge
+        places[0, at, :] = jnp.where(value <= 0, LEN, jnp.minimum(value, LEN) - 1)
+        return carry
+
+    lax.fori_loop(0, LEN // 8, line_rows, 0, unroll=4)
+    for table in (1, 2):
+        def look(a, best):
+            at = pl.ds(pl.multiple_of(a * 8, 8), 8)
+            near = jnp.broadcast_to(coord_col[at, table : table + 1], (8, 128))
+            code = near * LEN + (lax.broadcasted_iota(jnp.int32, (8, 128), 0) + a * 8)
+            return tuple(
+                jnp.maximum(best[g], jnp.where(near < lane + 128 * g, code, -1)) for g in range(16)
+            )
+
+        best = lax.fori_loop(
+            0, LEN // 8, look, tuple(jnp.full((8, 128), -1, jnp.int32) for _ in range(16)), unroll=2
+        )
+        tick()
+        for g in range(16):
+            most = jnp.max(best[g], axis=0, keepdims=True)
+            lut[g : g + 1, :] = jnp.where(most < 0, LEN, most & (LEN - 1))
+        luts = [jnp.broadcast_to(lut[g : g + 1, :], (8, 128)) for g in range(16)]
+
+        def find(a, carry):
+            at = pl.ds(pl.multiple_of(a * 8, 8), 8)
+            value = jnp.clip(coord_col[at, table : table + 1] + edge, 0, 2047)
+            low, high = value & 127, value >> 7
+            found = jnp.full((8, 128), LEN, jnp.int32)
+            for g in range(16):
+                found = jnp.where(high == g, jnp.take_along_axis(luts[g], low, axis=1), found)
+            places[table, at, :] = found
+            return carry
+
+        for part in range(2):
+            lax.fori_loop(part * 32, part * 32 + 32, find, 0, unroll=4)
+            tick()
+
+
+def relayout(plane, flat, out, group):
+    def blocks(count, dst, src, rows, stride):
+        def one(i, carry):
+            out[plane, rows_at(dst(i), rows), :] = flat[pl.ds(LEAD + src(i), rows, stride=stride), :].astype(BF16)
+            return carry
+
+        lax.fori_loop(0, count, one, 0)
 
     def window(dst, src, count):
-        def run():
-            out[plane, pl.ds(dst, count), :] = flat[pl.ds(LEAD + src, count), :].astype(BF16)
-
-        tasks.append((dst + count, run))
+        out[plane, pl.ds(dst, count), :] = flat[pl.ds(LEAD + src, count), :].astype(BF16)
 
     def clear(low, high):
-        def run():
-            out[plane, pl.ds(low, high - low), :] = jnp.zeros((high - low, 128), BF16)
-
-        tasks.append((high, run))
-
-    if plane == 0:
-        for pos in range(18):
-            block(pos * D, (pos % 3) * 6 + pos // 3, D, 18)
-        for c in range(6):
-            block(OUT0 + c * D, F_OUT + c, D, 6)
-        for c in range(24):
-            block(UP0 + c * UP_A, F_UP + c, UP_A, 24)
+        out[plane, pl.ds(low, high - low), :] = jnp.zeros((high - low, 128), BF16)
+
+    if plane == 0 and group == 0:
+        blocks(24, lambda c: UP0 + c * UP_A, lambda c: F_UP + c, UP_A, 24)
         window(SM0, 13824, 16)
         window(SM0 + 16, 18440, 32)
-        used = SM0 + 48
-    else:
-        for c in range(24):
-            block(UP1 + c * UP_B, c - 98, UP_B, 24)
-        for j in range(12):
-            for c in range(6):
-                block(DOWN1 + j * 1536 + c * 256, F_DOWN1 + j * 1536 + c, 256, 6)
+        clear(SM0 + 48, ROWS)
+    elif plane == 0 and group == 1:
+        blocks(18, lambda pos: pos * D, lambda pos: lax.rem(pos, 3) * 6 + pos // 3, D, 18)
+    elif plane == 0:
+        blocks(6, lambda c: OUT0 + c * D, lambda c: F_OUT + c, D, 6)
+    elif group == 0:
+        for c in range(6):
+            blocks(12, lambda j: DOWN1 + j * 1536 + c * 256, lambda j: F_DOWN1 + j * 1536 + c, 256, 6)
         clear(DOWN_END, LAY1)
-        for c in range(6):
-            block(LAY1 + c * FEAT, F_LAY1 + c, FEAT, 6)
+        blocks(6, lambda c: LAY1 + c * FEAT, lambda c: F_LAY1 + c, FEAT, 6)
         window(SM1, 8728, 32)
         window(SM1 + 32, 27184, 32)
         window(SM1 + 64, 27976, 16)
-        used = SM1 + 80
-
-    clear(used, ROWS)
-    return tasks
-
-
-def direct_type(position):
-    return position % 4 == 1
-
-
-def gather_kernel(
-    stages, p_hbm, xin, cot, cnt, wall, xdoc, cdoc, total,
-    flat, zall, xs, cs, cnt_slots, in_sem, x_send, x_recv, c_send, c_recv, act_send, act_recv,
-    n_send, n_recv, out_sem, *stage_sems,
+        clear(SM1 + 80, ROWS)
+    elif group == 1:
+        blocks(24, lambda c: UP1 + c * UP_B, lambda c: c - 98, UP_B, 24)
+
+
+class Gather:
+    def __init__(self, stages, zall, x_send, x_recv, c_send, c_recv, sems):
+        self.stages, self.zall, self.sems = stages, zall, sems
+        self.x_send, self.x_recv, self.c_send, self.c_recv = x_send, x_recv, c_send, c_recv
+        self.dp, self.fs = place()
+        self.other = 1 - self.fs
+        self.levels = len(stages)
+        self.parts = offsets(self.dp, stages, CHUNK)
+        self.x_peer = (self.dp, self.other)
+        self.core_peer = (self.dp + 1 - 2 * (self.dp % 2), self.fs)
+
+    def base(self, position):
+        return lax.rem(CHUNKS - 1 + position, CHUNKS) * CHUNK
+
+    def direct(self, position):
+        return (position == 4) | (position == 9) | (position == 12)
+
+    def x_copy(self, position, plane, direct):
+        start, size = self.parts[0] if direct else self.parts[-1]
+        where = self.zall.at[plane, rows_at(self.base(position) + start, size)]
+        return remote(where, where, self.x_send.at[position], self.x_recv.at[position], self.x_peer)
+
+    def send(self, low, high):
+        def one(position, carry):
+            direct = self.direct(position)
+
+            @pl.when(direct)
+            def _():
+                self.x_copy(position, self.fs, True).start()
+
+            @pl.when(jnp.logical_not(direct))
+            def _():
+                self.x_copy(position, self.fs, False).start()
+
+            return carry
+
+        lax.fori_loop(low, high, one, 0)
+
+    def stage_copies(self, level, position, receive):
+        radix, stride = self.stages[level]
+        start, size = self.parts[level + 1]
+        mine = (self.dp // stride) % radix
+        copies = []
+        for step in range(1, radix):
+            peer = (member(self.dp, radix, stride, (mine + step) % radix), self.fs)
+            shift = ((mine - step + radix) % radix - mine) * size if receive else 0
+            where = self.zall.at[self.other, rows_at(self.base(position) + start + shift, size)]
+            copies.append(
+                remote(
+                    where, where, self.sems[2 * level].at[position, step - 1],
+                    self.sems[2 * level + 1].at[position, step - 1], peer,
+                )
+            )
+        return copies
+
+    def core_copy(self, position, receive):
+        size = CHUNK // 2
+        start = (1 - self.dp % 2 if receive else self.dp % 2) * size
+        where = self.zall.at[self.other, rows_at(self.base(position) + start, size)]
+        return remote(where, where, self.c_send.at[position], self.c_recv.at[position], self.core_peer)
+
+    def work(self, position, step):
+        direct = self.direct(position)
+        levels = self.levels
+        if step == levels + 1:
+            self.core_copy(position, True).wait_recv()
+            self.core_copy(position, False).wait_send()
+
+            @pl.when(direct)
+            def _():
+                self.x_copy(position, self.fs, True).wait_send()
+
+            @pl.when(jnp.logical_not(direct))
+            def _():
+                self.x_copy(position, self.fs, False).wait_send()
+                for level in range(levels):
+                    for copy in self.stage_copies(level, position, False):
+                        copy.wait_send()
+
+            return
+        if step == 0:
+
+            @pl.when(direct)
+            def _():
+                self.x_copy(position, self.other, True).wait_recv()
+                self.core_copy(position, False).start()
+
+        @pl.when(jnp.logical_not(direct))
+        def _():
+            if step == 0:
+                self.x_copy(position, self.other, False).wait_recv()
+            else:
+                for copy in self.stage_copies(levels - step, position, True):
+                    copy.wait_recv()
+            if step < levels:
+                for copy in self.stage_copies(levels - 1 - step, position, False):
+                    copy.start()
+            else:
+                self.core_copy(position, False).start()
+
+    def tick(self, number):
+        for step in range(self.levels + 1, -1, -1):
+            position = number - SKEW * step
+
+            @pl.when((position >= 0) & (position < CHUNKS))
+            def _(position=position, step=step):
+                self.work(position, step)
+
+    def ticks(self):
+        return CHUNKS + SKEW * (self.levels + 1)
+
+
+def forward_kernel(
+    stages, p_hbm, xin, cot, cnt, features, coord_row, coord_col, pick, keep,
+    wall_out, cdoc_out, total, rounded_out, qkv_out, probs_out, mixed_out, one_out, inverse_one, low_out, hidden_out,
+    slope_out, two_out, inverse_two, places_out, layer_out,
+    flat, wall, xs, cs, cnt_slots, start, up_bias, acc, indices, lut, rounded, qkv, probs, mixed, normed, low, hidden,
+    slope, places, layer,
+    in_sem, x_send, x_recv, c_send, c_recv, act_send, act_recv, n_send, n_recv, out_sem, probs_sem, feed_sem, *stage_sems,
 ):
-    dp, fs = place()
-    other = 1 - fs
+    net = Gather(stages, wall, x_send, x_recv, c_send, c_recv, stage_sems)
+    dp, fs, other = net.dp, net.fs, net.other
+    half = LEN // 2
     pieces = 8
     span = FLAT // pieces
     loads = [
@@ -207,77 +409,18 @@
     flat[pl.ds(0, LEAD), :] = jnp.zeros((LEAD, 128), F32)
     flat[pl.ds(LEAD + FLAT, 288), :] = jnp.zeros((288, 128), F32)
     greet(stages)
-    x_peer = (dp, other)
-    core_peer = (dp + 1 - 2 * (dp % 2), fs)
-    half = LEN // 2
-
-    def act_copies(send):
-        where = rows_at((fs if send else other) * half, half)
-        return [
-            remote(xin.at[other], xs.at[where], act_send.at[0], act_recv.at[0], x_peer),
-            remote(cot.at[other], cs.at[where], act_send.at[1], act_recv.at[1], x_peer),
-        ]
-
-    for copy in act_copies(True):
-        copy.start()
-    for load in loads:
-        load.wait()
-
-    order = [(CHUNKS - 1 + i) % CHUNKS for i in range(CHUNKS)]
-    parts = offsets(dp, stages, CHUNK)
-
-    def x_copy(position, plane):
-        start, size = parts[0] if direct_type(position) else parts[-1]
-        where = zall.at[plane, rows_at(order[position] * CHUNK + start, size)]
-        return remote(where, where, x_send.at[position], x_recv.at[position], x_peer)
-
-    def stage_copies(level, position, receive):
-        radix, stride = stages[level]
-        start, size = parts[level + 1]
-        mine = (dp // stride) % radix
-        send_sem, recv_sem = stage_sems[2 * level], stage_sems[2 * level + 1]
-        copies = []
-        for step in range(1, radix):
-            peer = (member(dp, radix, stride, (mine + step) % radix), fs)
-            shift = ((mine - step + radix) % radix - mine) * size if receive else 0
-            where = zall.at[other, rows_at(order[position] * CHUNK + start + shift, size)]
-            copies.append(
-                remote(where, where, send_sem.at[position, step - 1], recv_sem.at[position, step - 1], peer)
-            )
-        return copies
-
-    def core_copy(position, receive):
-        size = CHUNK // 2
-        start = (1 - dp % 2 if receive else dp % 2) * size
-        where = zall.at[other, rows_at(order[position] * CHUNK + start, size)]
-        return remote(where, where, c_send.at[position], c_recv.at[position], core_peer)
-
-    levels = len(stages)
-
-    def advance(position, stage):
-        if direct_type(position):
-            if stage == 0:
-                x_copy(position, other).wait_recv()
-                core_copy(position, False).start()
-            return
-        if stage == 0:
-            x_copy(position, other).wait_recv()
-        else:
-            for copy in stage_copies(levels - stage, position, True):
-                copy.wait_recv()
-        if stage < levels:
-            for copy in stage_copies(levels - 1 - stage, position, False):
-                copy.start()
-        else:
-            core_copy(position, False).start()
-
-    rounds = [[core_peer], [x_peer]] + [
+
+    def act_copy(number, source, target, receive):
+        where = rows_at((other if receive else fs) * half, half)
+        return remote(source.at[other], target.at[where], act_send.at[number], act_recv.at[number], net.x_peer)
+
+    rounds = [
         [
             (member(dp, radix, stride, ((dp // stride) % radix + step) % radix), fs)
             for step in range(1, radix)
         ]
         for radix, stride in stages
-    ]
+    ] + [[net.core_peer], [net.x_peer]]
 
     def count_copies(number):
         base = sum(len(r) for r in rounds[:number])
@@ -287,12 +430,11 @@
         ]
 
     def count_round(number):
-        if number > 0:
-            for copy in count_copies(number - 1):
+        if 0 < number <= len(rounds):
+            gathered = total[...]
+            base = sum(len(r) for r in rounds[: number - 1])
+            for i, copy in enumerate(count_copies(number - 1)):
                 copy.wait()
-            base = sum(len(r) for r in rounds[: number - 1])
-            gathered = total[...]
-            for i in range(len(rounds[number - 1])):
                 gathered = gathered + cnt_slots[base + i]
             total[...] = gathered
         if number < len(rounds):
@@ -301,223 +443,20 @@
 
     total[...] = cnt[...]
     count_round(0)
-
-    tasks = [relayout_tasks(0, flat, zall), relayout_tasks(1, flat, zall)]
-    done = [set(), set()]
-    for position in range(CHUNKS + levels + 1):
-        if position < CHUNKS:
-            low, high = order[position] * CHUNK, (order[position] + 1) * CHUNK
-            for plane in range(2):
-                run, start = [], 0
-                for number, (end, task) in enumerate(tasks[plane]):
-                    if start < high and end > low and number not in done[plane]:
-                        done[plane].add(number)
-                        run.append(task)
-                    start = end
-
-                @pl.when(fs == plane)
-                def _(run=run):
-                    for task in run:
-                        task()
-
-            x_copy(position, fs).start()
-        for stage in range(levels + 1):
-            if 0 <= position - 1 - stage < CHUNKS:
-                advance(position - 1 - stage, stage)
-        if 2 <= position and (position - 2) % 2 == 0 and (position - 2) // 2 + 1 <= len(rounds):
-            count_round((position - 2) // 2 + 1)
-    xdoc[pl.ds(fs * half, half), :] = xin[fs]
-    cdoc[pl.ds(fs * half, half), :] = cot[fs]
-    outs = [
-        pltpu.make_async_copy(zall.at[fs], wall.at[fs], out_sem.at[0]),
-    ]
-    outs[0].start()
-    for copy in act_copies(False):
-        copy.wait_recv()
-    xdoc[pl.ds(other * half, half), :] = xs[pl.ds(other * half, half), :]
-    cdoc[pl.ds(other * half, half), :] = cs[pl.ds(other * half, half), :]
-    for copy in act_copies(True):
-        copy.wait_send()
-    for position in range(CHUNKS):
-        core_copy(position, True).wait_recv()
-        core_copy(position, False).wait_send()
-        x_copy(position, fs).wait_send()
-        if not direct_type(position):
-            for level in range(levels):
-                for copy in stage_copies(level, position, False):
-                    copy.wait_send()
-    outs.append(pltpu.make_async_copy(zall.at[other], wall.at[other], out_sem.at[1]))
-    outs[1].start()
-    for copy in outs:
-        copy.wait()
-
-
-def gather_weights(stages, p2, xin, cot, cnt):
-    count_peers = 2 + sum(radix - 1 for radix, _ in stages)
-    sems = []
-    for radix, _ in stages:
-        sems += [pltpu.SemaphoreType.DMA((CHUNKS, radix - 1))] * 2
-    half = LEN // 2
-    return pl.pallas_call(
-        functools.partial(gather_kernel, stages),
-        name="gather_weights",
-        out_shape=(
-            jax.ShapeDtypeStruct((2, ROWS, 128), BF16),
-            jax.ShapeDtypeStruct((LEN, D), BF16),
-            jax.ShapeDtypeStruct((LEN, D), BF16),
-            jax.ShapeDtypeStruct((8, 128), F32),
-        ),
-        in_specs=[ANY, VMEM, VMEM, VMEM],
-        out_specs=(ANY, VMEM, VMEM, VMEM),
-        scratch_shapes=[
-            pltpu.VMEM((LEAD + FLAT + 288, 128), F32),
-            pltpu.VMEM((2, ROWS, 128), BF16),
-            pltpu.VMEM((LEN, D), BF16),
-            pltpu.VMEM((LEN, D), BF16),
-            pltpu.VMEM((count_peers, 8, 128), F32),
-            pltpu.SemaphoreType.DMA((8,)),
-            pltpu.SemaphoreType.DMA((CHUNKS,)),
-            pltpu.SemaphoreType.DMA((CHUNKS,)),
-            pltpu.SemaphoreType.DMA((CHUNKS,)),
-            pltpu.SemaphoreType.DMA((CHUNKS,)),
-            pltpu.SemaphoreType.DMA((2,)),
-            pltpu.SemaphoreType.DMA((2,)),
-            pltpu.SemaphoreType.DMA((count_peers,)),
-            pltpu.SemaphoreType.DMA((count_peers,)),
-            pltpu.SemaphoreType.DMA((2,)),
-        ]
-        + sems,
-        compiler_params=pltpu.CompilerParams(
-            collective_id=1, has_side_effects=True, vmem_limit_bytes=60 * 2**20
-        ),
-    )(p2, xin, cot, cnt)
-
-
-def table_constants():
-    width = BUCKETS * HEADS
-    lane = np.arange(width)
-    pick = np.zeros((3, width, 128), np.float32)
-    for table in range(3):
-        pick[table, lane, 32 * table + lane // HEADS] = 1.0
-    keep = (lane[None, :] % HEADS == np.arange(16)[:, None]).astype(np.float32)
-    return pick.astype(jnp.bfloat16), keep
-
-
-def bucket_of(offset):
-    spread = jnp.abs(offset)
-    result = jnp.minimum(spread, 8) + jnp.where(offset > 0, 16, 0)
-    for level in range(9, 16):
-        result = result + jnp.where(spread >= 8 * 2 ** (level - 8), 1, 0)
-    return result
-
-
-def up_block(wall, j):
-    columns = []
-    for c in (2 * j, 2 * j + 1):
-        first = wall[0, rows_at(UP0 + c * UP_A, UP_A), :]
-        second = wall[1, rows_at(UP1 + c * UP_B + 16, UP_B - 16), :]
-        columns.append(jnp.concatenate([first, second], axis=0))
-    return jnp.concatenate(columns, axis=1)
-
-
-def down_rows(wall, j):
-    return jnp.concatenate(
-        [wall[1, rows_at(DOWN1 + j * 1536 + c * 256, 256), :] for c in range(6)], axis=1
-    )
-
-
-def merge_up(wall):
-    row = lax.broadcasted_iota(jnp.int32, (16, 128), 0)
-
-    def one(c, carry):
-        low_at = rows_at(UP0 + c * UP_A + UP_A - 16, 16)
-        low = wall[0, low_at, :].astype(F32)
-        high = wall[1, rows_at(UP1 + c * UP_B, 16), :].astype(F32)
-        cut = jnp.where(c < 2, CUT + 1 - 400, CUT - 400)
-        wall[0, low_at, :] = jnp.where(row < cut, low, high).astype(BF16)
-        return carry
-
-    lax.fori_loop(0, 24, one, 0)
-
-
-def stats(values):
-    mean = jnp.mean(values, axis=1, keepdims=True)
-    centered = values - mean
-    inverse = lax.rsqrt(jnp.mean(centered * centered, axis=1, keepdims=True) + norm_eps)
-    return centered * inverse, inverse
-
-
-def find_places(coord_col, lut, places):
-    lane = lax.broadcasted_iota(jnp.int32, (8, 128), 1)
-    step = lane % 16
-    level = jnp.where(step <= 8, step, lax.shift_left(jnp.full_like(step, 8), jnp.maximum(step - 8, 0)))
-    edge = jnp.where(lane < 16, 1 - level, jnp.where(lane == 16, 1 << 12, level))
-
-    def line_rows(a, carry):
-        at = pl.ds(pl.multiple_of(a * 8, 8), 8)
-        value = coord_col[at, 0:1] + edge
-        places[0, at, :] = jnp.where(value <= 0, LEN, jnp.minimum(value, LEN) - 1)
-        return carry
-
-    lax.fori_loop(0, LEN // 8, line_rows, 0, unroll=4)
-    for table in (1, 2):
-        def look(a, best):
-            at = pl.ds(pl.multiple_of(a * 8, 8), 8)
-            near = jnp.broadcast_to(coord_col[at, table : table + 1], (8, 128))
-            code = near * LEN + (lax.broadcasted_iota(jnp.int32, (8, 128), 0) + a * 8)
-            return tuple(
-                jnp.maximum(best[g], jnp.where(near < lane + 128 * g, code, -1)) for g in range(16)
-            )
-
-        best = lax.fori_loop(
-            0, LEN // 8, look, tuple(jnp.full((8, 128), -1, jnp.int32) for _ in range(16)), unroll=2
-        )
-        for g in range(16):
-            most = jnp.max(best[g], axis=0, keepdims=True)
-            lut[g : g + 1, :] = jnp.where(most < 0, LEN, most & (LEN - 1))
-        luts = [jnp.broadcast_to(lut[g : g + 1, :], (8, 128)) for g in range(16)]
-
-        def find(a, carry):
-            at = pl.ds(pl.multiple_of(a * 8, 8), 8)
-            value = jnp.clip(coord_col[at, table : table + 1] + edge, 0, 2047)
-            low, high = value & 127, value >> 7
-            found = jnp.full((8, 128), LEN, jnp.int32)
-            for g in range(16):
-                found = jnp.where(high == g, jnp.take_along_axis(luts[g], low, axis=1), found)
-            places[table, at, :] = found
-            return carry
-
-        lax.fori_loop(0, LEN // 8, find, 0, unroll=4)
-
-
-def forward_kernel(
-    wall_hbm, xdoc, features, coord_row, coord_col, pick, keep,
-    layer_out, rounded, qkv, probs, mixed, normed_one, inverse_one, first_low, hidden, slope,
-    normed_two, inverse_two, places, wall_out,
-    wall, start, up_bias, acc, bias, indices, lut, sem,
-):
-    load = pltpu.make_async_copy(wall_hbm, wall, sem.at[0])
-    load.start()
-    load.wait()
-    merge_up(wall)
-    store = pltpu.make_async_copy(wall, wall_out, sem.at[0])
-    store.start()
-    small0 = wall[0, pl.ds(SM0, 48), :].astype(F32)
-    small1 = wall[1, pl.ds(SM1, 80), :].astype(F32)
-    qv_bias = row_of(small0, 0, 12)
-    out_bias, gain_one, shift_one = (row_of(small0, 20 + 6 * i, 6) for i in range(3))
-    down_bias, gain_two, shift_two = (row_of(small1, 38 + 6 * i, 6) for i in range(3))
-
-    w_layout = jnp.concatenate([wall[1, pl.ds(LAY1 + c * FEAT, FEAT), :] for c in range(6)], axis=1)
-    start[...] = xdoc[...].astype(F32) + nn(features[...], w_layout)
-    rounded[...] = start[...].astype(BF16)
-
-    heads_by_lane = jnp.zeros((16, 128), F32)
-    for table in range(3):
-        flat_row = row_of(small1, 64 + 3 * table, 3)
-        spread = (jnp.broadcast_to(flat_row, (16, 384)) * keep[...]).astype(BF16)
-        heads_by_lane = heads_by_lane + nn(spread, pick[table])
-    rows_by_head = [jnp.broadcast_to(heads_by_lane[h : h + 1, :], (8, 128)) for h in range(HEADS)]
+    for load in loads:
+        load.wait()
+    for group, (low_at, high_at) in enumerate(((0, 1), (1, 7), (7, CHUNKS))):
+        for plane in range(2):
+
+            @pl.when(fs == plane)
+            def _(plane=plane, group=group):
+                relayout(plane, flat, wall, group)
+
+        net.send(low_at, high_at)
+        if group == 1:
+            act_copy(0, xin, xs, False).start()
+    xs[pl.ds(fs * half, half), :] = xin[fs]
+    cs[pl.ds(fs * half, half), :] = cot[fs]
 
     def index_rows(a, carry):
         at = pl.ds(pl.multiple_of(a * 8, 8), 8)
@@ -531,108 +470,213 @@
         return carry
 
     lax.fori_loop(0, LEN // 8, index_rows, 0, unroll=4)
+    passed = [0]
+
+    def tick():
+        net.tick(passed[0])
+        if passed[0] % 2 == 0:
+            count_round(passed[0] // 2 + 1)
+        passed[0] += 1
+
+    find_places(coord_col, lut, places, tick)
+    outs = []
+
+    def put(source, target):
+        copy = pltpu.make_async_copy(source, target, out_sem.at[len(outs)])
+        copy.start()
+        outs.append(copy)
+
+    put(places, places_out)
+    while passed[0] < 1 + SKEW * (net.levels + 1):
+        tick()
+
+    small1 = wall[1, pl.ds(SM1, 80), :].astype(F32)
+    heads_by_lane = jnp.zeros((16, 128), F32)
+    for table in range(3):
+        flat_row = row_of(small1, 64 + 3 * table, 3)
+        spread = (jnp.broadcast_to(flat_row, (16, 384)) * keep[...]).astype(BF16)
+        heads_by_lane = heads_by_lane + nn(spread, pick[table])
+    rows_by_head = [jnp.broadcast_to(heads_by_lane[h : h + 1, :], (8, 128)) for h in range(HEADS)]
+    begun = passed[0]
 
     def bias_rows(a, carry):
-        at = pl.ds(pl.multiple_of(a * 8, 8), 8)
-        for j in range(4):
-            lanes = pl.ds(j * 128, 128)
-            sums = [None] * HEADS
-            for table in range(3):
-                index = indices[table, at, lanes]
+        @pl.when(lax.rem(a, 2) == 1)
+        def _():
+            net.tick(begun + a // 2)
+
+        for b in range(4):
+            row = a * 32 + b * 8
+            at = pl.ds(pl.multiple_of(row, 8), 8)
+            for j in range(4):
+                sums = [None] * HEADS
+                for table in range(3):
+                    index = indices[table, at, j * 128 : (j + 1) * 128]
+                    for h in range(HEADS):
+                        found = jnp.take_along_axis(rows_by_head[h], index, axis=1)
+                        sums[h] = found if sums[h] is None else sums[h] + found
                 for h in range(HEADS):
-                    found = jnp.take_along_axis(rows_by_head[h], index, axis=1)
-                    sums[h] = found if sums[h] is None else sums[h] + found
-            for h in range(HEADS):
-                bias[h, at, lanes] = sums[h]
+                    flat[pl.ds(pl.multiple_of((4 * h + j) * LEN + row, 8), 8), :] = sums[h]
         return carry
 
-    lax.fori_loop(0, LEN // 8, bias_rows, 0, unroll=4)
-    find_places(coord_col, lut, places)
-
+    lax.fori_loop(0, LEN // 32, bias_rows, 0)
+
+    act_copy(1, cot, cs, False).start()
+    small0 = wall[0, pl.ds(SM0, 48), :].astype(F32)
+    qv_bias = row_of(small0, 0, 12)
+    out_bias, gain_one, shift_one = (row_of(small0, 20 + 6 * i, 6) for i in range(3))
+    down_bias, gain_two, shift_two = (row_of(small1, 38 + 6 * i, 6) for i in range(3))
+    act_copy(0, xin, xs, True).wait_recv()
+
+    w_layout = jnp.concatenate([wall[1, pl.ds(LAY1 + c * FEAT, FEAT), :] for c in range(6)], axis=1)
+
+    def start_rows(r, carry):
+        at = pl.ds(pl.multiple_of(r * QROWS, QROWS), QROWS)
+        rows = xs[at, :].astype(F32) + nn(features[at, :], w_layout)
+        start[at, :] = rows
+        rounded[at, :] = rows.astype(BF16)
+        return carry
+
+    lax.fori_loop(0, LEN // QROWS, start_rows, 0)
+    put(rounded, rounded_out)
+    for i in range(18):
+        up_bias[:, i * 128 : (i + 1) * 128] = (
+            jnp.zeros((1, 128), F32)
+            if i % 3 == 1
+            else qv_bias[:, (i // 3 + 3 * (i % 3)) * 128 : (i // 3 + 3 * (i % 3) + 1) * 128]
+        )
     left = lax.broadcasted_iota(jnp.int32, (LEN, 128), 1) < HDIM
-    for pair in range(PAIRS):
-        weight = jnp.concatenate(
-            [wall[0, pl.ds((3 * pair + i) * D, D), :] for i in range(3)], axis=1
-        )
-        part = nn(rounded[...], weight)
-        lanes = slice(pair * 128, (pair + 1) * 128)
-        query = (part[:, :128] + qv_bias[:, lanes]).astype(BF16)
-        qkv[3 * pair] = query * HDIM**-0.5
-        qkv[3 * pair + 1] = part[:, 128:256].astype(BF16)
-        value_bias = qv_bias[:, D + pair * 128 : D + (pair + 1) * 128]
-        qkv[3 * pair + 2] = (part[:, 256:] + value_bias).astype(BF16)
+
+    def probs_copy(pair):
+        where = rows_at(pair * 8 * LEN, 8 * LEN)
+        return pltpu.make_async_copy(probs.at[where], probs_out.at[where], probs_sem.at[pair])
+
+    begun += LEN // 64
+    assert net.ticks() - begun <= PAIRS
 
     def attend(pair, carry):
-        query, key, value = qkv[3 * pair], qkv[3 * pair + 1], qkv[3 * pair + 2]
+        @pl.when(begun + pair < net.ticks())
+        def _():
+            net.tick(begun + pair)
+
+        at = pl.multiple_of(3 * pair * D, 16)
+        weight = jnp.concatenate([wall[0, rows_at(at + i * D, D), :] for i in range(3)], axis=1)
+        part = nn(rounded[...], weight) + up_bias[:, pl.ds(pl.multiple_of(pair * 384, 128), 384)]
+        query = part[:, :128].astype(BF16) * HDIM**-0.5
+        key = part[:, 128:256].astype(BF16)
+        value = part[:, 256:].astype(BF16)
+        qkv[3 * pair] = query
+        qkv[3 * pair + 1] = key
+        qkv[3 * pair + 2] = value
         found = [[], []]
         for side in range(2):
             head = 2 * pair + side
             mine = left if side == 0 else jnp.logical_not(left)
-            for r in range(0, LEN, QROWS):
-                at = slice(r, r + QROWS)
-                part = query[at]
-                scores = nt(jnp.where(mine[at], part, jnp.zeros_like(part)), key) + bias[head, at, :]
+            for r in range(0, LEN, AROWS):
+                some = query[r : r + AROWS]
+                extra = jnp.concatenate(
+                    [flat[rows_at((4 * head + j) * LEN + r, AROWS), :] for j in range(4)], axis=1
+                )
+                scores = nt(jnp.where(mine[r : r + AROWS], some, jnp.zeros_like(some)), key) + extra
                 scores = jnp.exp(scores - jnp.max(scores, axis=1, keepdims=True))
                 soft = (scores * (1.0 / jnp.sum(scores, axis=1, keepdims=True))).astype(BF16)
                 for j in range(4):
-                    probs[rows_at((4 * head + j) * LEN + r, QROWS), :] = soft[:, j * 128 : (j + 1) * 128]
+                    probs[rows_at((4 * head + j) * LEN + r, AROWS), :] = soft[:, j * 128 : (j + 1) * 128]
                 found[side].append(nn(soft, value))
         mixed[:, pl.ds(pl.multiple_of(pair * 128, 128), 128)] = jnp.where(
             left, jnp.concatenate(found[0], axis=0), jnp.concatenate(found[1], axis=0)
         ).astype(BF16)
+        probs_copy(pair).start()
         return carry
 
     lax.fori_loop(0, PAIRS, attend, 0)
+    merge_up(wall)
+    put(wall, wall_out)
+    put(qkv, qkv_out)
+    put(mixed, mixed_out)
 
     w_out = jnp.concatenate([wall[0, pl.ds(OUT0 + c * D, D), :] for c in range(6)], axis=1)
 
     def first_rows(r, carry):
         at = pl.ds(pl.multiple_of(r * QROWS, QROWS), QROWS)
-        normed, inverse = stats(start[at, :] + nn(mixed[at, :], w_out) + out_bias)
-        normed_one[at, :] = normed
+        unit, inverse = stats(start[at, :] + nn(mixed[at, :], w_out) + out_bias)
+        normed[at, :] = unit
         inverse_one[at, :] = inverse
-        result = normed * gain_one + shift_one
-        first_low[at, :] = result.astype(BF16)
+        result = unit * gain_one + shift_one
+        low[at, :] = result.astype(BF16)
         acc[at, :] = result + down_bias
         return carry
 
     lax.fori_loop(0, LEN // QROWS, first_rows, 0)
+    put(normed, one_out)
+    put(low, low_out)
     for j in range(12):
         up_bias[:, j * 256 : (j + 1) * 256] = row_of(small1, 6 + 2 * j, 2)
 
+    def feed_copies(j):
+        lanes = pl.ds(pl.multiple_of(j * 256, 256), 256)
+        return [
+            pltpu.make_async_copy(hidden.at[:, lanes], hidden_out.at[:, lanes], feed_sem.at[0, j]),
+            pltpu.make_async_copy(slope.at[:, lanes], slope_out.at[:, lanes], feed_sem.at[1, j]),
+        ]
+
     def feed_step(j, carry):
         lanes = pl.ds(pl.multiple_of(j * 256, 256), 256)
-        up = nn(first_low[...], up_block(wall, j)) + up_bias[:, lanes]
+        up = nn(low[...], up_block(wall, j)) + up_bias[:, lanes]
         half_up = 0.5 + 0.5 * lax.erf(up * math.sqrt(0.5))
         bell = jnp.exp(-0.5 * up * up) * (1.0 / math.sqrt(2.0 * math.pi))
         slope[:, lanes] = (half_up + up * bell).astype(BF16)
         part = (up * half_up).astype(BF16)
         hidden[:, lanes] = part
         acc[...] += nn(part, down_rows(wall, j))
+        for copy in feed_copies(j):
+            copy.start()
         return carry
 
-    lax.fori_loop(0, 12, feed_step, 0)
+    lax.fori_loop(0, 12, feed_step, 0, unroll=3)
 
     def second_rows(r, carry):
         at = pl.ds(pl.multiple_of(r * QROWS, QROWS), QROWS)
-        normed, inverse = stats(acc[at, :])
-        normed_two[at, :] = normed
+        unit, inverse = stats(acc[at, :])
+        acc[at, :] = unit
         inverse_two[at, :] = inverse
-        layer_out[at, :] = (normed * gain_two + shift_two).astype(BF16)
+        layer[at, :] = (unit * gain_two + shift_two).astype(BF16)
         return carry
 
     lax.fori_loop(0, LEN // QROWS, second_rows, 0)
-    store.wait()
-
-
-def forward_pass(wall, xdoc, features, coord_row, coord_col):
+    put(acc, two_out)
+    put(layer, layer_out)
+    act_copy(1, cot, cs, True).wait_recv()
+    put(cs, cdoc_out)
+    for number in range(2):
+        act_copy(number, (xin, cot)[number], (xs, cs)[number], False).wait_send()
+    for pair in range(PAIRS):
+        probs_copy(pair).wait()
+    for copy in outs:
+        copy.wait()
+
+    def feed_wait(j, carry):
+        for copy in feed_copies(j):
+            copy.wait()
+        return carry
+
+    lax.fori_loop(0, 12, feed_wait, 0)
+
+
+def forward_pass(stages, p2, xin, cot, cnt, features, coord_row, coord_col):
     pick, keep = table_constants()
     sds = jax.ShapeDtypeStruct
+    dma = pltpu.SemaphoreType.DMA
+    count_peers = 2 + sum(radix - 1 for radix, _ in stages)
+    sems = []
+    for radix, _ in stages:
+        sems += [dma((CHUNKS, radix - 1))] * 2
     return pl.pallas_call(
-        forward_kernel,
-        name="forward",
+        functools.partial(forward_kernel, stages),
+        name="gather_forward",
         out_shape=(
+            sds((2, ROWS, 128), BF16),
             sds((LEN, D), BF16),
+            sds((8, 128), F32),
             sds((LEN, D), BF16),
             sds((18, LEN, 128), BF16),
             sds((HEADS * 4 * LEN, 128), BF16),
@@ -645,22 +689,39 @@
             sds((LEN, D), F32),
             sds((LEN, 1), F32),
             sds((3, LEN, 128), jnp.int32),
-            sds((2, ROWS, 128), BF16),
+            sds((LEN, D), BF16),
         ),
-        in_specs=[ANY] + [VMEM] * 6,
-        out_specs=(VMEM,) * 13 + (ANY,),
+        in_specs=[ANY] + [VMEM] * 8,
+        out_specs=(ANY, ANY, VMEM, ANY, ANY, ANY, ANY, ANY, VMEM, ANY, ANY, ANY, ANY, VMEM, ANY, ANY),
         scratch_shapes=[
+            pltpu.VMEM((LEAD + FLAT + 288, 128), F32),
             pltpu.VMEM((2, ROWS, 128), BF16),
+            pltpu.VMEM((LEN, D), BF16),
+            pltpu.VMEM((LEN, D), BF16),
+            pltpu.VMEM((count_peers, 8, 128), F32),
             pltpu.VMEM((LEN, D), F32),
             pltpu.VMEM((1, FF), F32),
             pltpu.VMEM((LEN, D), F32),
-            pltpu.VMEM((HEADS, LEN, LEN), F32),
             pltpu.VMEM((3, LEN, LEN), jnp.int32),
             pltpu.VMEM((16, 128), jnp.int32),
-            pltpu.SemaphoreType.DMA((1,)),
-        ],
-        compiler_params=pltpu.CompilerParams(vmem_limit_bytes=62 * 2**20),
-    )(wall, xdoc, features, coord_row, coord_col, jnp.asarray(pick), jnp.asarray(keep))
+            pltpu.VMEM((LEN, D), BF16),
+            pltpu.VMEM((18, LEN, 128), BF16),
+            pltpu.VMEM((HEADS * 4 * LEN, 128), BF16),
+            pltpu.VMEM((LEN, D), BF16),
+            pltpu.VMEM((LEN, D), F32),
+            pltpu.VMEM((LEN, D), BF16),
+            pltpu.VMEM((LEN, FF), BF16),
+            pltpu.VMEM((LEN, FF), BF16),
+            pltpu.VMEM((3, LEN, 128), jnp.int32),
+            pltpu.VMEM((LEN, D), BF16),
+            dma((8,)), dma((CHUNKS,)), dma((CHUNKS,)), dma((CHUNKS,)), dma((CHUNKS,)), dma((2,)), dma((2,)),
+            dma((count_peers,)), dma((count_peers,)), dma((16,)), dma((PAIRS,)), dma((2, 12)),
+        ]
+        + sems,
+        compiler_params=pltpu.CompilerParams(
+            collective_id=1, has_side_effects=True, vmem_limit_bytes=64 * 2**20 - 2**16
+        ),
+    )(p2, xin, cot, cnt, features, coord_row, coord_col, jnp.asarray(pick), jnp.asarray(keep))
 
 
 G_SMALL = (("qv_bias", 0, 0, 12), ("out_bias", 0, 12, 6), ("gain_one", 0, 18, 6), ("shift_one", 0, 24, 6),
@@ -686,9 +747,6 @@
     for radix, _ in stages:
         replicas *= radix
     return max(1024, 16 * replicas)
-
-
-SKEW = 2
 
 
 class Reduction:
@@ -878,9 +936,9 @@
 
 def backward_kernel(
     stages,
-    wall_hbm, cdoc_hbm, total, rounded_hbm, qkv_hbm, probs_hbm, mixed_hbm, one_hbm, inverse_one, low_hbm, hidden_hbm,
+    wall_hbm, cdoc_hbm, total, layer_hbm, rounded_hbm, qkv_hbm, probs_hbm, mixed_hbm, one_hbm, inverse_one, low_hbm, hidden_hbm,
     slope_hbm, two_hbm, inverse_two, places_hbm, features, coord_row, coord_col, pick, keep,
-    input_grad, reduced, norm,
+    layer_out, input_grad, reduced, norm,
     wall, gstack, acc, branch, hidden, d_up, low, rounded, qkv, mixed, normed_one, less, places, prefix, small,
     square_slots, load_sem, step_sem, probs_sem, act_send, act_recv, act_sem, n_send, n_recv, *rest,
 ):
@@ -930,6 +988,16 @@
     for load in rest_loads:
         load.start()
     greet(stages)
+
+    def layer_copy(receive):
+        return remote(
+            layer_hbm.at[rows_at(other * half, half)], layer_out.at[other if receive else fs],
+            act_send.at[1], act_recv.at[1], red.x_peer,
+        )
+
+    layer_copy(False).start()
+    layer_own = pltpu.make_async_copy(layer_hbm.at[rows_at(fs * half, half)], layer_out.at[fs], act_sem.at[1])
+    layer_own.start()
     small[...] = jnp.zeros_like(small)
     gstack[1, pl.ds(DOWN_END, LAY1 - DOWN_END), :] = jnp.zeros((LAY1 - DOWN_END, 128), BF16)
     for load in early:
@@ -1086,16 +1154,16 @@
             head = 2 * pair + side
             mine = left if side == 0 else jnp.logical_not(left)
             base = UP0 + slot * 8 * LEN + side * 4 * LEN
-            for r in range(0, LEN, QROWS):
-                part = grad[r : r + QROWS]
-                d_probs = nt(jnp.where(mine[r : r + QROWS], part, jnp.zeros_like(part)), value)
+            for r in range(0, LEN, BROWS):
+                part = grad[r : r + BROWS]
+                d_probs = nt(jnp.where(mine[r : r + BROWS], part, jnp.zeros_like(part)), value)
                 soft = jnp.concatenate(
-                    [wall[0, rows_at(base + j * LEN + r, QROWS), :] for j in range(4)], axis=1
+                    [wall[0, rows_at(base + j * LEN + r, BROWS), :] for j in range(4)], axis=1
                 ).astype(F32)
                 inner = jnp.sum(soft * d_probs, axis=1, keepdims=True)
                 scores = (soft * (d_probs - inner)).astype(BF16)
                 for j in range(4):
-                    wall[1, score_rows(head, j, r, QROWS), :] = scores[:, j * 128 : (j + 1) * 128]
+                    wall[1, score_rows(head, j, r, BROWS), :] = scores[:, j * 128 : (j + 1) * 128]
             scores = jnp.concatenate([wall[1, score_rows(head, j, 0, LEN), :] for j in range(4)], axis=1)
             chances = jnp.concatenate([wall[0, rows_at(base + j * LEN, LEN), :] for j in range(4)], axis=1)
             found.append((nn(scores, key), tn(scores, query), tn(chances, grad)))
@@ -1190,6 +1258,9 @@
     act_own.wait()
     act_out.wait_send()
     act_in.wait_recv()
+    layer_own.wait()
+    layer_copy(False).wait_send()
+    layer_copy(True).wait_recv()
 
 
 def table_grads(wall, coord_row, coord_col, pick, keep, less, places, prefix, small, spots, red, late, pace):
@@ -1259,7 +1330,7 @@
             small[plane, row_at : row_at + 1, :] = flat_row[:, i * 128 : (i + 1) * 128]
 
 
-def backward_pass(stages, wall, cdoc, total, saved, features, coord_row, coord_col):
+def backward_pass(stages, wall, cdoc, total, out_doc, saved, features, coord_row, coord_col):
     pick, keep = table_constants()
     sds = jax.ShapeDtypeStruct
     count_peers = 2 + sum(radix - 1 for radix, _ in stages)
@@ -1268,9 +1339,9 @@
     return pl.pallas_call(
         functools.partial(backward_kernel, stages),
         name="backward_reduce",
-        out_shape=(sds((2, LEN // 2, D), BF16), sds((ROWS, 128), BF16), sds((8, 128), F32)),
-        in_specs=[ANY, ANY, VMEM, ANY, ANY, ANY, ANY, ANY, VMEM, ANY, ANY, ANY, ANY, VMEM, ANY] + [VMEM] * 5,
-        out_specs=(ANY, ANY, VMEM),
+        out_shape=(sds((2, LEN // 2, D), BF16), sds((2, LEN // 2, D), BF16), sds((ROWS, 128), BF16), sds((8, 128), F32)),
+        in_specs=[ANY, ANY, VMEM, ANY, ANY, ANY, ANY, ANY, ANY, VMEM, ANY, ANY, ANY, ANY, VMEM, ANY] + [VMEM] * 5,
+        out_specs=(ANY, ANY, ANY, VMEM),
         scratch_shapes=[
             pltpu.VMEM((2, ROWS, 128), BF16),
             pltpu.VMEM((2, ROWS, 128), BF16),
@@ -1288,14 +1359,14 @@
             pltpu.VMEM((HEADS, 64, LEN), F32),
             pltpu.VMEM((2, 64, 128), F32),
             pltpu.VMEM((count_peers, 8, 128), F32),
-            dma((10,)), dma((5, 12)), dma((2,)), dma((1,)), dma((1,)), dma((1,)), dma((count_peers,)), dma((count_peers,)),
+            dma((10,)), dma((5, 12)), dma((2,)), dma((2,)), dma((2,)), dma((2,)), dma((count_peers,)), dma((count_peers,)),
         ]
         + buffers
         + sems,
         compiler_params=pltpu.CompilerParams(
             collective_id=2, has_side_effects=True, vmem_limit_bytes=64 * 2**20 - 2**16
         ),
-    )(wall, cdoc, total, *saved, features, coord_row, coord_col, jnp.asarray(pick), jnp.asarray(keep))
+    )(wall, cdoc, total, out_doc, *saved, features, coord_row, coord_col, jnp.asarray(pick), jnp.asarray(keep))
 
 
 BLOCK = 1760
@@ -1394,7 +1465,6 @@
 
 def local(stages, inputs, box_coords, mlm_mask, cotangent, params, first_moment, second_moment):
     fs = lax.axis_index("fsdp")
-    half = LEN // 2
     masked = cotangent * mlm_mask.astype(BF16)[..., None]
     count = jnp.full((8, 128), jnp.sum(mlm_mask.astype(F32)))
     boxes = lax.dynamic_index_in_dim(box_coords, fs, 0, keepdims=False)
@@ -1404,14 +1474,12 @@
     )
     coord_row = coord_col.T
     flat = [v.reshape(FLAT, 128) for v in (params, first_moment, second_moment)]
-    wall, xdoc, cdoc, total = gather_weights(stages, flat[0], inputs, masked, count)
-    out_doc, *saved, wall = forward_pass(wall, xdoc, features, coord_row, coord_col)
-    input_grad, reduced, norm = backward_pass(stages, wall, cdoc, total, saved, features, coord_row, coord_col)
-    out_other = lax.ppermute(
-        lax.dynamic_slice_in_dim(out_doc, (1 - fs) * half, half, 0), "fsdp", [(0, 1), (1, 0)]
+    wall, cdoc, total, *saved, out_doc = forward_pass(
+        stages, flat[0], inputs, masked, count, features, coord_row, coord_col
     )
-    out_mine = lax.dynamic_slice_in_dim(out_doc, fs * half, half, 0)
-    layer_out = jnp.where(fs == 0, jnp.stack([out_mine, out_other]), jnp.stack([out_other, out_mine]))
+    layer_out, input_grad, reduced, norm = backward_pass(
+        stages, wall, cdoc, total, out_doc, saved, features, coord_row, coord_col
+    )
     grad, update, new_first = adam(reduced, *flat)
     return (layer_out, input_grad, grad.reshape(-1), norm[0, 0], update.reshape(-1), new_first.reshape(-1))
 

time: 356 us -> 280 us (0.79)
  Pallas kernels: 339 us -> 267 us
    pallas_call x2 -> x1, Pallas kernels: 164 us -> 93.5 us  [forward_pass(): pl.pallas_call(functools.partial(forward_kernel, stages), name='gather_fo...]
  transfers between devices with their start and end apart: 1 -> 0, of which waited for: 0 -> 0; matrix products, arithmetic and copies ran while one was open for 0% -> 0% of each run, Pallas kernels for 49% -> 0%
where the time goes in v3:
time: 280 us; the launch traced here: 279 us
  Pallas kernels  267 us (95%)
  local copies, waits for them, and re-layouts  6.51 us (2%)
  other arithmetic  5.35 us (2%)
    pallas_call x1, Pallas kernels, backward_pass(): pl.pallas_call(functools.partial(backward_kernel, stages), name='backward...  130 us
    pallas_call x1, Pallas kernels, forward_pass(): pl.pallas_call(functools.partial(forward_kernel, stages), name='gather_fo...  93.5 us
    pallas_call x1, Pallas kernels, adam(): pl.pallas_call(adam_kernel, name='adamw', grid=(FLAT // BLOCK,), out_shap...  43.6 us

profile of v3, /device:TPU:0, one launch (start us, length us, event | category | flops | bytes accessed | tf_op | source)
XLA Modules:
  0.0 279.3 jit_solution(14729887754181065281)
XLA Ops:
  0.6 1.3 convert_reduce_fusion
  1.9 0.7 convert_element_type.12
  2.6 1.2 broadcast_in_dim.2.cnt
  3.9 0.7 dynamic-slice_bitcast_fusion
  4.6 0.6 pad_add_fusion
  5.2 0.6 sine_convert_fusion
  5.8 0.8 copy.26.features
  6.6 0.9 copy.27.coord_col
  7.4 2.1 broadcast_multiply_fusion.cot
  9.6 93.5 %gather_forward.1 = (bf16[2,28672,128]{2,1,0:T(8,128)(2,1)}, bf16[512,768]{1,0:T(8,128)(2,1)}, f32[8,128]{1,0:T(8,128)}, bf16[512,768]{1,0:T(8,128)(2,1)}, bf16[...) custom-call(f32[28160,128]{1,0:T(8,128)} %bitcast.12, ...), custom_call_target="tpu_custom_call" | custom-call | tf_op jit(solution)/shard_map/gather_forward/pallas_call | solution.py:673
  103.1 129.7 %backward_reduce.1 = (bf16[2,256,768]{2,1,0:T(8,128)(2,1)}, bf16[2,256,768]{2,1,0:T(8,128)(2,1)}, bf16[28672,128]{1,0:T(8,128)(2,1)}, f32[8,128]{1,0:T(8,128)}) custom-call(bf16[2,28672,128]{2,1,0:T(8,128)(2,1)} %get-tuple-element.29.wall_hbm, bf16[512,768]{1,0:T(8,128)(2,1)} %get-tuple-element.30.cdoc_hbm, f32[8,128]{1,0:T(8,128)} %get-tuple-element.31.total, ...), custom_call_target="tpu_custom_call" | custom-call | tf_op jit(solution)/shard_map/backward_reduce/pallas_call | solution.py:1339
  232.8 1.2 slice.19
  233.9 0.0 copy-start.1
  233.9 0.0 copy-start
  233.9 43.6 %adamw.1 = (f32[28160,128]{1,0:T(8,128)}, f32[28160,128]{1,0:T(8,128)}, f32[28160,128]{1,0:T(8,128)}) custom-call(bf16[28672,128]{1,0:T(8,128)(2,1)} %get-tuple-element.47.source, f32[28160,128]{1,0:T(8,128)} %bitcast.13, f32[28160,128]{1,0:T(8,128)} %bitcast.14, f32[28160,128]{1,0:T(8,128)} %bitcast.15), custom_call_target="tpu_custom_call" | custom-call | tf_op jit(solution)/shard_map/adamw/pallas_call | solution.py:1445
  277.5 0.0 copy-done.1
  277.5 0.9 copy.32
  278.4 0.0 copy-done
  278.4 0.9 copy.33
  (4 shorter events, 0.0 us)
Async XLA Ops:
  233.9 43.6 %copy-start.1 = (bf16[2,256,768]{2,1,0:T(8,128)(2,1)S(1)}, bf16[2,256,768]{2,1,0:T(8,128)(2,1)}, u32[]{:S(2)}) copy-start(bf16[2,256,768]{2,1,0:T(8,128)(2,1)} %get-tuple-element.64) | copy-start | bytes 2359300
  233.9 44.5 %copy-start = (bf16[2,256,768]{2,1,0:T(8,128)(2,1)S(1)}, bf16[2,256,768]{2,1,0:T(8,128)(2,1)}, u32[]{:S(2)}) copy-start(bf16[2,256,768]{2,1,0:T(8,128)(2,1)} %get-tuple-element.65) | copy-start | bytes 2359300

commit v4 on v3

--- a/solution.py
+++ b/solution.py
@@ -104,12 +104,14 @@
     return found
 
 
-def greet(stages):
+def greet_signal(stages):
     barrier = pltpu.get_barrier_semaphore()
-    all_peers = peers(stages)
-    for peer in all_peers:
+    for peer in peers(stages):
         pl.semaphore_signal(barrier, inc=1, device_id=peer, device_id_type=MESH)
-    pl.semaphore_wait(barrier, len(all_peers))
+
+
+def greet_wait(stages):
+    pl.semaphore_wait(pltpu.get_barrier_semaphore(), len(peers(stages)))
 
 
 def remote(src, dst, send, recv, peer):
@@ -191,7 +193,7 @@
     return centered * inverse, inverse
 
 
-def find_places(coord_col, lut, places, tick):
+def find_places(coord_col, lut, ranks, places):
     lane = lax.broadcasted_iota(jnp.int32, (8, 128), 1)
     step = lane % 16
     level = jnp.where(step <= 8, step, lax.shift_left(jnp.full_like(step, 8), jnp.maximum(step - 8, 0)))
@@ -204,37 +206,30 @@
         return carry
 
     lax.fori_loop(0, LEN // 8, line_rows, 0, unroll=4)
+    lanes = lax.broadcasted_iota(jnp.int32, (LEN, 128), 1)
+    ones = jnp.ones((LEN, 128), BF16)
+
+    def flags(condition):
+        return jnp.where(condition, 1.0, 0.0).astype(BF16)
+
     for table in (1, 2):
-        def look(a, best):
-            at = pl.ds(pl.multiple_of(a * 8, 8), 8)
-            near = jnp.broadcast_to(coord_col[at, table : table + 1], (8, 128))
-            code = near * LEN + (lax.broadcasted_iota(jnp.int32, (8, 128), 0) + a * 8)
-            return tuple(
-                jnp.maximum(best[g], jnp.where(near < lane + 128 * g, code, -1)) for g in range(16)
-            )
-
-        best = lax.fori_loop(
-            0, LEN // 8, look, tuple(jnp.full((8, 128), -1, jnp.int32) for _ in range(16)), unroll=2
-        )
-        tick()
-        for g in range(16):
-            most = jnp.max(best[g], axis=0, keepdims=True)
-            lut[g : g + 1, :] = jnp.where(most < 0, LEN, most & (LEN - 1))
+        near = jnp.broadcast_to(coord_col[:, table : table + 1], (LEN, 128))
+        group = near >> 7
+        below = tn(flags(group == lanes), flags((near & 127) < lanes)) + tn(flags(group < lanes), ones)
+        lut[...] = below[:16].astype(jnp.int32)
         luts = [jnp.broadcast_to(lut[g : g + 1, :], (8, 128)) for g in range(16)]
 
         def find(a, carry):
             at = pl.ds(pl.multiple_of(a * 8, 8), 8)
             value = jnp.clip(coord_col[at, table : table + 1] + edge, 0, 2047)
             low, high = value & 127, value >> 7
-            found = jnp.full((8, 128), LEN, jnp.int32)
+            found = jnp.zeros((8, 128), jnp.int32)
             for g in range(16):
                 found = jnp.where(high == g, jnp.take_along_axis(luts[g], low, axis=1), found)
-            places[table, at, :] = found
+            places[table, at, :] = jnp.where(found == 0, LEN, found - 1)
             return carry
 
-        for part in range(2):
-            lax.fori_loop(part * 32, part * 32 + 32, find, 0, unroll=4)
-            tick()
+        lax.fori_loop(0, LEN // 8, find, 0, unroll=8)
 
 
 def relayout(plane, flat, out, group):
@@ -288,12 +283,12 @@
         return lax.rem(CHUNKS - 1 + position, CHUNKS) * CHUNK
 
     def direct(self, position):
-        return (position == 4) | (position == 9) | (position == 12)
+        return (position == 2) | (position == 6) | (position == 10)
 
     def x_copy(self, position, plane, direct):
         start, size = self.parts[0] if direct else self.parts[-1]
         where = self.zall.at[plane, rows_at(self.base(position) + start, size)]
-        return remote(where, where, self.x_send.at[position], self.x_recv.at[position], self.x_peer)
+        return remote(where, where, self.x_send.at[0], self.x_recv.at[position], self.x_peer)
 
     def send(self, low, high):
         def one(position, carry):
@@ -311,47 +306,37 @@
 
         lax.fori_loop(low, high, one, 0)
 
-    def stage_copies(self, level, position, receive):
+    def stage_copies(self, level, position):
         radix, stride = self.stages[level]
         start, size = self.parts[level + 1]
         mine = (self.dp // stride) % radix
         copies = []
         for step in range(1, radix):
             peer = (member(self.dp, radix, stride, (mine + step) % radix), self.fs)
-            shift = ((mine - step + radix) % radix - mine) * size if receive else 0
-            where = self.zall.at[self.other, rows_at(self.base(position) + start + shift, size)]
+            where = self.zall.at[self.other, rows_at(self.base(position) + start, size)]
             copies.append(
-                remote(
-                    where, where, self.sems[2 * level].at[position, step - 1],
-                    self.sems[2 * level + 1].at[position, step - 1], peer,
-                )
+                remote(where, where, self.sems[2 * level].at[0], self.sems[2 * level + 1].at[position], peer)
             )
         return copies
+
+    def stage_wait(self, level, position):
+        size = (self.stages[level][0] - 1) * self.parts[level + 1][1]
+        where = self.zall.at[self.other, rows_at(self.base(position) + self.parts[level][0], size)]
+        remote(
+            where, where, self.sems[2 * level].at[0], self.sems[2 * level + 1].at[position], self.x_peer
+        ).wait_recv()
 
     def core_copy(self, position, receive):
         size = CHUNK // 2
         start = (1 - self.dp % 2 if receive else self.dp % 2) * size
         where = self.zall.at[self.other, rows_at(self.base(position) + start, size)]
-        return remote(where, where, self.c_send.at[position], self.c_recv.at[position], self.core_peer)
+        return remote(where, where, self.c_send.at[0], self.c_recv.at[position], self.core_peer)
 
     def work(self, position, step):
         direct = self.direct(position)
         levels = self.levels
         if step == levels + 1:
             self.core_copy(position, True).wait_recv()
-            self.core_copy(position, False).wait_send()
-
-            @pl.when(direct)
-            def _():
-                self.x_copy(position, self.fs, True).wait_send()
-
-            @pl.when(jnp.logical_not(direct))
-            def _():
-                self.x_copy(position, self.fs, False).wait_send()
-                for level in range(levels):
-                    for copy in self.stage_copies(level, position, False):
-                        copy.wait_send()
-
             return
         if step == 0:
 
@@ -365,10 +350,9 @@
             if step == 0:
                 self.x_copy(position, self.other, False).wait_recv()
             else:
-                for copy in self.stage_copies(levels - step, position, True):
-                    copy.wait_recv()
+                self.stage_wait(levels - step, position)
             if step < levels:
-                for copy in self.stage_copies(levels - 1 - step, position, False):
+                for copy in self.stage_copies(levels - 1 - step, position):
                     copy.start()
             else:
                 self.core_copy(position, False).start()
@@ -384,13 +368,22 @@
     def ticks(self):
         return CHUNKS + SKEW * (self.levels + 1)
 
+    def finish(self):
+        staged = CHUNKS - 3
+        sent = [(self.x_send, 3 * self.parts[0][1] + staged * self.parts[-1][1]), (self.c_send, CHUNKS * CHUNK // 2)]
+        for level, (radix, _) in enumerate(self.stages):
+            sent.append((self.sems[2 * level], staged * (radix - 1) * self.parts[level + 1][1]))
+        for sem, size in sent:
+            where = self.zall.at[0, pl.ds(0, size)]
+            remote(where, where, sem.at[0], self.x_recv.at[0], self.x_peer).wait_send()
+
 
 def forward_kernel(
     stages, p_hbm, xin, cot, cnt, features, coord_row, coord_col, pick, keep,
     wall_out, cdoc_out, total, rounded_out, qkv_out, probs_out, mixed_out, one_out, inverse_one, low_out, hidden_out,
-    slope_out, two_out, inverse_two, places_out, layer_out,
-    flat, wall, xs, cs, cnt_slots, start, up_bias, acc, indices, lut, rounded, qkv, probs, mixed, normed, low, hidden,
-    slope, places, layer,
+    slope_out, two_out, inverse_two, layer_out,
+    flat, wall, xs, cs, cnt_slots, start, up_bias, acc, indices, short, rounded, qkv, probs, mixed, normed, low, hidden,
+    slope, layer,
     in_sem, x_send, x_recv, c_send, c_recv, act_send, act_recv, n_send, n_recv, out_sem, probs_sem, feed_sem, *stage_sems,
 ):
     net = Gather(stages, wall, x_send, x_recv, c_send, c_recv, stage_sems)
@@ -408,7 +401,21 @@
         load.start()
     flat[pl.ds(0, LEAD), :] = jnp.zeros((LEAD, 128), F32)
     flat[pl.ds(LEAD + FLAT, 288), :] = jnp.zeros((288, 128), F32)
-    greet(stages)
+    greet_signal(stages)
+
+    def index_rows(a, carry):
+        at = pl.ds(pl.multiple_of(a * 8, 8), 8)
+        for table in range(3):
+            near = jnp.broadcast_to(coord_col[at, table : table + 1], (8, 128))
+            for j in range(4):
+                far = coord_row[table : table + 1, j * 128 : (j + 1) * 128]
+                indices[table, at, j * 128 : (j + 1) * 128] = (
+                    bucket_of(jnp.broadcast_to(far, (8, 128)) - near) + 32 * table
+                )
+        return carry
+
+    lax.fori_loop(0, LEN // 8, index_rows, 0, unroll=4)
+    greet_wait(stages)
 
     def act_copy(number, source, target, receive):
         where = rows_at((other if receive else fs) * half, half)
@@ -445,6 +452,21 @@
     count_round(0)
     for load in loads:
         load.wait()
+
+    for plane, windows in enumerate((((13824, 16), (18440, 32)), ((8728, 32), (27184, 32), (27976, 16)))):
+
+        @pl.when(fs == plane)
+        def _(plane=plane, windows=windows):
+            dst = 0
+            for src, size in windows:
+                short[plane, pl.ds(dst, size), :] = flat[pl.ds(LEAD + src, size), :].astype(BF16)
+                dst += size
+            short[plane, pl.ds(dst, 96 - dst), :] = jnp.zeros((96 - dst, 128), BF16)
+
+    def short_copy(plane):
+        return remote(short.at[plane], short.at[plane], act_send.at[2], act_recv.at[2], net.x_peer)
+
+    short_copy(fs).start()
     for group, (low_at, high_at) in enumerate(((0, 1), (1, 7), (7, CHUNKS))):
         for plane in range(2):
 
@@ -457,28 +479,9 @@
             act_copy(0, xin, xs, False).start()
     xs[pl.ds(fs * half, half), :] = xin[fs]
     cs[pl.ds(fs * half, half), :] = cot[fs]
-
-    def index_rows(a, carry):
-        at = pl.ds(pl.multiple_of(a * 8, 8), 8)
-        for table in range(3):
-            near = jnp.broadcast_to(coord_col[at, table : table + 1], (8, 128))
-            for j in range(4):
-                far = coord_row[table : table + 1, j * 128 : (j + 1) * 128]
-                indices[table, at, j * 128 : (j + 1) * 128] = (
-                    bucket_of(jnp.broadcast_to(far, (8, 128)) - near) + 32 * table
-                )
-        return carry
-
-    lax.fori_loop(0, LEN // 8, index_rows, 0, unroll=4)
-    passed = [0]
-
-    def tick():
-        net.tick(passed[0])
-        if passed[0] % 2 == 0:
-            count_round(passed[0] // 2 + 1)
-        passed[0] += 1
-
-    find_places(coord_col, lut, places, tick)
+    count_round(1)
+
+    count_round(2)
     outs = []
 
     def put(source, target):
@@ -486,23 +489,20 @@
         copy.start()
         outs.append(copy)
 
-    put(places, places_out)
-    while passed[0] < 1 + SKEW * (net.levels + 1):
-        tick()
-
-    small1 = wall[1, pl.ds(SM1, 80), :].astype(F32)
+    short_copy(other).wait_recv()
+
+    small0, small1 = short[0].astype(F32), short[1].astype(F32)
     heads_by_lane = jnp.zeros((16, 128), F32)
     for table in range(3):
         flat_row = row_of(small1, 64 + 3 * table, 3)
         spread = (jnp.broadcast_to(flat_row, (16, 384)) * keep[...]).astype(BF16)
         heads_by_lane = heads_by_lane + nn(spread, pick[table])
     rows_by_head = [jnp.broadcast_to(heads_by_lane[h : h + 1, :], (8, 128)) for h in range(HEADS)]
-    begun = passed[0]
 
     def bias_rows(a, carry):
-        @pl.when(lax.rem(a, 2) == 1)
+        @pl.when(lax.rem(a, 2) == 0)
         def _():
-            net.tick(begun + a // 2)
+            net.tick(a // 2)
 
         for b in range(4):
             row = a * 32 + b * 8
@@ -521,7 +521,14 @@
     lax.fori_loop(0, LEN // 32, bias_rows, 0)
 
     act_copy(1, cot, cs, False).start()
-    small0 = wall[0, pl.ds(SM0, 48), :].astype(F32)
+    count_round(3)
+    lag = SKEW * (net.levels + 1)
+
+    def drain(number, carry):
+        net.tick(number)
+        return carry
+
+    lax.fori_loop(LEN // 64, 2 + lag, drain, 0)
     qv_bias = row_of(small0, 0, 12)
     out_bias, gain_one, shift_one = (row_of(small0, 20 + 6 * i, 6) for i in range(3))
     down_bias, gain_two, shift_two = (row_of(small1, 38 + 6 * i, 6) for i in range(3))
@@ -550,14 +557,8 @@
         where = rows_at(pair * 8 * LEN, 8 * LEN)
         return pltpu.make_async_copy(probs.at[where], probs_out.at[where], probs_sem.at[pair])
 
-    begun += LEN // 64
-    assert net.ticks() - begun <= PAIRS
-
     def attend(pair, carry):
-        @pl.when(begun + pair < net.ticks())
-        def _():
-            net.tick(begun + pair)
-
+        net.tick(2 + lag + pair)
         at = pl.multiple_of(3 * pair * D, 16)
         weight = jnp.concatenate([wall[0, rows_at(at + i * D, D), :] for i in range(3)], axis=1)
         part = nn(rounded[...], weight) + up_bias[:, pl.ds(pl.multiple_of(pair * 384, 128), 384)]
@@ -589,10 +590,10 @@
         return carry
 
     lax.fori_loop(0, PAIRS, attend, 0)
-    merge_up(wall)
-    put(wall, wall_out)
     put(qkv, qkv_out)
     put(mixed, mixed_out)
+    count_round(4)
+    lax.fori_loop(2 + lag + PAIRS, 10 + lag, drain, 0)
 
     w_out = jnp.concatenate([wall[0, pl.ds(OUT0 + c * D, D), :] for c in range(6)], axis=1)
 
@@ -609,6 +610,11 @@
     lax.fori_loop(0, LEN // QROWS, first_rows, 0)
     put(normed, one_out)
     put(low, low_out)
+    count_round(5)
+    lax.fori_loop(10 + lag, net.ticks(), drain, 0)
+    net.finish()
+    merge_up(wall)
+    put(wall, wall_out)
     for j in range(12):
         up_bias[:, j * 256 : (j + 1) * 256] = row_of(small1, 6 + 2 * j, 2)
 
@@ -649,6 +655,7 @@
     put(cs, cdoc_out)
     for number in range(2):
         act_copy(number, (xin, cot)[number], (xs, cs)[number], False).wait_send()
+    short_copy(fs).wait_send()
     for pair in range(PAIRS):
         probs_copy(pair).wait()
     for copy in outs:
@@ -669,7 +676,7 @@
     count_peers = 2 + sum(radix - 1 for radix, _ in stages)
     sems = []
     for radix, _ in stages:
-        sems += [dma((CHUNKS, radix - 1))] * 2
+        sems += [dma((1,)), dma((CHUNKS,))]
     return pl.pallas_call(
         functools.partial(forward_kernel, stages),
         name="gather_forward",
@@ -688,11 +695,10 @@
             sds((LEN, FF), BF16),
             sds((LEN, D), F32),
             sds((LEN, 1), F32),
-            sds((3, LEN, 128), jnp.int32),
             sds((LEN, D), BF16),
         ),
         in_specs=[ANY] + [VMEM] * 8,
-        out_specs=(ANY, ANY, VMEM, ANY, ANY, ANY, ANY, ANY, VMEM, ANY, ANY, ANY, ANY, VMEM, ANY, ANY),
+        out_specs=(ANY, ANY, VMEM, ANY, ANY, ANY, ANY, ANY, VMEM, ANY, ANY, ANY, ANY, VMEM, ANY),
         scratch_shapes=[
             pltpu.VMEM((LEAD + FLAT + 288, 128), F32),
             pltpu.VMEM((2, ROWS, 128), BF16),
@@ -703,7 +709,7 @@
             pltpu.VMEM((1, FF), F32),
             pltpu.VMEM((LEN, D), F32),
             pltpu.VMEM((3, LEN, LEN), jnp.int32),
-            pltpu.VMEM((16, 128), jnp.int32),
+            pltpu.VMEM((2, 96, 128), BF16),
             pltpu.VMEM((LEN, D), BF16),
             pltpu.VMEM((18, LEN, 128), BF16),
             pltpu.VMEM((HEADS * 4 * LEN, 128), BF16),
@@ -712,9 +718,8 @@
             pltpu.VMEM((LEN, D), BF16),
             pltpu.VMEM((LEN, FF), BF16),
             pltpu.VMEM((LEN, FF), BF16),
-            pltpu.VMEM((3, LEN, 128), jnp.int32),
             pltpu.VMEM((LEN, D), BF16),
-            dma((8,)), dma((CHUNKS,)), dma((CHUNKS,)), dma((CHUNKS,)), dma((CHUNKS,)), dma((2,)), dma((2,)),
+            dma((8,)), dma((1,)), dma((CHUNKS,)), dma((1,)), dma((CHUNKS,)), dma((3,)), dma((3,)),
             dma((count_peers,)), dma((count_peers,)), dma((16,)), dma((PAIRS,)), dma((2, 12)),
         ]
         + sems,
@@ -725,8 +730,7 @@
 
 
 G_SMALL = (("qv_bias", 0, 0, 12), ("out_bias", 0, 12, 6), ("gain_one", 0, 18, 6), ("shift_one", 0, 24, 6),
-           ("up_bias", 1, 0, 24), ("down_bias", 1, 24, 6), ("gain_two", 1, 30, 6), ("shift_two", 1, 36, 6),
-           ("tables", 1, 42, 9))
+           ("up_bias", 1, 0, 24), ("down_bias", 1, 24, 6), ("gain_two", 1, 30, 6), ("shift_two", 1, 36, 6))
 
 
 def spread_norm(normed, inverse, gain, grad):
@@ -775,14 +779,14 @@
         where = rows_at(self.base(position) + (1 - self.dp % 2) * self.half, self.half)
         return remote(
             self.gstack.at[plane, where], self.core_slots.at[plane, position],
-            self.c_send.at[plane, position], self.c_recv.at[plane, position], self.core_peer,
+            self.c_send.at[0], self.c_recv.at[plane, position], self.core_peer,
         )
 
     def x_copy(self, position):
         where = rows_at(self.base(position) + self.parts[0][0], self.half)
         return remote(
             self.gstack.at[self.other, where], self.x_slots.at[position],
-            self.x_send.at[position], self.x_recv.at[position], self.x_peer,
+            self.x_send.at[0], self.x_recv.at[position], self.x_peer,
         )
 
     def scatter_copies(self, level, position):
@@ -797,25 +801,35 @@
             copies.append(
                 remote(
                     self.gstack.at[self.fs, where], self.slots[level].at[position, step - 1],
-                    self.sems[4 * level].at[position, step - 1], self.sems[4 * level + 1].at[position, step - 1],
+                    self.sems[4 * level].at[0], self.sems[4 * level + 1].at[position],
                     (member(self.dp, radix, stride, target), self.fs),
                 )
             )
         return copies
 
-    def spread_copies(self, level, position, receive):
+    def scatter_wait(self, level, position):
+        where = self.slots[level].at[position]
+        remote(where, where, self.sems[4 * level].at[0], self.sems[4 * level + 1].at[position], self.x_peer).wait_recv()
+
+    def spread_wait(self, level, position):
+        size = (self.stages[level][0] - 1) * self.parts[level + 1][1]
+        where = self.out.at[rows_at(self.base(position) + self.parts[level][0], size)]
+        remote(
+            where, where, self.sems[4 * level + 2].at[0], self.sems[4 * level + 3].at[position], self.x_peer
+        ).wait_recv()
+
+    def spread_copies(self, level, position):
         radix, stride = self.stages[level]
         start, size = self.parts[level + 1]
         mine = (self.dp // stride) % radix
         copies = []
         for step in range(1, radix):
-            shift = ((mine - step + radix) % radix - mine) * size if receive else 0
-            where = self.out.at[rows_at(self.base(position) + start + shift, size)]
-            source = self.pieces.at[position] if level == self.levels - 1 and not receive else where
+            where = self.out.at[rows_at(self.base(position) + start, size)]
+            source = self.pieces.at[position] if level == self.levels - 1 else where
             copies.append(
                 remote(
                     source, where,
-                    self.sems[4 * level + 2].at[position, step - 1], self.sems[4 * level + 3].at[position, step - 1],
+                    self.sems[4 * level + 2].at[0], self.sems[4 * level + 3].at[position],
                     (member(self.dp, radix, stride, (mine + step) % radix), self.fs),
                 )
             )
@@ -831,7 +845,7 @@
     def back_copy(self, position, receive):
         start = (1 - self.dp % 2 if receive else self.dp % 2) * self.half
         where = self.out.at[rows_at(self.base(position) + start, self.half)]
-        return remote(where, where, self.b_send.at[position], self.b_recv.at[position], self.core_peer)
+        return remote(where, where, self.b_send.at[0], self.b_recv.at[position], self.core_peer)
 
     def feed(self, plane, low, high):
         def one(position, carry):
@@ -862,8 +876,7 @@
                 self.x_copy(position).wait_recv()
                 terms = [self.core_slots[self.fs, position], self.x_slots[position]]
             else:
-                for copy in self.scatter_copies(step - 1, position):
-                    copy.wait()
+                self.scatter_wait(step - 1, position)
                 terms = [self.slots[step - 1][position, i] for i in range(self.stages[step - 1][0] - 1)]
             value = self.gstack[self.fs, where, :].astype(F32)
             for term in terms:
@@ -875,21 +888,15 @@
             else:
                 self.pieces[position] = value.astype(BF16)
                 self.own_copy(position).start()
-                for copy in self.spread_copies(levels - 1, position, False):
+                for copy in self.spread_copies(levels - 1, position):
                     copy.start()
         else:
             level = 2 * levels - step
-            for copy in self.spread_copies(level, position, True):
-                copy.wait_recv()
-            for copy in self.spread_copies(level, position, False):
-                copy.wait_send()
+            self.spread_wait(level, position)
             if level == levels - 1:
                 self.own_copy(position).wait()
-                self.x_copy(position).wait_send()
-                for plane in range(2):
-                    self.core_copy(position, plane).wait_send()
             if level > 0:
-                for copy in self.spread_copies(level - 1, position, False):
+                for copy in self.spread_copies(level - 1, position):
                     copy.start()
             else:
                 self.back_copy(position, False).start()
@@ -908,10 +915,16 @@
     def finish(self):
         def one(position, carry):
             self.back_copy(position, True).wait_recv()
-            self.back_copy(position, False).wait_send()
             return carry
 
         lax.fori_loop(0, self.count, one, 0)
+        sent = [(self.c_send, 2 * self.half), (self.x_send, self.half), (self.b_send, self.half)]
+        for level, (radix, _) in enumerate(self.stages):
+            size = (radix - 1) * self.parts[level + 1][1]
+            sent += [(self.sems[4 * level], size), (self.sems[4 * level + 2], size)]
+        for sem, size in sent:
+            where = self.gstack.at[0, pl.ds(0, self.count * size)]
+            remote(where, where, sem.at[0], self.x_recv.at[0], self.x_peer).wait_send()
 
 
 def reduction_scratch(stages):
@@ -922,7 +935,7 @@
     for radix, _ in stages:
         half = half // radix
         slots.append(pltpu.VMEM((count, radix - 1, half, 128), BF16))
-        sems += [dma((count, radix - 1))] * 4
+        sems += [dma((1,)), dma((count,))] * 2
     return (
         [
             pltpu.VMEM((2, count, size // 2, 128), BF16),
@@ -930,16 +943,16 @@
             pltpu.VMEM((count, half, 128), BF16),
         ]
         + slots,
-        [dma((2, count)), dma((2, count))] + [dma((count,))] * 5 + sems,
+        [dma((1,)), dma((2, count)), dma((1,)), dma((count,)), dma((1,)), dma((count,)), dma((count,))] + sems,
     )
 
 
 def backward_kernel(
     stages,
     wall_hbm, cdoc_hbm, total, layer_hbm, rounded_hbm, qkv_hbm, probs_hbm, mixed_hbm, one_hbm, inverse_one, low_hbm, hidden_hbm,
-    slope_hbm, two_hbm, inverse_two, places_hbm, features, coord_row, coord_col, pick, keep,
-    layer_out, input_grad, reduced, norm,
-    wall, gstack, acc, branch, hidden, d_up, low, rounded, qkv, mixed, normed_one, less, places, prefix, small,
+    slope_hbm, two_hbm, inverse_two, features, coord_row, coord_col, pick, keep,
+    layer_out, input_grad, reduced, tables, norm,
+    wall, gstack, acc, branch, hidden, d_up, low, rounded, qkv, mixed, normed_one, places, lut, ranks, layer, small,
     square_slots, load_sem, step_sem, probs_sem, act_send, act_recv, act_sem, n_send, n_recv, *rest,
 ):
     levels = len(stages)
@@ -953,6 +966,7 @@
         pltpu.make_async_copy(cdoc_hbm, branch, load_sem.at[1]),
         pltpu.make_async_copy(two_hbm, acc, load_sem.at[2]),
     ]
+    early.append(pltpu.make_async_copy(layer_hbm, layer, load_sem.at[9]))
     lows = [pltpu.make_async_copy(low_hbm, low, load_sem.at[3])]
     rest_loads = [
         pltpu.make_async_copy(one_hbm, normed_one, load_sem.at[4]),
@@ -960,7 +974,6 @@
         pltpu.make_async_copy(mixed_hbm, mixed, load_sem.at[6]),
         pltpu.make_async_copy(qkv_hbm, qkv, load_sem.at[7]),
         pltpu.make_async_copy(rounded_hbm, rounded, load_sem.at[8]),
-        pltpu.make_async_copy(places_hbm, places, load_sem.at[9]),
     ]
 
     def step_loads(j):
@@ -987,22 +1000,30 @@
     lax.fori_loop(0, 12, start_loads, 0)
     for load in rest_loads:
         load.start()
-    greet(stages)
+    greet_signal(stages)
+    find_places(coord_col, lut, ranks, places)
+    for table in (1, 2):
+        key_row = jnp.broadcast_to(coord_row[table : table + 1, :], (256, LEN))
+        for r in (0, 256):
+            near = jnp.broadcast_to(coord_col[r : r + 256, table : table + 1], (256, LEN))
+            lower = jnp.where(key_row < near, 1.0, 0.0).astype(BF16)
+            ranks[table - 1, r : r + 256, :] = nn(lower, jnp.ones((LEN, 128), BF16))
+    greet_wait(stages)
 
     def layer_copy(receive):
         return remote(
-            layer_hbm.at[rows_at(other * half, half)], layer_out.at[other if receive else fs],
+            layer.at[rows_at(other * half, half)], layer_out.at[other if receive else fs],
             act_send.at[1], act_recv.at[1], red.x_peer,
         )
 
-    layer_copy(False).start()
-    layer_own = pltpu.make_async_copy(layer_hbm.at[rows_at(fs * half, half)], layer_out.at[fs], act_sem.at[1])
-    layer_own.start()
+    layer_own = pltpu.make_async_copy(layer.at[rows_at(fs * half, half)], layer_out.at[fs], act_sem.at[1])
     small[...] = jnp.zeros_like(small)
     gstack[1, pl.ds(DOWN_END, LAY1 - DOWN_END), :] = jnp.zeros((LAY1 - DOWN_END, 128), BF16)
     for load in early:
         load.wait()
 
+    layer_copy(False).start()
+    layer_own.start()
     small0 = wall[0, pl.ds(SM0, 48), :].astype(F32)
     small1 = wall[1, pl.ds(SM1, 80), :].astype(F32)
     gain_one = row_of(small0, 26, 6)
@@ -1204,17 +1225,19 @@
         red.push(sent(4), sent(5))
 
     late = 2 + per_pair * PAIRS
-    pace = 2 if fine else 5
-    table_grads(wall, coord_row, coord_col, pick, keep, less, places, prefix, small, spots, red, late, pace)
-    late += (23 + pace) // pace
-
     for plane in range(2):
         gstack[plane, pl.ds(SM0, 64), :] = small[plane].astype(BF16)
         gstack[plane, pl.ds(SM0 + 64, ROWS - SM0 - 64), :] = jnp.zeros((ROWS - SM0 - 64, 128), BF16)
         red.feed(plane, last, last + 1)
+    drain(late, 0)
     red.push(last, last + 1)
+    late += 1
+    pace = 2 if fine else 4
+    table_grads(wall, coord_col, pick, keep, hidden, places, ranks, normed_one, tables, red, late, pace)
+    late += 24 // pace
 
     summed = red.count + SKEW * levels
+    assert late <= summed
     lax.fori_loop(late, summed, drain, 0)
 
     def squares(position, carry):
@@ -1223,7 +1246,7 @@
 
     value = lax.fori_loop(0, red.count, squares, jnp.zeros((8, 128), F32))
     value = jnp.sum(jnp.sum(value, axis=0, keepdims=True), axis=1, keepdims=True)
-    norm[...] = jnp.broadcast_to(value, (8, 128))
+    tables[9:10, :] = jnp.broadcast_to(value, (1, 128))
     rounds = [
         [
             (member(dp, radix, stride, ((dp // stride) % radix + step) % radix), fs)
@@ -1235,7 +1258,7 @@
     def square_copies(number):
         base = sum(len(r) for r in rounds[:number])
         return [
-            remote(norm.at[...], square_slots.at[base + i], n_send.at[base + i], n_recv.at[base + i], peer)
+            remote(tables.at[...], square_slots.at[base + i], n_send.at[base + i], n_recv.at[base + i], peer)
             for i, peer in enumerate(rounds[number])
         ]
 
@@ -1246,13 +1269,15 @@
         if summed + number < red.ticks():
             red.tick(summed + number)
         if number < len(rounds):
-            gathered = norm[...]
+            gathered = tables[...]
             base = sum(len(r) for r in rounds[:number])
             for i, copy in enumerate(square_copies(number)):
                 copy.wait()
                 gathered = gathered + square_slots[base + i]
-            norm[...] = gathered
-    norm[...] = jnp.sqrt(norm[...])
+            tables[...] = gathered
+    gathered = tables[0:9, :]
+    gathered = jnp.sum(jnp.sum(gathered * gathered, axis=0, keepdims=True), axis=1, keepdims=True)
+    norm[...] = jnp.broadcast_to(jnp.sqrt(tables[9:10, :] + gathered), (8, 128))
 
     red.finish()
     act_own.wait()
@@ -1263,15 +1288,19 @@
     layer_copy(True).wait_recv()
 
 
-def table_grads(wall, coord_row, coord_col, pick, keep, less, places, prefix, small, spots, red, late, pace):
+def table_grads(wall, coord_col, pick, keep, less, places, ranks, prefix, tables, red, late, pace):
+    tables[...] = jnp.zeros_like(tables)
     block = 64
     for table in range(3):
-        key_row = jnp.broadcast_to(coord_row[table : table + 1, :], (16, LEN))
+        order = lax.broadcasted_iota(jnp.int32, (16, LEN), 1)
 
         def less_rows(a, carry):
             at = pl.ds(pl.multiple_of(a * 16, 16), 16)
-            near = jnp.broadcast_to(coord_col[at, table : table + 1], (16, LEN))
-            less[at, :] = jnp.where(near <= key_row, 1.0, 0.0).astype(BF16)
+            if table == 0:
+                near = jnp.broadcast_to(coord_col[at, 0:1], (16, LEN))
+            else:
+                near = jnp.concatenate([ranks[table - 1, at, :].astype(jnp.int32)] * 4, axis=1)
+            less[at, 0:LEN] = jnp.where(near <= order, 1.0, 0.0).astype(BF16)
             return carry
 
         lax.fori_loop(0, LEN // 16, less_rows, 0, unroll=4)
@@ -1291,22 +1320,27 @@
                 ],
                 axis=0,
             )
-            prefix[...] = nn(scores, less[...]).reshape(HEADS, block, LEN)
+            summed = nn(scores, less[:, 0:LEN])
+            for h in range(HEADS):
+                for j in range(4):
+                    r, c = (4 * h + j) // 6 * 64, (4 * h + j) % 6 * 128
+                    prefix[r : r + 64, c : c + 128] = summed[h * block : (h + 1) * block, j * 128 : (j + 1) * 128]
 
             def pick_up(a, carry):
-                at = pl.ds(pl.multiple_of(a * 8, 8), 8)
                 place_of = places[table, pl.ds(pl.multiple_of(start + a * 8, 8), 8), :]
                 low, high = place_of & 127, place_of >> 7
                 result = []
                 for h in range(HEADS):
                     value = jnp.zeros((8, 128), F32)
                     for j in range(4):
-                        part = jnp.take_along_axis(prefix[h, at, j * 128 : (j + 1) * 128], low, axis=1)
+                        r, c = (4 * h + j) // 6 * 64, (4 * h + j) % 6 * 128
+                        rows = pl.ds(pl.multiple_of(r + a * 8, 8), 8)
+                        part = jnp.take_along_axis(prefix[rows, c : c + 128], low, axis=1)
                         value = jnp.where(high == j, part, value)
                     result.append(carry[h] + value)
                 return tuple(result)
 
-            return lax.fori_loop(0, block // 8, pick_up, sums, unroll=4)
+            return lax.fori_loop(0, block // 8, pick_up, sums, unroll=8)
 
         sums = lax.fori_loop(
             0, LEN // block, query_rows, tuple(jnp.zeros((8, 128), F32) for _ in range(HEADS))
@@ -1323,11 +1357,14 @@
         buckets = jnp.where(lanes == 31, whole - heads, buckets)
         buckets = jnp.where(lanes < 32, buckets, 0.0)
         placed = buckets if table == 0 else pltpu.roll(buckets, 32 * table, 1)
-        flat_row = jnp.sum(nt(placed.astype(BF16), pick[table]) * keep[...], axis=0, keepdims=True)
-        plane, at = spots["tables"]
+        parts, left_over = [], placed
+        for _ in range(2):
+            parts.append(left_over.astype(BF16))
+            left_over = left_over - parts[-1].astype(F32)
+        spread = sum(nt(part, pick[table]) for part in parts)
+        flat_row = jnp.sum(spread * keep[...], axis=0, keepdims=True)
         for i in range(3):
-            row_at = at + 3 * table + i
-            small[plane, row_at : row_at + 1, :] = flat_row[:, i * 128 : (i + 1) * 128]
+            tables[3 * table + i : 3 * table + i + 1, :] = flat_row[:, i * 128 : (i + 1) * 128]
 
 
 def backward_pass(stages, wall, cdoc, total, out_doc, saved, features, coord_row, coord_col):
@@ -1339,9 +1376,9 @@
     return pl.pallas_call(
         functools.partial(backward_kernel, stages),
         name="backward_reduce",
-        out_shape=(sds((2, LEN // 2, D), BF16), sds((2, LEN // 2, D), BF16), sds((ROWS, 128), BF16), sds((8, 128), F32)),
-        in_specs=[ANY, ANY, VMEM, ANY, ANY, ANY, ANY, ANY, ANY, VMEM, ANY, ANY, ANY, ANY, VMEM, ANY] + [VMEM] * 5,
-        out_specs=(ANY, ANY, ANY, VMEM),
+        out_shape=(sds((2, LEN // 2, D), BF16), sds((2, LEN // 2, D), BF16), sds((ROWS, 128), BF16), sds((16, 128), F32), sds((8, 128), F32)),
+        in_specs=[ANY, ANY, VMEM, ANY, ANY, ANY, ANY, ANY, ANY, VMEM, ANY, ANY, ANY, ANY, VMEM] + [VMEM] * 5,
+        out_specs=(ANY, ANY, ANY, VMEM, VMEM),
         scratch_shapes=[
             pltpu.VMEM((2, ROWS, 128), BF16),
             pltpu.VMEM((2, ROWS, 128), BF16),
@@ -1354,11 +1391,12 @@
             pltpu.VMEM((18, LEN, 128), BF16),
             pltpu.VMEM((LEN, D), BF16),
             pltpu.VMEM((LEN, D), F32),
-            pltpu.VMEM((LEN, LEN), BF16),
             pltpu.VMEM((3, LEN, 128), jnp.int32),
-            pltpu.VMEM((HEADS, 64, LEN), F32),
+            pltpu.VMEM((16, 128), jnp.int32),
+            pltpu.VMEM((2, LEN, 128), F32),
+            pltpu.VMEM((LEN, D), BF16),
             pltpu.VMEM((2, 64, 128), F32),
-            pltpu.VMEM((count_peers, 8, 128), F32),
+            pltpu.VMEM((count_peers, 16, 128), F32),
             dma((10,)), dma((5, 12)), dma((2,)), dma((2,)), dma((2,)), dma((2,)), dma((count_peers,)), dma((count_peers,)),
         ]
         + buffers
@@ -1369,52 +1407,77 @@
     )(wall, cdoc, total, out_doc, *saved, features, coord_row, coord_col, jnp.asarray(pick), jnp.asarray(keep))
 
 
-BLOCK = 1760
-
-
-def flatten_rows(plane, source, flat):
-    def block(src, dst, count, stride):
-        flat[pl.ds(LEAD + dst, count, stride=stride), :] = source[pl.ds(src, count), :].astype(F32)
+BLOCK = 3520
+
+
+DOWN_STEPS = (0, 0, 2, 4, 6, 9, 11, 12, 12)
+
+
+def flatten_rows(plane, step, source, tables, flat):
+    def blocks(low, high, src, dst, rows, stride):
+        def one(i, carry):
+            flat[pl.ds(LEAD + dst(i), rows, stride=stride), :] = source[rows_at(src(i), rows), :].astype(F32)
+            return carry
+
+        lax.fori_loop(low, high, one, 0)
 
     if plane == 0:
-        for c in range(24):
-            block(UP0 + c * UP_A, F_UP + c, UP_A, 24)
-        for pos in range(18):
-            block(pos * D, (pos % 3) * 6 + pos // 3, D, 18)
-        for c in range(6):
-            block(OUT0 + c * D, F_OUT + c, D, 6)
-        small = source[pl.ds(SM0, 64), :].astype(F32)
-        flat[pl.ds(LEAD + 13824, 12), :] = small[0:12]
-        flat[pl.ds(LEAD + 18444, 18), :] = small[12:30]
+        if step == 0:
+            blocks(0, 18, lambda pos: pos * D, lambda pos: lax.rem(pos, 3) * 6 + pos // 3, D, 18)
+            small = source[pl.ds(SM0, 64), :].astype(F32)
+            flat[pl.ds(LEAD + 13824, 12), :] = small[0:12]
+            flat[pl.ds(LEAD + 18444, 18), :] = small[12:30]
+        elif step == 2:
+            blocks(0, 6, lambda c: OUT0 + c * D, lambda c: F_OUT + c, D, 6)
+        elif step == 4:
+            blocks(0, 24, lambda c: UP0 + c * UP_A, lambda c: F_UP + c, UP_A, 24)
     else:
-        for c in range(24):
-            block(UP1 + c * UP_B, c - 98, UP_B, 24)
-        for j in range(12):
+        if step == 0:
+            blocks(0, 24, lambda c: UP1 + c * UP_B, lambda c: c - 98, UP_B, 24)
+            small = source[pl.ds(SM1, 64), :].astype(F32)
+            flat[pl.ds(LEAD + F_UPB1, 24), :] = small[0:24]
+            flat[pl.ds(LEAD + F_SM1, 18), :] = small[24:42]
+            flat[pl.ds(LEAD + F_TAB1, 9), :] = tables[0:9, :]
+            rest = FLAT - F_TAB1 - 9
+            flat[pl.ds(LEAD + F_TAB1 + 9, rest), :] = jnp.zeros((rest, 128), F32)
+        elif step == 6:
+            blocks(0, 6, lambda c: LAY1 + c * FEAT, lambda c: F_LAY1 + c, FEAT, 6)
+        low, high = DOWN_STEPS[step], DOWN_STEPS[step + 1]
+        if low < high:
             for c in range(6):
-                block(DOWN1 + j * 1536 + c * 256, F_DOWN1 + j * 1536 + c, 256, 6)
-        for c in range(6):
-            block(LAY1 + c * FEAT, F_LAY1 + c, FEAT, 6)
-        small = source[pl.ds(SM1, 64), :].astype(F32)
-        flat[pl.ds(LEAD + F_UPB1, 24), :] = small[0:24]
-        flat[pl.ds(LEAD + F_SM1, 18), :] = small[24:42]
-        flat[pl.ds(LEAD + F_TAB1, 9), :] = small[42:51]
-        rest = FLAT - F_TAB1 - 9
-        flat[pl.ds(LEAD + F_TAB1 + 9, rest), :] = jnp.zeros((rest, 128), F32)
-
-
-def adam_kernel(source, weights, first, second, grad_out, update_out, first_out, flat):
+                blocks(
+                    low, high, lambda j: DOWN1 + j * 1536 + c * 256, lambda j: F_DOWN1 + j * 1536 + c, 256, 6
+                )
+
+
+def adam_kernel(
+    source_hbm, tables, weights, first, second, grad_out, update_out, first_out, source, flat, sem,
+):
     step = pl.program_id(0)
     fs = lax.axis_index("fsdp")
+    spans = ((0, OUT0), (SM0, ROWS - SM0), (OUT0, SM0 - OUT0))
+    loads = [
+        pltpu.make_async_copy(source_hbm.at[pl.ds(a, n)], source.at[pl.ds(a, n)], sem.at[i])
+        for i, (a, n) in enumerate(spans)
+    ]
 
     @pl.when(step == 0)
     def _():
-        @pl.when(fs == 0)
-        def _():
-            flatten_rows(0, source, flat)
-
-        @pl.when(fs == 1)
-        def _():
-            flatten_rows(1, source, flat)
+        for load in loads:
+            load.start()
+        for load in loads[:2]:
+            load.wait()
+
+    @pl.when(step == 1)
+    def _():
+        loads[2].wait()
+
+    for number in range(FLAT // BLOCK):
+        for plane in range(2):
+
+            @pl.when((step == number) & (fs == plane))
+            def _(plane=plane, number=number):
+                flatten_rows(plane, number, source, tables, flat)
 
     part = 160
     row = lax.broadcasted_iota(jnp.int32, (part, 128), 0)
@@ -1426,11 +1489,8 @@
         grad_out[at, :] = grad
         new_first = adam_one * first[at, :] + (1.0 - adam_one) * grad
         new_second = adam_two * second[at, :] + (1.0 - adam_two) * grad * grad
-        corrected = (
-            new_first
-            / (1.0 - adam_one**adam_steps)
-            / (jnp.sqrt(new_second / (1.0 - adam_two**adam_steps)) + adam_eps)
-        )
+        spread = jnp.sqrt(new_second * (1.0 / (1.0 - adam_two**adam_steps))) + adam_eps
+        corrected = new_first * (1.0 / (1.0 - adam_one**adam_steps)) / spread
         rate = jnp.where((fs == 1) & (row + begin >= F_LAY1), table_factor, 1.0)
         update_out[at, :] = rate * (corrected + decay_rate * weights[at, :])
         first_out[at, :] = new_first
@@ -1439,7 +1499,7 @@
     lax.fori_loop(0, BLOCK // part, some, 0)
 
 
-def adam(source, weights, first, second):
+def adam(source, tables, weights, first, second):
     block = pl.BlockSpec((BLOCK, 128), lambda i: (i, 0))
     vector = jax.ShapeDtypeStruct((FLAT, 128), F32)
     return pl.pallas_call(
@@ -1447,11 +1507,15 @@
         name="adamw",
         grid=(FLAT // BLOCK,),
         out_shape=(vector, vector, vector),
-        in_specs=[VMEM, block, block, block],
+        in_specs=[ANY, pl.BlockSpec((16, 128), lambda i: (0, 0)), block, block, block],
         out_specs=(block, block, block),
-        scratch_shapes=[pltpu.VMEM((LEAD + FLAT + 288, 128), F32)],
+        scratch_shapes=[
+            pltpu.VMEM((ROWS, 128), BF16),
+            pltpu.VMEM((LEAD + FLAT + 288, 128), F32),
+            pltpu.SemaphoreType.DMA((3,)),
+        ],
         compiler_params=pltpu.CompilerParams(vmem_limit_bytes=60 * 2**20),
-    )(source, weights, first, second)
+    )(source, tables, weights, first, second)
 
 
 def layout_features(coords):
@@ -1477,10 +1541,10 @@
     wall, cdoc, total, *saved, out_doc = forward_pass(
         stages, flat[0], inputs, masked, count, features, coord_row, coord_col
     )
-    layer_out, input_grad, reduced, norm = backward_pass(
+    layer_out, input_grad, reduced, tables, norm = backward_pass(
         stages, wall, cdoc, total, out_doc, saved, features, coord_row, coord_col
     )
-    grad, update, new_first = adam(reduced, *flat)
+    grad, update, new_first = adam(reduced, tables, *flat)
     return (layer_out, input_grad, grad.reshape(-1), norm[0, 0], update.reshape(-1), new_first.reshape(-1))
 
 

time: 280 us -> 262 us (0.936)
  Pallas kernels: 267 us -> 249 us
    pallas_call x1, Pallas kernels: 93.5 us -> 76.9 us  [forward_pass(): pl.pallas_call(functools.partial(forward_kernel, stages), name='gather_fo...]
    pallas_call x1, Pallas kernels: 43.6 us -> 40.3 us  [adam(): pl.pallas_call(adam_kernel, name='adamw', grid=(FLAT // BLOCK,), out_shap...]
where the time goes in v4:
time: 262 us
  Pallas kernels  249 us (95%)
  local copies, waits for them, and re-layouts  6.52 us (2%)
  other arithmetic  5.35 us (2%)
    pallas_call x1, Pallas kernels, backward_pass(): pl.pallas_call(functools.partial(backward_kernel, stages), name='backward...  132 us
    pallas_call x1, Pallas kernels, forward_pass(): pl.pallas_call(functools.partial(forward_kernel, stages), name='gather_fo...  76.9 us
    pallas_call x1, Pallas kernels, adam(): pl.pallas_call(adam_kernel, name='adamw', grid=(FLAT // BLOCK,), out_shap...  40.3 us

profile of v4, /device:TPU:0, one launch (start us, length us, event | category | flops | bytes accessed | tf_op | source)
XLA Modules:
  0.0 261.6 jit_solution(7116555745628232971)
XLA Ops:
  0.6 1.3 convert_reduce_fusion
  1.9 0.7 convert_element_type.12
  2.6 1.2 broadcast_in_dim.2.cnt
  3.9 0.7 dynamic-slice_bitcast_fusion
  4.6 0.6 pad_add_fusion
  5.2 0.6 sine_convert_fusion
  5.8 0.8 copy.26.features
  6.6 0.9 copy.27.coord_col
  7.4 2.1 broadcast_multiply_fusion.cot
  9.6 76.9 %gather_forward.1 = (bf16[2,28672,128]{2,1,0:T(8,128)(2,1)}, bf16[512,768]{1,0:T(8,128)(2,1)}, f32[8,128]{1,0:T(8,128)}, bf16[512,768]{1,0:T(8,128)(2,1)}, bf16[...) custom-call(f32[28160,128]{1,0:T(8,128)} %bitcast.12, ...), custom_call_target="tpu_custom_call" | custom-call | tf_op jit(solution)/shard_map/gather_forward/pallas_call | solution.py:680
  86.4 131.9 %backward_reduce.1 = (bf16[2,256,768]{2,1,0:T(8,128)(2,1)}, bf16[2,256,768]{2,1,0:T(8,128)(2,1)}, bf16[28672,128]{1,0:T(8,128)(2,1)}, f32[16,128]{1,0:T(8,128)}, f32[8,128]{1,0:T(8,128)}) custom-call(bf16[2,28672,128]{2,1,0:T(8,128)(2,1)} %get-tuple-element.29.wall_hbm, bf16[512,768]{1,0:T(8,128)(2,1)} %get-tuple-element.30.cdoc_hbm, ...), custom_call_target="tpu_custom_call" | custom-call | tf_op jit(solution)/shard_map/backward_reduce/pallas_call | solution.py:1376
  218.3 1.2 slice.19
  219.5 0.0 copy-start.1
  219.5 0.0 copy-start
  219.5 40.3 %adamw.1 = (f32[28160,128]{1,0:T(8,128)}, f32[28160,128]{1,0:T(8,128)}, f32[28160,128]{1,0:T(8,128)}) custom-call(bf16[28672,128]{1,0:T(8,128)(2,1)} %get-tuple-element.46.source_hbm, f32[16,128]{1,0:T(8,128)} %get-tuple-element.47.tables, f32[28160,128]{1,0:T(8,128)} %bitcast.13, f32[28160,128]{1,0:T(8,128)} %bitcast.14, f32[28160,128]{1,0:T(8,128)} %bitcast.15), custom_call_target="tpu_custom_call" | custom-call | tf_op jit(solution)/shard_map/adamw/pallas_call | solution.py:1505
  259.8 0.0 copy-done.1
  259.8 0.9 copy.32
  260.7 0.0 copy-done
  260.7 0.9 copy.33
  (4 shorter events, 0.0 us)
Async XLA Ops:
  219.5 40.3 %copy-start.1 = (bf16[2,256,768]{2,1,0:T(8,128)(2,1)S(1)}, bf16[2,256,768]{2,1,0:T(8,128)(2,1)}, u32[]{:S(2)}) copy-start(bf16[2,256,768]{2,1,0:T(8,128)(2,1)} %get-tuple-element.64) | copy-start | bytes 2359300
  219.5 41.2 %copy-start = (bf16[2,256,768]{2,1,0:T(8,128)(2,1)S(1)}, bf16[2,256,768]{2,1,0:T(8,128)(2,1)}, u32[]{:S(2)}) copy-start(bf16[2,256,768]{2,1,0:T(8,128)(2,1)} %get-tuple-element.65) | copy-start | bytes 2359300

commit v5 on v4

--- a/solution.py
+++ b/solution.py
@@ -193,7 +193,7 @@
     return centered * inverse, inverse
 
 
-def find_places(coord_col, lut, ranks, places):
+def find_places(coord_col, lut, ranks, places, tick):
     lane = lax.broadcasted_iota(jnp.int32, (8, 128), 1)
     step = lane % 16
     level = jnp.where(step <= 8, step, lax.shift_left(jnp.full_like(step, 8), jnp.maximum(step - 8, 0)))
@@ -229,7 +229,9 @@
             places[table, at, :] = jnp.where(found == 0, LEN, found - 1)
             return carry
 
-        lax.fori_loop(0, LEN // 8, find, 0, unroll=8)
+        for part in range(2):
+            tick()
+            lax.fori_loop(part * 32, part * 32 + 32, find, 0, unroll=8)
 
 
 def relayout(plane, flat, out, group):
@@ -283,7 +285,7 @@
         return lax.rem(CHUNKS - 1 + position, CHUNKS) * CHUNK
 
     def direct(self, position):
-        return (position == 2) | (position == 6) | (position == 10)
+        return position >= CHUNKS - 3
 
     def x_copy(self, position, plane, direct):
         start, size = self.parts[0] if direct else self.parts[-1]
@@ -467,7 +469,7 @@
         return remote(short.at[plane], short.at[plane], act_send.at[2], act_recv.at[2], net.x_peer)
 
     short_copy(fs).start()
-    for group, (low_at, high_at) in enumerate(((0, 1), (1, 7), (7, CHUNKS))):
+    for group, (low_at, high_at) in enumerate(((0, 1), (1, 7), (7, CHUNKS - 3))):
         for plane in range(2):
 
             @pl.when(fs == plane)
@@ -475,8 +477,8 @@
                 relayout(plane, flat, wall, group)
 
         net.send(low_at, high_at)
-        if group == 1:
-            act_copy(0, xin, xs, False).start()
+    act_copy(0, xin, xs, False).start()
+    net.send(CHUNKS - 3, CHUNKS)
     xs[pl.ds(fs * half, half), :] = xin[fs]
     cs[pl.ds(fs * half, half), :] = cot[fs]
     count_round(1)
@@ -949,24 +951,22 @@
 
 def backward_kernel(
     stages,
-    wall_hbm, cdoc_hbm, total, layer_hbm, rounded_hbm, qkv_hbm, probs_hbm, mixed_hbm, one_hbm, inverse_one, low_hbm, hidden_hbm,
+    wall_hbm, cdoc_hbm, total, rounded_hbm, qkv_hbm, probs_hbm, mixed_hbm, one_hbm, inverse_one, low_hbm, hidden_hbm,
     slope_hbm, two_hbm, inverse_two, features, coord_row, coord_col, pick, keep,
-    layer_out, input_grad, reduced, tables, norm,
-    wall, gstack, acc, branch, hidden, d_up, low, rounded, qkv, mixed, normed_one, places, lut, ranks, layer, small,
-    square_slots, load_sem, step_sem, probs_sem, act_send, act_recv, act_sem, n_send, n_recv, *rest,
+    input_grad, reduced, tables, norm,
+    wall, gstack, acc, branch, hidden, d_up, low, rounded, qkv, mixed, normed_one, places, lut, ranks, small,
+    square_slots, load_sem, step_sem, probs_sem, act_sem, n_send, n_recv, *rest,
 ):
     levels = len(stages)
     parts_vmem, sems = rest[: 3 + levels], rest[3 + levels :]
     red = Reduction(stages, gstack, reduced, parts_vmem[0], parts_vmem[1], parts_vmem[2], parts_vmem[3:], sems)
     dp, fs, other = red.dp, red.fs, red.other
-    half = LEN // 2
 
     early = [
         pltpu.make_async_copy(wall_hbm.at[:, pl.ds(SM0, 256)], wall.at[:, pl.ds(SM0, 256)], load_sem.at[0]),
         pltpu.make_async_copy(cdoc_hbm, branch, load_sem.at[1]),
         pltpu.make_async_copy(two_hbm, acc, load_sem.at[2]),
     ]
-    early.append(pltpu.make_async_copy(layer_hbm, layer, load_sem.at[9]))
     lows = [pltpu.make_async_copy(low_hbm, low, load_sem.at[3])]
     rest_loads = [
         pltpu.make_async_copy(one_hbm, normed_one, load_sem.at[4]),
@@ -1001,29 +1001,12 @@
     for load in rest_loads:
         load.start()
     greet_signal(stages)
-    find_places(coord_col, lut, ranks, places)
-    for table in (1, 2):
-        key_row = jnp.broadcast_to(coord_row[table : table + 1, :], (256, LEN))
-        for r in (0, 256):
-            near = jnp.broadcast_to(coord_col[r : r + 256, table : table + 1], (256, LEN))
-            lower = jnp.where(key_row < near, 1.0, 0.0).astype(BF16)
-            ranks[table - 1, r : r + 256, :] = nn(lower, jnp.ones((LEN, 128), BF16))
     greet_wait(stages)
-
-    def layer_copy(receive):
-        return remote(
-            layer.at[rows_at(other * half, half)], layer_out.at[other if receive else fs],
-            act_send.at[1], act_recv.at[1], red.x_peer,
-        )
-
-    layer_own = pltpu.make_async_copy(layer.at[rows_at(fs * half, half)], layer_out.at[fs], act_sem.at[1])
     small[...] = jnp.zeros_like(small)
     gstack[1, pl.ds(DOWN_END, LAY1 - DOWN_END), :] = jnp.zeros((LAY1 - DOWN_END, 128), BF16)
     for load in early:
         load.wait()
 
-    layer_copy(False).start()
-    layer_own.start()
     small0 = wall[0, pl.ds(SM0, 48), :].astype(F32)
     small1 = wall[1, pl.ds(SM1, 80), :].astype(F32)
     gain_one = row_of(small0, 26, 6)
@@ -1071,6 +1054,10 @@
         for plane in range(2):
             red.feed(plane, fed(plane, it - 2), fed(plane, it - 1))
         red.push(of_other([fed(p, it - 3) for p in range(2)]), of_other([fed(p, it - 2) for p in range(2)]))
+        @pl.when(it == 10)
+        def _():
+            red.tick(0)
+
         lanes = pl.ds(pl.multiple_of(j * 256, 256), 256)
         grad = nt(branch[...], down_rows(wall, j))
         part = (grad * d_up[:, lanes].astype(F32)).astype(BF16)
@@ -1107,6 +1094,7 @@
     red.feed(0, fed(0, 10), fed(0, 11))
     red.feed(1, fed(1, 10), last)
     red.push(of_other([fed(p, 9) for p in range(2)]), of_other([fed(p, 10) for p in range(2)]))
+    red.tick(1)
     for load in rest_loads:
         load.wait()
 
@@ -1127,6 +1115,8 @@
         keep_small(name, vector)
     red.push(of_other([fed(p, 10) for p in range(2)]), jnp.where(other == 0, fed(0, 11), last))
 
+    red.tick(2)
+
     def drain(number, carry):
         red.tick(number)
         return carry
@@ -1141,8 +1131,10 @@
         return carry
 
     lax.fori_loop(0, 3, out_step, 0)
-    drain(0, 0)
-    drain(1, 0)
+    begun = 3
+    if fine:
+        red.tick(3)
+        begun = 4
 
     left = lax.broadcasted_iota(jnp.int32, (LEN, 128), 1) < HDIM
 
@@ -1166,12 +1158,14 @@
         def _():
             red.push(sent(it - 3), sent(it - 2))
 
-        lax.fori_loop(2 + per_pair * it, 2 + per_pair * (it + 1), drain, 0)
+        red.tick(begun + per_pair * it)
         probs_copy(pair, slot).wait()
         query, key, value = qkv[3 * pair], qkv[3 * pair + 1], qkv[3 * pair + 2]
         grad = low[:, pl.ds(pl.multiple_of(pair * 128, 128), 128)]
         found = []
         for side in range(2):
+            if side == 1 and per_pair == 2:
+                red.tick(begun + per_pair * it + 1)
             head = 2 * pair + side
             mine = left if side == 0 else jnp.logical_not(left)
             base = UP0 + slot * 8 * LEN + side * 4 * LEN
@@ -1211,11 +1205,8 @@
         red.push(sent(3), sent(4))
 
     branch[...] = acc[...].astype(BF16)
-    act_out = remote(branch.at[rows_at(other * half, half)], input_grad.at[fs], act_send.at[0], act_recv.at[0], red.x_peer)
-    act_in = remote(branch.at[rows_at(other * half, half)], input_grad.at[other], act_send.at[0], act_recv.at[0], red.x_peer)
-    act_own = pltpu.make_async_copy(branch.at[rows_at(fs * half, half)], input_grad.at[fs], act_sem.at[0])
+    act_out = pltpu.make_async_copy(branch, input_grad, act_sem.at[0])
     act_out.start()
-    act_own.start()
     layout = tn(features[...], branch[...]).astype(BF16)
     for c in range(6):
         gstack[1, pl.ds(LAY1 + c * FEAT, FEAT), :] = layout[:, c * 128 : (c + 1) * 128]
@@ -1224,7 +1215,7 @@
     def _():
         red.push(sent(4), sent(5))
 
-    late = 2 + per_pair * PAIRS
+    late = begun + per_pair * PAIRS
     for plane in range(2):
         gstack[plane, pl.ds(SM0, 64), :] = small[plane].astype(BF16)
         gstack[plane, pl.ds(SM0 + 64, ROWS - SM0 - 64), :] = jnp.zeros((ROWS - SM0 - 64, 128), BF16)
@@ -1232,12 +1223,24 @@
     drain(late, 0)
     red.push(last, last + 1)
     late += 1
+    summed = red.count + SKEW * levels
+    passed = [late]
+
+    def tick():
+        red.tick(passed[0])
+        passed[0] += 1
+
+    find_places(coord_col, lut, ranks, places, tick if fine else lambda: None)
+    for table in (1, 2):
+        key_row = jnp.broadcast_to(coord_row[table : table + 1, :], (256, LEN))
+        for r in (0, 256):
+            near = jnp.broadcast_to(coord_col[r : r + 256, table : table + 1], (256, LEN))
+            lower = jnp.where(key_row < near, 1.0, 0.0).astype(BF16)
+            ranks[table - 1, r : r + 256, :] = nn(lower, jnp.ones((LEN, 128), BF16))
+    late = passed[0]
     pace = 2 if fine else 4
-    table_grads(wall, coord_col, pick, keep, hidden, places, ranks, normed_one, tables, red, late, pace)
-    late += 24 // pace
-
-    summed = red.count + SKEW * levels
-    assert late <= summed
+    table_grads(wall, coord_col, pick, keep, hidden, places, ranks, normed_one, tables, red, late, pace, summed)
+    late = min(late + 24 // pace, summed)
     lax.fori_loop(late, summed, drain, 0)
 
     def squares(position, carry):
@@ -1280,15 +1283,10 @@
     norm[...] = jnp.broadcast_to(jnp.sqrt(tables[9:10, :] + gathered), (8, 128))
 
     red.finish()
-    act_own.wait()
-    act_out.wait_send()
-    act_in.wait_recv()
-    layer_own.wait()
-    layer_copy(False).wait_send()
-    layer_copy(True).wait_recv()
-
-
-def table_grads(wall, coord_col, pick, keep, less, places, ranks, prefix, tables, red, late, pace):
+    act_out.wait()
+
+
+def table_grads(wall, coord_col, pick, keep, less, places, ranks, prefix, tables, red, late, pace, summed):
     tables[...] = jnp.zeros_like(tables)
     block = 64
     for table in range(3):
@@ -1306,9 +1304,11 @@
         lax.fori_loop(0, LEN // 16, less_rows, 0, unroll=4)
 
         def query_rows(b, sums):
-            @pl.when(lax.rem(table * 8 + b, pace) == 0)
+            number = late + (table * 8 + b) // pace
+
+            @pl.when((lax.rem(table * 8 + b, pace) == 0) & (number < summed))
             def _():
-                red.tick(late + (table * 8 + b) // pace)
+                red.tick(number)
 
             start = b * block
             scores = jnp.concatenate(
@@ -1320,11 +1320,11 @@
                 ],
                 axis=0,
             )
-            summed = nn(scores, less[:, 0:LEN])
+            running = nn(scores, less[:, 0:LEN])
             for h in range(HEADS):
                 for j in range(4):
                     r, c = (4 * h + j) // 6 * 64, (4 * h + j) % 6 * 128
-                    prefix[r : r + 64, c : c + 128] = summed[h * block : (h + 1) * block, j * 128 : (j + 1) * 128]
+                    prefix[r : r + 64, c : c + 128] = running[h * block : (h + 1) * block, j * 128 : (j + 1) * 128]
 
             def pick_up(a, carry):
                 place_of = places[table, pl.ds(pl.multiple_of(start + a * 8, 8), 8), :]
@@ -1367,7 +1367,7 @@
             tables[3 * table + i : 3 * table + i + 1, :] = flat_row[:, i * 128 : (i + 1) * 128]
 
 
-def backward_pass(stages, wall, cdoc, total, out_doc, saved, features, coord_row, coord_col):
+def backward_pass(stages, wall, cdoc, total, saved, features, coord_row, coord_col):
     pick, keep = table_constants()
     sds = jax.ShapeDtypeStruct
     count_peers = 2 + sum(radix - 1 for radix, _ in stages)
@@ -1376,9 +1376,9 @@
     return pl.pallas_call(
         functools.partial(backward_kernel, stages),
         name="backward_reduce",
-        out_shape=(sds((2, LEN // 2, D), BF16), sds((2, LEN // 2, D), BF16), sds((ROWS, 128), BF16), sds((16, 128), F32), sds((8, 128), F32)),
-        in_specs=[ANY, ANY, VMEM, ANY, ANY, ANY, ANY, ANY, ANY, VMEM, ANY, ANY, ANY, ANY, VMEM] + [VMEM] * 5,
-        out_specs=(ANY, ANY, ANY, VMEM, VMEM),
+        out_shape=(sds((LEN, D), BF16), sds((ROWS, 128), BF16), sds((16, 128), F32), sds((8, 128), F32)),
+        in_specs=[ANY, ANY, VMEM, ANY, ANY, ANY, ANY, ANY, VMEM, ANY, ANY, ANY, ANY, VMEM] + [VMEM] * 5,
+        out_specs=(ANY, ANY, VMEM, VMEM),
         scratch_shapes=[
             pltpu.VMEM((2, ROWS, 128), BF16),
             pltpu.VMEM((2, ROWS, 128), BF16),
@@ -1394,23 +1394,20 @@
             pltpu.VMEM((3, LEN, 128), jnp.int32),
             pltpu.VMEM((16, 128), jnp.int32),
             pltpu.VMEM((2, LEN, 128), F32),
-            pltpu.VMEM((LEN, D), BF16),
             pltpu.VMEM((2, 64, 128), F32),
             pltpu.VMEM((count_peers, 16, 128), F32),
-            dma((10,)), dma((5, 12)), dma((2,)), dma((2,)), dma((2,)), dma((2,)), dma((count_peers,)), dma((count_peers,)),
+            dma((10,)), dma((5, 12)), dma((2,)), dma((1,)), dma((count_peers,)), dma((count_peers,)),
         ]
         + buffers
         + sems,
         compiler_params=pltpu.CompilerParams(
             collective_id=2, has_side_effects=True, vmem_limit_bytes=64 * 2**20 - 2**16
         ),
-    )(wall, cdoc, total, out_doc, *saved, features, coord_row, coord_col, jnp.asarray(pick), jnp.asarray(keep))
-
-
-BLOCK = 3520
-
-
-DOWN_STEPS = (0, 0, 2, 4, 6, 9, 11, 12, 12)
+    )(wall, cdoc, total, *saved, features, coord_row, coord_col, jnp.asarray(pick), jnp.asarray(keep))
+
+
+BLOCK = 1408
+DEEP_IN, DEEP_OUT = 4, 3
 
 
 def flatten_rows(plane, step, source, tables, flat):
@@ -1422,98 +1419,132 @@
         lax.fori_loop(low, high, one, 0)
 
     if plane == 0:
-        if step == 0:
-            blocks(0, 18, lambda pos: pos * D, lambda pos: lax.rem(pos, 3) * 6 + pos // 3, D, 18)
+        for part in (0, 1) if step == 0 else (step + 1,) if step < 7 else ():
+            blocks(
+                0, 18, lambda pos: pos * D + 96 * part,
+                lambda pos: lax.rem(pos, 3) * 6 + pos // 3 + 96 * 18 * part, 96, 18,
+            )
+        if step == 4:
             small = source[pl.ds(SM0, 64), :].astype(F32)
             flat[pl.ds(LEAD + 13824, 12), :] = small[0:12]
             flat[pl.ds(LEAD + 18444, 18), :] = small[12:30]
-        elif step == 2:
+        elif step == 7:
             blocks(0, 6, lambda c: OUT0 + c * D, lambda c: F_OUT + c, D, 6)
-        elif step == 4:
-            blocks(0, 24, lambda c: UP0 + c * UP_A, lambda c: F_UP + c, UP_A, 24)
+        elif step in (10, 11):
+            first = 208 * (step - 10)
+            blocks(0, 24, lambda c: UP0 + c * UP_A + first, lambda c: F_UP + c + 24 * first, 208, 24)
     else:
-        if step == 0:
-            blocks(0, 24, lambda c: UP1 + c * UP_B, lambda c: c - 98, UP_B, 24)
+        if step < 4:
+            first, rows = 96 * step, min(96, UP_B - 96 * step)
+            blocks(0, 24, lambda c: UP1 + c * UP_B + first, lambda c: c - 98 + 24 * first, rows, 24)
+        elif step < 16:
+            j = step - 4
+            blocks(
+                0, 6, lambda c: DOWN1 + j * 1536 + c * 256, lambda c: F_DOWN1 + j * 1536 + c, 256, 6
+            )
+        if step == 4:
             small = source[pl.ds(SM1, 64), :].astype(F32)
             flat[pl.ds(LEAD + F_UPB1, 24), :] = small[0:24]
             flat[pl.ds(LEAD + F_SM1, 18), :] = small[24:42]
             flat[pl.ds(LEAD + F_TAB1, 9), :] = tables[0:9, :]
             rest = FLAT - F_TAB1 - 9
             flat[pl.ds(LEAD + F_TAB1 + 9, rest), :] = jnp.zeros((rest, 128), F32)
-        elif step == 6:
+        elif step == 16:
             blocks(0, 6, lambda c: LAY1 + c * FEAT, lambda c: F_LAY1 + c, FEAT, 6)
-        low, high = DOWN_STEPS[step], DOWN_STEPS[step + 1]
-        if low < high:
-            for c in range(6):
-                blocks(
-                    low, high, lambda j: DOWN1 + j * 1536 + c * 256, lambda j: F_DOWN1 + j * 1536 + c, 256, 6
-                )
 
 
 def adam_kernel(
-    source_hbm, tables, weights, first, second, grad_out, update_out, first_out, source, flat, sem,
+    source_hbm, tables, weights_hbm, first_hbm, second_hbm, grad_hbm, update_hbm, new_hbm,
+    source, flat, weights, first, second, update, new, sem, in_sem, out_sem,
 ):
-    step = pl.program_id(0)
     fs = lax.axis_index("fsdp")
-    spans = ((0, OUT0), (SM0, ROWS - SM0), (OUT0, SM0 - OUT0))
+    steps = FLAT // BLOCK
     loads = [
         pltpu.make_async_copy(source_hbm.at[pl.ds(a, n)], source.at[pl.ds(a, n)], sem.at[i])
-        for i, (a, n) in enumerate(spans)
+        for i, (a, n) in enumerate(((0, OUT0), (OUT0, ROWS - OUT0)))
     ]
 
-    @pl.when(step == 0)
-    def _():
-        for load in loads:
-            load.start()
-        for load in loads[:2]:
-            load.wait()
-
-    @pl.when(step == 1)
-    def _():
-        loads[2].wait()
-
-    for number in range(FLAT // BLOCK):
+    def fetch(step):
+        where, slot = pl.ds(step * BLOCK, BLOCK), step % DEEP_IN
+        return [
+            pltpu.make_async_copy(ref.at[where], buffer.at[slot], in_sem.at[i, slot])
+            for i, (ref, buffer) in enumerate(((weights_hbm, weights), (first_hbm, first), (second_hbm, second)))
+        ]
+
+    def store(step):
+        where, slot = pl.ds(step * BLOCK, BLOCK), step % DEEP_OUT
+        return [
+            pltpu.make_async_copy(flat.at[pl.ds(LEAD + step * BLOCK, BLOCK)], grad_hbm.at[where], out_sem.at[0, slot]),
+            pltpu.make_async_copy(update.at[slot], update_hbm.at[where], out_sem.at[1, slot]),
+            pltpu.make_async_copy(new.at[slot], new_hbm.at[where], out_sem.at[2, slot]),
+        ]
+
+    loads[0].start()
+    for step in range(DEEP_IN):
+        for copy in fetch(step):
+            copy.start()
+        if step == 0:
+            loads[1].start()
+    part = 176
+    row = lax.broadcasted_iota(jnp.int32, (part, 128), 0)
+    for step in range(steps):
+        if step == 0:
+            loads[0].wait()
+        if step == 3:
+            loads[1].wait()
         for plane in range(2):
 
-            @pl.when((step == number) & (fs == plane))
-            def _(plane=plane, number=number):
-                flatten_rows(plane, number, source, tables, flat)
-
-    part = 160
-    row = lax.broadcasted_iota(jnp.int32, (part, 128), 0)
-
-    def some(i, carry):
-        at = pl.ds(pl.multiple_of(i * part, 8), part)
-        begin = pl.multiple_of(step * BLOCK + i * part, 8)
-        grad = flat[pl.ds(LEAD + begin, part), :]
-        grad_out[at, :] = grad
-        new_first = adam_one * first[at, :] + (1.0 - adam_one) * grad
-        new_second = adam_two * second[at, :] + (1.0 - adam_two) * grad * grad
-        spread = jnp.sqrt(new_second * (1.0 / (1.0 - adam_two**adam_steps))) + adam_eps
-        corrected = new_first * (1.0 / (1.0 - adam_one**adam_steps)) / spread
-        rate = jnp.where((fs == 1) & (row + begin >= F_LAY1), table_factor, 1.0)
-        update_out[at, :] = rate * (corrected + decay_rate * weights[at, :])
-        first_out[at, :] = new_first
-        return carry
-
-    lax.fori_loop(0, BLOCK // part, some, 0)
+            @pl.when(fs == plane)
+            def _(plane=plane, step=step):
+                flatten_rows(plane, step, source, tables, flat)
+
+        if step >= DEEP_OUT:
+            for copy in store(step - DEEP_OUT):
+                copy.wait()
+        for copy in fetch(step):
+            copy.wait()
+        slot_in, slot_out = step % DEEP_IN, step % DEEP_OUT
+
+        def some(i, carry):
+            at = pl.ds(pl.multiple_of(i * part, 8), part)
+            begin = pl.multiple_of(step * BLOCK + i * part, 8)
+            grad = flat[pl.ds(LEAD + begin, part), :]
+            new_first = adam_one * first[slot_in, at, :] + (1.0 - adam_one) * grad
+            new_second = adam_two * second[slot_in, at, :] + (1.0 - adam_two) * grad * grad
+            spread = jnp.sqrt(new_second * (1.0 / (1.0 - adam_two**adam_steps))) + adam_eps
+            corrected = new_first * (1.0 / (1.0 - adam_one**adam_steps)) / spread
+            rate = jnp.where((fs == 1) & (row + begin >= F_LAY1), table_factor, 1.0)
+            update[slot_out, at, :] = rate * (corrected + decay_rate * weights[slot_in, at, :])
+            new[slot_out, at, :] = new_first
+            return carry
+
+        lax.fori_loop(0, BLOCK // part, some, 0)
+        for copy in store(step):
+            copy.start()
+        if step + DEEP_IN < steps:
+            for copy in fetch(step + DEEP_IN):
+                copy.start()
+    for step in range(steps - DEEP_OUT, steps):
+        for copy in store(step):
+            copy.wait()
 
 
 def adam(source, tables, weights, first, second):
-    block = pl.BlockSpec((BLOCK, 128), lambda i: (i, 0))
     vector = jax.ShapeDtypeStruct((FLAT, 128), F32)
+    dma = pltpu.SemaphoreType.DMA
     return pl.pallas_call(
         adam_kernel,
         name="adamw",
-        grid=(FLAT // BLOCK,),
         out_shape=(vector, vector, vector),
-        in_specs=[ANY, pl.BlockSpec((16, 128), lambda i: (0, 0)), block, block, block],
-        out_specs=(block, block, block),
+        in_specs=[ANY, VMEM, ANY, ANY, ANY],
+        out_specs=(ANY, ANY, ANY),
         scratch_shapes=[
             pltpu.VMEM((ROWS, 128), BF16),
             pltpu.VMEM((LEAD + FLAT + 288, 128), F32),
-            pltpu.SemaphoreType.DMA((3,)),
-        ],
+        ]
+        + [pltpu.VMEM((DEEP_IN, BLOCK, 128), F32)] * 3
+        + [pltpu.VMEM((DEEP_OUT, BLOCK, 128), F32)] * 2
+        + [dma((2,)), dma((3, DEEP_IN)), dma((3, DEEP_OUT))],
         compiler_params=pltpu.CompilerParams(vmem_limit_bytes=60 * 2**20),
     )(source, tables, weights, first, second)
 
@@ -1541,11 +1572,28 @@
     wall, cdoc, total, *saved, out_doc = forward_pass(
         stages, flat[0], inputs, masked, count, features, coord_row, coord_col
     )
-    layer_out, input_grad, reduced, tables, norm = backward_pass(
-        stages, wall, cdoc, total, out_doc, saved, features, coord_row, coord_col
+    grad_doc, reduced, tables, norm = backward_pass(
+        stages, wall, cdoc, total, saved, features, coord_row, coord_col
     )
+    half = LEN // 2
+
+    def moved(doc):
+        return lax.ppermute(lax.dynamic_slice_in_dim(doc, (1 - fs) * half, half, 0), "fsdp", [(0, 1), (1, 0)])
+
+    def owned(doc, other):
+        mine = lax.dynamic_slice_in_dim(doc, fs * half, half, 0)
+        return jnp.where(fs == 0, jnp.stack([mine, other]), jnp.stack([other, mine]))
+
+    out_other, grad_other = moved(out_doc), moved(grad_doc)
     grad, update, new_first = adam(reduced, tables, *flat)
-    return (layer_out, input_grad, grad.reshape(-1), norm[0, 0], update.reshape(-1), new_first.reshape(-1))
+    return (
+        owned(out_doc, out_other),
+        owned(grad_doc, grad_other),
+        grad.reshape(-1),
+        norm[0, 0],
+        update.reshape(-1),
+        new_first.reshape(-1),
+    )
 
 
 def solution(mesh):

time: 262 us -> 247 us (0.943)
  Pallas kernels: 249 us -> 225 us
  starting transfers between devices: 0 us -> 3.89 us
  other arithmetic: 5.35 us -> 8.47 us
    pallas_call x1, Pallas kernels: 76.9 us -> 68.6 us  [forward_pass(): pl.pallas_call(functools.partial(forward_kernel, stages), name='gather_fo...]
    pallas_call x1, Pallas kernels: 132 us -> 124 us  [backward_pass(): pl.pallas_call(functools.partial(backward_kernel, stages), name='backward...]
    pallas_call x1, Pallas kernels: 40.3 us -> 33 us  [adam(): pl.pallas_call(adam_kernel, name='adamw', out_shape=(vector, vector, vect...]
    ppermute x0 -> x2, starting transfers between devices: none -> 3.89 us  [moved(): lax.ppermute(lax.dynamic_slice_in_dim(doc, (1 - fs) * half, half, 0), 'fs...]
    another operation x0 -> x2, local copies, waits for them, and re-layouts: none -> 3.23 us  [owned(): jnp.stack([mine, other])]
    select_n x0 -> x2, other arithmetic: none -> 3.12 us  [owned(): jnp.where(fs == 0, jnp.stack([mine, other]), jnp.stack([other, mine]))]
  transfers between devices with their start and end apart: 0 -> 2, of which waited for: 0 -> 0; matrix products, arithmetic and copies ran while one was open for 0% -> 2% of each run, Pallas kernels for 0% -> 64%
where the time goes in v5:
time: 247 us; the launch traced here: 246 us
  Pallas kernels  225 us (91%)
  other arithmetic  8.47 us (3%)
  local copies, waits for them, and re-layouts  7.98 us (3%)
  starting transfers between devices  3.89 us (2%)
    pallas_call x1, Pallas kernels, backward_pass(): pl.pallas_call(functools.partial(backward_kernel, stages), name='backward...  124 us
    pallas_call x1, Pallas kernels, forward_pass(): pl.pallas_call(functools.partial(forward_kernel, stages), name='gather_fo...  68.6 us
    pallas_call x1, Pallas kernels, adam(): pl.pallas_call(adam_kernel, name='adamw', out_shape=(vector, vector, vect...  33 us
  transfers between devices with their start and end apart: 2, of which 0 were waited for; matrix products, arithmetic and copies ran while one was open for 2% of the time, Pallas kernels for 64%

profile of v5, /device:TPU:0, one launch (start us, length us, event | category | flops | bytes accessed | tf_op | source)
XLA Modules:
  0.0 246.4 jit_solution(12954312116407269905)
XLA Ops:
  0.6 1.3 convert_reduce_fusion
  1.9 0.7 convert_element_type.12
  2.6 0.7 dynamic-slice_bitcast_fusion.2
  3.3 0.6 sine_convert_fusion
  3.9 0.8 copy.26.features
  4.7 0.6 pad_add_fusion
  5.3 0.9 copy.27.coord_col
  6.2 2.1 broadcast_multiply_fusion.cot
  8.3 1.2 broadcast_in_dim.2.cnt
  9.6 68.6 %gather_forward.1 = (bf16[2,28672,128]{2,1,0:T(8,128)(2,1)}, bf16[512,768]{1,0:T(8,128)(2,1)}, f32[8,128]{1,0:T(8,128)}, bf16[512,768]{1,0:T(8,128)(2,1)}, bf16[...) custom-call(f32[28160,128]{1,0:T(8,128)} %bitcast.18, ...), custom_call_target="tpu_custom_call" | custom-call | tf_op jit(solution)/shard_map/gather_forward/pallas_call | solution.py:682
  78.1 2.0 dynamic-slice_bitcast_fusion.1
  80.2 1.5 collective-permute-start
  81.7 123.8 %backward_reduce.1 = (bf16[512,768]{1,0:T(8,128)(2,1)}, bf16[28672,128]{1,0:T(8,128)(2,1)}, f32[16,128]{1,0:T(8,128)}, f32[8,128]{1,0:T(8,128)}) custom-call(bf16[2,28672,128]{2,1,0:T(8,128)(2,1)} %get-tuple-element.29.wall_hbm, bf16[512,768]{1,0:T(8,128)(2,1)} %get-tuple-element.30.cdoc_hbm, f32[8,128]{1,0:T(8,128)} %get-tuple-element.31.total, ...), custom_call_target="tpu_custom_call" | custom-call | tf_op jit(solution)/shard_map/backward_reduce/pallas_call | solution.py:1376
  205.6 1.2 dynamic-slice_bitcast_fusion
  206.8 2.3 collective-permute-start.1
  209.1 1.2 slice.19
  210.3 0.0 copy-start
  210.3 33.0 %adamw.1 = (f32[28160,128]{1,0:T(8,128)}, f32[28160,128]{1,0:T(8,128)}, f32[28160,128]{1,0:T(8,128)}) custom-call(bf16[28672,128]{1,0:T(8,128)(2,1)} %get-tuple-element.44.source_hbm, f32[16,128]{1,0:T(8,128)} %get-tuple-element.45.tables, f32[28160,128]{1,0:T(8,128)} %bitcast.19, f32[28160,128]{1,0:T(8,128)} %bitcast.20, f32[28160,128]{1,0:T(8,128)} %bitcast.21), custom_call_target="tpu_custom_call" | custom-call | tf_op jit(solution)/shard_map/adamw/pallas_call | solution.py:1535
  243.3 0.0 collective-permute-done
  243.3 0.0 copy-done
  243.3 2.1 maximum_select_fusion
  245.4 0.0 collective-permute-done.1
  245.4 1.0 maximum_select_fusion.1
  (4 shorter events, 0.0 us)
Async XLA Ops:
  80.2 163.1 %collective-permute-start = (bf16[256,768]{1,0:T(8,128)(2,1)}, bf16[256,768]{1,0:T(8,128)(2,1)}, u32[]{:S(2)}, u32[]{:S(2)}) collective-permute-start(bf16[256,768]{1,0:T(8,128)(2,1)} %get-tuple-element.53), channel_id=1, source_target_pairs={{0,1},{1,0},{2,3},{3,2},{4,5},{5,4},{6,7},{7,6},{8,9},{9,8},{10,11... | collective-permute-start | bytes 1179656 | tf_op jit(solution)/shard_map/ppermute | solution.py:1581
  206.8 38.6 %collective-permute-start.1 = (bf16[256,768]{1,0:T(8,128)(2,1)S(1)}, bf16[256,768]{1,0:T(8,128)(2,1)S(1)}, u32[]{:S(2)}, u32[]{:S(2)}) collective-permute-start(bf16[256,768]{1,0:T(8,128)(2,1)S(1)} %get-tuple-element.51), channel_id=1, source_target_pairs={{0,1},{1,0},{2,3},{3,2},{4,5},{5,4},{6,7},{7,6},{8,9},{9,8},{10,11... | collective-permute-start | bytes 1179656 | tf_op jit(solution)/shard_map/ppermute | solution.py:1581
  210.3 33.0 %copy-start = (bf16[1,256,768]{2,1,0:T(8,128)(2,1)S(1)}, bf16[1,256,768]{2,1,0:T(8,128)(2,1)}, u32[]{:S(2)}) copy-start(bf16[1,256,768]{2,1,0:T(8,128)(2,1)} %get-tuple-element.52) | copy-start | bytes 1179652

commit v6 on v5

--- a/solution.py
+++ b/solution.py
@@ -381,16 +381,15 @@
 
 
 def forward_kernel(
-    stages, p_hbm, xin, cot, cnt, features, coord_row, coord_col, pick, keep,
+    stages, p_hbm, xin, cot, mask, features, coord_row, coord_col, pick, keep,
     wall_out, cdoc_out, total, rounded_out, qkv_out, probs_out, mixed_out, one_out, inverse_one, low_out, hidden_out,
     slope_out, two_out, inverse_two, layer_out,
-    flat, wall, xs, cs, cnt_slots, start, up_bias, acc, indices, short, rounded, qkv, probs, mixed, normed, low, hidden,
+    flat, wall, xs, cs, masked, cnt_slots, start, up_bias, acc, indices, short, rounded, qkv, probs, mixed, normed, low, hidden,
     slope, layer,
     in_sem, x_send, x_recv, c_send, c_recv, act_send, act_recv, n_send, n_recv, out_sem, probs_sem, feed_sem, *stage_sems,
 ):
     net = Gather(stages, wall, x_send, x_recv, c_send, c_recv, stage_sems)
     dp, fs, other = net.dp, net.fs, net.other
-    half = LEN // 2
     pieces = 8
     span = FLAT // pieces
     loads = [
@@ -417,11 +416,28 @@
         return carry
 
     lax.fori_loop(0, LEN // 8, index_rows, 0, unroll=4)
+
+    half = LEN // 2
+    square = [lax.broadcasted_iota(jnp.int32, (half, half), axis) for axis in range(2)]
+
+    def masked_rows(which):
+        row = jnp.broadcast_to(mask[pl.ds(which, 1), :], (half, half))
+        column = nn(
+            jnp.where((square[0] == square[1]) & (row > 0), 1.0, 0.0).astype(BF16), jnp.ones((half, 128), BF16)
+        )
+        return (cot[which].astype(F32) * jnp.concatenate([column] * 6, axis=1)).astype(BF16)
+
+    masked[...] = masked_rows(other)
+    cs[pl.ds(fs * half, half), :] = masked_rows(fs)
+    xs[pl.ds(fs * half, half), :] = xin[fs]
+    marks = jnp.sum(mask[...].astype(F32), axis=0, keepdims=True)
+    total[...] = jnp.broadcast_to(jnp.sum(marks, axis=1, keepdims=True), (8, 128))
     greet_wait(stages)
 
-    def act_copy(number, source, target, receive):
+    def act_copy(number, receive):
         where = rows_at((other if receive else fs) * half, half)
-        return remote(source.at[other], target.at[where], act_send.at[number], act_recv.at[number], net.x_peer)
+        source, target = ((xin.at[other], xs), (masked, cs))[number]
+        return remote(source, target.at[where], act_send.at[number], act_recv.at[number], net.x_peer)
 
     rounds = [
         [
@@ -450,7 +466,6 @@
             for copy in count_copies(number):
                 copy.start()
 
-    total[...] = cnt[...]
     count_round(0)
     for load in loads:
         load.wait()
@@ -477,10 +492,8 @@
                 relayout(plane, flat, wall, group)
 
         net.send(low_at, high_at)
-    act_copy(0, xin, xs, False).start()
+    act_copy(0, False).start()
     net.send(CHUNKS - 3, CHUNKS)
-    xs[pl.ds(fs * half, half), :] = xin[fs]
-    cs[pl.ds(fs * half, half), :] = cot[fs]
     count_round(1)
 
     count_round(2)
@@ -522,7 +535,7 @@
 
     lax.fori_loop(0, LEN // 32, bias_rows, 0)
 
-    act_copy(1, cot, cs, False).start()
+    act_copy(1, False).start()
     count_round(3)
     lag = SKEW * (net.levels + 1)
 
@@ -534,7 +547,7 @@
     qv_bias = row_of(small0, 0, 12)
     out_bias, gain_one, shift_one = (row_of(small0, 20 + 6 * i, 6) for i in range(3))
     down_bias, gain_two, shift_two = (row_of(small1, 38 + 6 * i, 6) for i in range(3))
-    act_copy(0, xin, xs, True).wait_recv()
+    act_copy(0, True).wait_recv()
 
     w_layout = jnp.concatenate([wall[1, pl.ds(LAY1 + c * FEAT, FEAT), :] for c in range(6)], axis=1)
 
@@ -653,10 +666,10 @@
     lax.fori_loop(0, LEN // QROWS, second_rows, 0)
     put(acc, two_out)
     put(layer, layer_out)
-    act_copy(1, cot, cs, True).wait_recv()
+    act_copy(1, True).wait_recv()
     put(cs, cdoc_out)
     for number in range(2):
-        act_copy(number, (xin, cot)[number], (xs, cs)[number], False).wait_send()
+        act_copy(number, False).wait_send()
     short_copy(fs).wait_send()
     for pair in range(PAIRS):
         probs_copy(pair).wait()
@@ -671,7 +684,7 @@
     lax.fori_loop(0, 12, feed_wait, 0)
 
 
-def forward_pass(stages, p2, xin, cot, cnt, features, coord_row, coord_col):
+def forward_pass(stages, p2, xin, cot, mask, features, coord_row, coord_col):
     pick, keep = table_constants()
     sds = jax.ShapeDtypeStruct
     dma = pltpu.SemaphoreType.DMA
@@ -706,6 +719,7 @@
             pltpu.VMEM((2, ROWS, 128), BF16),
             pltpu.VMEM((LEN, D), BF16),
             pltpu.VMEM((LEN, D), BF16),
+            pltpu.VMEM((LEN // 2, D), BF16),
             pltpu.VMEM((count_peers, 8, 128), F32),
             pltpu.VMEM((LEN, D), F32),
             pltpu.VMEM((1, FF), F32),
@@ -728,7 +742,7 @@
         compiler_params=pltpu.CompilerParams(
             collective_id=1, has_side_effects=True, vmem_limit_bytes=64 * 2**20 - 2**16
         ),
-    )(p2, xin, cot, cnt, features, coord_row, coord_col, jnp.asarray(pick), jnp.asarray(keep))
+    )(p2, xin, cot, mask, features, coord_row, coord_col, jnp.asarray(pick), jnp.asarray(keep))
 
 
 G_SMALL = (("qv_bias", 0, 0, 12), ("out_bias", 0, 12, 6), ("gain_one", 0, 18, 6), ("shift_one", 0, 24, 6),
@@ -951,11 +965,11 @@
 
 def backward_kernel(
     stages,
-    wall_hbm, cdoc_hbm, total, rounded_hbm, qkv_hbm, probs_hbm, mixed_hbm, one_hbm, inverse_one, low_hbm, hidden_hbm,
+    wall_hbm, cdoc_hbm, total, layer_hbm, rounded_hbm, qkv_hbm, probs_hbm, mixed_hbm, one_hbm, inverse_one, low_hbm, hidden_hbm,
     slope_hbm, two_hbm, inverse_two, features, coord_row, coord_col, pick, keep,
-    input_grad, reduced, tables, norm,
+    layer_out, input_grad, reduced, tables, norm,
     wall, gstack, acc, branch, hidden, d_up, low, rounded, qkv, mixed, normed_one, places, lut, ranks, small,
-    square_slots, load_sem, step_sem, probs_sem, act_sem, n_send, n_recv, *rest,
+    square_slots, load_sem, step_sem, probs_sem, act_send, act_recv, act_sem, n_send, n_recv, *rest,
 ):
     levels = len(stages)
     parts_vmem, sems = rest[: 3 + levels], rest[3 + levels :]
@@ -967,13 +981,24 @@
         pltpu.make_async_copy(cdoc_hbm, branch, load_sem.at[1]),
         pltpu.make_async_copy(two_hbm, acc, load_sem.at[2]),
     ]
+    early.append(pltpu.make_async_copy(layer_hbm, rounded, load_sem.at[9]))
     lows = [pltpu.make_async_copy(low_hbm, low, load_sem.at[3])]
+    rounded_load = pltpu.make_async_copy(rounded_hbm, rounded, load_sem.at[8])
+
+    half = LEN // 2
+
+    def out_copies(number, source, target, receive):
+        moved = remote(
+            source.at[rows_at(other * half, half)], target.at[other if receive else fs],
+            act_send.at[number], act_recv.at[number], red.x_peer,
+        )
+        own = pltpu.make_async_copy(source.at[rows_at(fs * half, half)], target.at[fs], act_sem.at[number])
+        return moved, own
     rest_loads = [
         pltpu.make_async_copy(one_hbm, normed_one, load_sem.at[4]),
         pltpu.make_async_copy(wall_hbm.at[0, pl.ds(0, UP0)], wall.at[0, pl.ds(0, UP0)], load_sem.at[5]),
         pltpu.make_async_copy(mixed_hbm, mixed, load_sem.at[6]),
         pltpu.make_async_copy(qkv_hbm, qkv, load_sem.at[7]),
-        pltpu.make_async_copy(rounded_hbm, rounded, load_sem.at[8]),
     ]
 
     def step_loads(j):
@@ -1007,6 +1032,8 @@
     for load in early:
         load.wait()
 
+    for copy in out_copies(0, rounded, layer_out, False):
+        copy.start()
     small0 = wall[0, pl.ds(SM0, 48), :].astype(F32)
     small1 = wall[1, pl.ds(SM1, 80), :].astype(F32)
     gain_one = row_of(small0, 26, 6)
@@ -1097,6 +1124,10 @@
     red.tick(1)
     for load in rest_loads:
         load.wait()
+    layer_moved, layer_own = out_copies(0, rounded, layer_out, False)
+    layer_moved.wait_send()
+    layer_own.wait()
+    rounded_load.start()
 
     w_out = jnp.concatenate([wall[0, pl.ds(OUT0 + c * D, D), :] for c in range(6)], axis=1)
 
@@ -1136,6 +1167,7 @@
         red.tick(3)
         begun = 4
 
+    rounded_load.wait()
     left = lax.broadcasted_iota(jnp.int32, (LEN, 128), 1) < HDIM
 
     def sent(it):
@@ -1205,8 +1237,6 @@
         red.push(sent(3), sent(4))
 
     branch[...] = acc[...].astype(BF16)
-    act_out = pltpu.make_async_copy(branch, input_grad, act_sem.at[0])
-    act_out.start()
     layout = tn(features[...], branch[...]).astype(BF16)
     for c in range(6):
         gstack[1, pl.ds(LAY1 + c * FEAT, FEAT), :] = layout[:, c * 128 : (c + 1) * 128]
@@ -1222,6 +1252,8 @@
         red.feed(plane, last, last + 1)
     drain(late, 0)
     red.push(last, last + 1)
+    for copy in out_copies(1, branch, input_grad, False):
+        copy.start()
     late += 1
     summed = red.count + SKEW * levels
     passed = [late]
@@ -1280,10 +1312,14 @@
             tables[...] = gathered
     gathered = tables[0:9, :]
     gathered = jnp.sum(jnp.sum(gathered * gathered, axis=0, keepdims=True), axis=1, keepdims=True)
-    norm[...] = jnp.broadcast_to(jnp.sqrt(tables[9:10, :] + gathered), (8, 128))
+    norm[...] = jnp.sqrt(tables[9:10, 0:1] + gathered)
 
     red.finish()
-    act_out.wait()
+    grad_moved, grad_own = out_copies(1, branch, input_grad, False)
+    grad_moved.wait_send()
+    grad_own.wait()
+    out_copies(0, rounded, layer_out, True)[0].wait_recv()
+    out_copies(1, branch, input_grad, True)[0].wait_recv()
 
 
 def table_grads(wall, coord_col, pick, keep, less, places, ranks, prefix, tables, red, late, pace, summed):
@@ -1367,7 +1403,7 @@
             tables[3 * table + i : 3 * table + i + 1, :] = flat_row[:, i * 128 : (i + 1) * 128]
 
 
-def backward_pass(stages, wall, cdoc, total, saved, features, coord_row, coord_col):
+def backward_pass(stages, wall, cdoc, total, out_doc, saved, features, coord_row, coord_col):
     pick, keep = table_constants()
     sds = jax.ShapeDtypeStruct
     count_peers = 2 + sum(radix - 1 for radix, _ in stages)
@@ -1376,9 +1412,9 @@
     return pl.pallas_call(
         functools.partial(backward_kernel, stages),
         name="backward_reduce",
-        out_shape=(sds((LEN, D), BF16), sds((ROWS, 128), BF16), sds((16, 128), F32), sds((8, 128), F32)),
-        in_specs=[ANY, ANY, VMEM, ANY, ANY, ANY, ANY, ANY, VMEM, ANY, ANY, ANY, ANY, VMEM] + [VMEM] * 5,
-        out_specs=(ANY, ANY, VMEM, VMEM),
+        out_shape=(sds((2, LEN // 2, D), BF16), sds((2, LEN // 2, D), BF16), sds((ROWS, 128), BF16), sds((16, 128), F32), sds((1, 1), F32)),
+        in_specs=[ANY, ANY, VMEM, ANY, ANY, ANY, ANY, ANY, ANY, VMEM, ANY, ANY, ANY, ANY, VMEM] + [VMEM] * 5,
+        out_specs=(ANY, ANY, ANY, VMEM, VMEM),
         scratch_shapes=[
             pltpu.VMEM((2, ROWS, 128), BF16),
             pltpu.VMEM((2, ROWS, 128), BF16),
@@ -1396,14 +1432,14 @@
             pltpu.VMEM((2, LEN, 128), F32),
             pltpu.VMEM((2, 64, 128), F32),
             pltpu.VMEM((count_peers, 16, 128), F32),
-            dma((10,)), dma((5, 12)), dma((2,)), dma((1,)), dma((count_peers,)), dma((count_peers,)),
+            dma((10,)), dma((5, 12)), dma((2,)), dma((2,)), dma((2,)), dma((2,)), dma((count_peers,)), dma((count_peers,)),
         ]
         + buffers
         + sems,
         compiler_params=pltpu.CompilerParams(
             collective_id=2, has_side_effects=True, vmem_limit_bytes=64 * 2**20 - 2**16
         ),
-    )(wall, cdoc, total, *saved, features, coord_row, coord_col, jnp.asarray(pick), jnp.asarray(keep))
+    )(wall, cdoc, total, out_doc, *saved, features, coord_row, coord_col, jnp.asarray(pick), jnp.asarray(keep))
 
 
 BLOCK = 1408
@@ -1560,8 +1596,6 @@
 
 def local(stages, inputs, box_coords, mlm_mask, cotangent, params, first_moment, second_moment):
     fs = lax.axis_index("fsdp")
-    masked = cotangent * mlm_mask.astype(BF16)[..., None]
-    count = jnp.full((8, 128), jnp.sum(mlm_mask.astype(F32)))
     boxes = lax.dynamic_index_in_dim(box_coords, fs, 0, keepdims=False)
     features = layout_features(boxes).astype(BF16)
     coord_col = jnp.stack(
@@ -1570,30 +1604,13 @@
     coord_row = coord_col.T
     flat = [v.reshape(FLAT, 128) for v in (params, first_moment, second_moment)]
     wall, cdoc, total, *saved, out_doc = forward_pass(
-        stages, flat[0], inputs, masked, count, features, coord_row, coord_col
+        stages, flat[0], inputs, cotangent, mlm_mask, features, coord_row, coord_col
     )
-    grad_doc, reduced, tables, norm = backward_pass(
-        stages, wall, cdoc, total, saved, features, coord_row, coord_col
+    layer_out, input_grad, reduced, tables, norm = backward_pass(
+        stages, wall, cdoc, total, out_doc, saved, features, coord_row, coord_col
     )
-    half = LEN // 2
-
-    def moved(doc):
-        return lax.ppermute(lax.dynamic_slice_in_dim(doc, (1 - fs) * half, half, 0), "fsdp", [(0, 1), (1, 0)])
-
-    def owned(doc, other):
-        mine = lax.dynamic_slice_in_dim(doc, fs * half, half, 0)
-        return jnp.where(fs == 0, jnp.stack([mine, other]), jnp.stack([other, mine]))
-
-    out_other, grad_other = moved(out_doc), moved(grad_doc)
     grad, update, new_first = adam(reduced, tables, *flat)
-    return (
-        owned(out_doc, out_other),
-        owned(grad_doc, grad_other),
-        grad.reshape(-1),
-        norm[0, 0],
-        update.reshape(-1),
-        new_first.reshape(-1),
-    )
+    return (layer_out, input_grad, grad.reshape(-1), norm.reshape(()), update.reshape(-1), new_first.reshape(-1))
 
 
 def solution(mesh):

time: 247 us -> 235 us (0.951)
  other arithmetic: 8.47 us -> 1.23 us
  starting transfers between devices: 3.89 us -> 0 us
  local copies, waits for them, and re-layouts: 7.98 us -> 4.1 us
    ppermute x2 -> x0, starting transfers between devices: 3.89 us -> none  [moved(): lax.ppermute(lax.dynamic_slice_in_dim(doc, (1 - fs) * half, half, 0), 'fs...]
    another operation x2 -> x0, local copies, waits for them, and re-layouts: 3.23 us -> none  [owned(): jnp.stack([mine, other])]
    select_n x2 -> x0, other arithmetic: 3.12 us -> none  [owned(): jnp.where(fs == 0, jnp.stack([mine, other]), jnp.stack([other, mine]))]
  transfers between devices with their start and end apart: 2 -> 0, of which waited for: 0 -> 0; matrix products, arithmetic and copies ran while one was open for 2% -> 0% of each run, Pallas kernels for 64% -> 0%
where the time goes in v6:
time: 235 us; the launch traced here: 234 us
  Pallas kernels  227 us (97%)
  local copies, waits for them, and re-layouts  4.1 us (2%)
  between operations  2.52 us (1%)
    pallas_call x1, Pallas kernels, backward_pass(): pl.pallas_call(functools.partial(backward_kernel, stages), name='backward...  125 us
    pallas_call x1, Pallas kernels, forward_pass(): pl.pallas_call(functools.partial(forward_kernel, stages), name='gather_fo...  68.5 us
    pallas_call x1, Pallas kernels, adam(): pl.pallas_call(adam_kernel, name='adamw', out_shape=(vector, vector, vect...  33 us

profile of v6, /device:TPU:0, one launch (start us, length us, event | category | flops | bytes accessed | tf_op | source)
XLA Modules:
  0.0 234.3 jit_solution(5772734669232610743)
XLA Ops:
  0.7 0.7 dynamic-slice_bitcast_fusion
  1.4 0.6 pad_add_fusion
  2.0 0.6 sine_convert_fusion
  2.6 0.8 copy.26.features
  3.4 0.9 copy.27.coord_col
  4.2 68.5 %gather_forward.1 = (bf16[2,28672,128]{2,1,0:T(8,128)(2,1)}, bf16[512,768]{1,0:T(8,128)(2,1)}, f32[8,128]{1,0:T(8,128)}, bf16[512,768]{1,0:T(8,128)(2,1)}, bf16[...) custom-call(f32[28160,128]{1,0:T(8,128)} %bitcast.12, ...), custom_call_target="tpu_custom_call" | custom-call | tf_op jit(solution)/shard_map/gather_forward/pallas_call | solution.py:695
  72.7 125.0 %backward_reduce.1 = (bf16[2,256,768]{2,1,0:T(8,128)(2,1)}, bf16[2,256,768]{2,1,0:T(8,128)(2,1)}, bf16[28672,128]{1,0:T(8,128)(2,1)}, f32[16,128]{1,0:T(8,128)}, f32[1,1]{1,0:T(1,128)}) custom-call(bf16[2,28672,128]{2,1,0:T(8,128)(2,1)} %get-tuple-element.29.wall_hbm, bf16[512,768]{1,0:T(8,128)(2,1)} %get-tuple-element.30.cdoc_hbm, ...), custom_call_target="tpu_custom_call" | custom-call | tf_op jit(solution)/shard_map/backward_reduce/pallas_call | solution.py:1412
  197.7 0.0 copy-start.1
  197.7 0.0 copy-start
  197.7 33.0 %adamw.1 = (f32[28160,128]{1,0:T(8,128)}, f32[28160,128]{1,0:T(8,128)}, f32[28160,128]{1,0:T(8,128)}) custom-call(bf16[28672,128]{1,0:T(8,128)(2,1)} %get-tuple-element.46.source_hbm, f32[16,128]{1,0:T(8,128)} %get-tuple-element.47.tables, f32[28160,128]{1,0:T(8,128)} %bitcast.13, f32[28160,128]{1,0:T(8,128)} %bitcast.14, f32[28160,128]{1,0:T(8,128)} %bitcast.15), custom_call_target="tpu_custom_call" | custom-call | tf_op jit(solution)/shard_map/adamw/pallas_call | solution.py:1571
  230.8 0.0 copy-done.1
  230.8 0.9 copy.33
  231.7 0.0 copy-done
  231.7 0.9 copy.34
  (4 shorter events, 0.0 us)
Async XLA Ops:
  197.7 33.1 %copy-start.1 = (bf16[2,256,768]{2,1,0:T(8,128)(2,1)S(1)}, bf16[2,256,768]{2,1,0:T(8,128)(2,1)}, u32[]{:S(2)}) copy-start(bf16[2,256,768]{2,1,0:T(8,128)(2,1)} %get-tuple-element.64) | copy-start | bytes 2359300
  197.7 33.9 %copy-start = (bf16[2,256,768]{2,1,0:T(8,128)(2,1)S(1)}, bf16[2,256,768]{2,1,0:T(8,128)(2,1)}, u32[]{:S(2)}) copy-start(bf16[2,256,768]{2,1,0:T(8,128)(2,1)} %get-tuple-element.65) | copy-start | bytes 2359300

commit v7 on v6

--- a/solution.py
+++ b/solution.py
@@ -158,11 +158,15 @@
 
 
 def up_block(wall, j):
+    row = lax.broadcasted_iota(jnp.int32, (16, 128), 0)
     columns = []
     for c in (2 * j, 2 * j + 1):
-        first = wall[0, rows_at(UP0 + c * UP_A, UP_A), :]
+        first = wall[0, rows_at(UP0 + c * UP_A, UP_A - 16), :]
+        low = wall[0, rows_at(UP0 + c * UP_A + UP_A - 16, 16), :].astype(F32)
+        high = wall[1, rows_at(UP1 + c * UP_B, 16), :].astype(F32)
         second = wall[1, rows_at(UP1 + c * UP_B + 16, UP_B - 16), :]
-        columns.append(jnp.concatenate([first, second], axis=0))
+        cut = jnp.where(c < 2, CUT + 1 - 400, CUT - 400)
+        columns.append(jnp.concatenate([first, jnp.where(row < cut, low, high).astype(BF16), second], axis=0))
     return jnp.concatenate(columns, axis=1)
 
 
@@ -170,20 +174,6 @@
     return jnp.concatenate(
         [wall[1, rows_at(DOWN1 + j * 1536 + c * 256, 256), :] for c in range(6)], axis=1
     )
-
-
-def merge_up(wall):
-    row = lax.broadcasted_iota(jnp.int32, (16, 128), 0)
-
-    def one(c, carry):
-        low_at = rows_at(UP0 + c * UP_A + UP_A - 16, 16)
-        low = wall[0, low_at, :].astype(F32)
-        high = wall[1, rows_at(UP1 + c * UP_B, 16), :].astype(F32)
-        cut = jnp.where(c < 2, CUT + 1 - 400, CUT - 400)
-        wall[0, low_at, :] = jnp.where(row < cut, low, high).astype(BF16)
-        return carry
-
-    lax.fori_loop(0, 24, one, 0)
 
 
 def stats(values):
@@ -280,9 +270,16 @@
         self.parts = offsets(self.dp, stages, CHUNK)
         self.x_peer = (self.dp, self.other)
         self.core_peer = (self.dp + 1 - 2 * (self.dp % 2), self.fs)
+        self.partners = [
+            [
+                (member(self.dp, radix, stride, ((self.dp // stride) % radix + step) % radix), self.fs)
+                for step in range(1, radix)
+            ]
+            for radix, stride in stages
+        ]
 
     def base(self, position):
-        return lax.rem(CHUNKS - 1 + position, CHUNKS) * CHUNK
+        return jnp.where(position == 0, CHUNKS - 1, position - 1) * CHUNK
 
     def direct(self, position):
         return position >= CHUNKS - 3
@@ -309,17 +306,12 @@
         lax.fori_loop(low, high, one, 0)
 
     def stage_copies(self, level, position):
-        radix, stride = self.stages[level]
         start, size = self.parts[level + 1]
-        mine = (self.dp // stride) % radix
-        copies = []
-        for step in range(1, radix):
-            peer = (member(self.dp, radix, stride, (mine + step) % radix), self.fs)
-            where = self.zall.at[self.other, rows_at(self.base(position) + start, size)]
-            copies.append(
-                remote(where, where, self.sems[2 * level].at[0], self.sems[2 * level + 1].at[position], peer)
-            )
-        return copies
+        where = self.zall.at[self.other, rows_at(self.base(position) + start, size)]
+        return [
+            remote(where, where, self.sems[2 * level].at[0], self.sems[2 * level + 1].at[position], peer)
+            for peer in self.partners[level]
+        ]
 
     def stage_wait(self, level, position):
         size = (self.stages[level][0] - 1) * self.parts[level + 1][1]
@@ -330,7 +322,7 @@
 
     def core_copy(self, position, receive):
         size = CHUNK // 2
-        start = (1 - self.dp % 2 if receive else self.dp % 2) * size
+        start = size - self.parts[0][0] if receive else self.parts[0][0]
         where = self.zall.at[self.other, rows_at(self.base(position) + start, size)]
         return remote(where, where, self.c_send.at[0], self.c_recv.at[position], self.core_peer)
 
@@ -340,7 +332,7 @@
         if step == levels + 1:
             self.core_copy(position, True).wait_recv()
             return
-        if step == 0:
+        if step == levels:
 
             @pl.when(direct)
             def _():
@@ -504,6 +496,7 @@
         copy.start()
         outs.append(copy)
 
+    put(wall.at[fs], wall_out.at[fs])
     short_copy(other).wait_recv()
 
     small0, small1 = short[0].astype(F32), short[1].astype(F32)
@@ -626,10 +619,8 @@
     put(normed, one_out)
     put(low, low_out)
     count_round(5)
-    lax.fori_loop(10 + lag, net.ticks(), drain, 0)
-    net.finish()
-    merge_up(wall)
-    put(wall, wall_out)
+    lax.fori_loop(10 + lag, 11 + lag, drain, 0)
+    put(wall.at[other, pl.ds(0, UP0)], wall_out.at[other, pl.ds(0, UP0)])
     for j in range(12):
         up_bias[:, j * 256 : (j + 1) * 256] = row_of(small1, 6 + 2 * j, 2)
 
@@ -653,7 +644,18 @@
             copy.start()
         return carry
 
-    lax.fori_loop(0, 12, feed_step, 0, unroll=3)
+    def feed_group(group, carry):
+        @pl.when(group > 0)
+        def _():
+            net.tick(11 + lag + group)
+
+        for i in range(3):
+            feed_step(3 * group + i, carry)
+        return carry
+
+    net.tick(11 + lag)
+    lax.fori_loop(0, 4, feed_group, 0)
+    put(wall.at[other, pl.ds(UP0, ROWS - UP0)], wall_out.at[other, pl.ds(UP0, ROWS - UP0)])
 
     def second_rows(r, carry):
         at = pl.ds(pl.multiple_of(r * QROWS, QROWS), QROWS)
@@ -671,6 +673,7 @@
     for number in range(2):
         act_copy(number, False).wait_send()
     short_copy(fs).wait_send()
+    net.finish()
     for pair in range(PAIRS):
         probs_copy(pair).wait()
     for copy in outs:
@@ -784,15 +787,26 @@
         self.half = self.size // 2
         self.x_peer = (self.dp, self.other)
         self.core_peer = (self.dp + 1 - 2 * (self.dp % 2), self.fs)
+        self.core_start = (1 - self.dp % 2) * self.half
+        self.partners = []
+        for level, (radix, stride) in enumerate(stages):
+            mine = (self.dp // stride) % radix
+            start, size = self.parts[level][0], self.parts[level + 1][1]
+            found = []
+            for step in range(1, radix):
+                target = (mine + step) % radix
+                found.append((step, (member(self.dp, radix, stride, target), self.fs), start + target * size))
+            self.partners.append(found)
 
     def base(self, position):
-        return lax.rem(2 * self.count - 2 - position, self.count) * self.size
+        last = self.count - 1
+        return jnp.where(position == last, last, last - 1 - position) * self.size
 
     def ready(self, row):
         return jnp.maximum(self.count - 1 - (row + self.size - 1) // self.size, 0)
 
     def core_copy(self, position, plane):
-        where = rows_at(self.base(position) + (1 - self.dp % 2) * self.half, self.half)
+        where = rows_at(self.base(position) + self.core_start, self.half)
         return remote(
             self.gstack.at[plane, where], self.core_slots.at[plane, position],
             self.c_send.at[0], self.c_recv.at[plane, position], self.core_peer,
@@ -806,22 +820,15 @@
         )
 
     def scatter_copies(self, level, position):
-        radix, stride = self.stages[level]
-        start, size = self.parts[level]
-        size = size // radix
-        mine = (self.dp // stride) % radix
-        copies = []
-        for step in range(1, radix):
-            target = (mine + step) % radix
-            where = rows_at(self.base(position) + start + target * size, size)
-            copies.append(
-                remote(
-                    self.gstack.at[self.fs, where], self.slots[level].at[position, step - 1],
-                    self.sems[4 * level].at[0], self.sems[4 * level + 1].at[position],
-                    (member(self.dp, radix, stride, target), self.fs),
-                )
+        size = self.parts[level + 1][1]
+        base = self.base(position)
+        return [
+            remote(
+                self.gstack.at[self.fs, rows_at(base + start, size)], self.slots[level].at[position, step - 1],
+                self.sems[4 * level].at[0], self.sems[4 * level + 1].at[position], peer,
             )
-        return copies
+            for step, peer, start in self.partners[level]
+        ]
 
     def scatter_wait(self, level, position):
         where = self.slots[level].at[position]
@@ -835,21 +842,13 @@
         ).wait_recv()
 
     def spread_copies(self, level, position):
-        radix, stride = self.stages[level]
         start, size = self.parts[level + 1]
-        mine = (self.dp // stride) % radix
-        copies = []
-        for step in range(1, radix):
-            where = self.out.at[rows_at(self.base(position) + start, size)]
-            source = self.pieces.at[position] if level == self.levels - 1 else where
-            copies.append(
-                remote(
-                    source, where,
-                    self.sems[4 * level + 2].at[0], self.sems[4 * level + 3].at[position],
-                    (member(self.dp, radix, stride, (mine + step) % radix), self.fs),
-                )
-            )
-        return copies
+        where = self.out.at[rows_at(self.base(position) + start, size)]
+        source = self.pieces.at[position] if level == self.levels - 1 else where
+        return [
+            remote(source, where, self.sems[4 * level + 2].at[0], self.sems[4 * level + 3].at[position], peer)
+            for _, peer, _ in self.partners[level]
+        ]
 
     def own_copy(self, position):
         start, size = self.parts[-1]
@@ -859,9 +858,9 @@
         )
 
     def back_copy(self, position, receive):
-        start = (1 - self.dp % 2 if receive else self.dp % 2) * self.half
+        start = self.core_start if receive else self.parts[0][0]
         where = self.out.at[rows_at(self.base(position) + start, self.half)]
-        return remote(where, where, self.b_send.at[0], self.b_recv.at[position], self.core_peer)
+        return remote(where, where, self.b_send.at[0], self.b_recv.at[0], self.core_peer)
 
     def feed(self, plane, low, high):
         def one(position, carry):
@@ -929,11 +928,8 @@
         return self.count + 2 * SKEW * self.levels
 
     def finish(self):
-        def one(position, carry):
-            self.back_copy(position, True).wait_recv()
-            return carry
-
-        lax.fori_loop(0, self.count, one, 0)
+        where = self.out.at[pl.ds(0, self.count * self.half)]
+        remote(where, where, self.b_send.at[0], self.b_recv.at[0], self.core_peer).wait_recv()
         sent = [(self.c_send, 2 * self.half), (self.x_send, self.half), (self.b_send, self.half)]
         for level, (radix, _) in enumerate(self.stages):
             size = (radix - 1) * self.parts[level + 1][1]
@@ -959,7 +955,7 @@
             pltpu.VMEM((count, half, 128), BF16),
         ]
         + slots,
-        [dma((1,)), dma((2, count)), dma((1,)), dma((count,)), dma((1,)), dma((count,)), dma((count,))] + sems,
+        [dma((1,)), dma((2, count)), dma((1,)), dma((count,)), dma((1,)), dma((1,)), dma((count,))] + sems,
     )
 
 
@@ -1006,13 +1002,17 @@
         areas = [(1, DOWN1 + 1536 * j, 1536), (0, UP0 + 2 * UP_A * j, 2 * UP_A), (1, UP1 + 2 * UP_B * j, 2 * UP_B)]
         copies = [
             pltpu.make_async_copy(
-                wall_hbm.at[plane, rows_at(start, size)], wall.at[plane, rows_at(start, size)], step_sem.at[i, j]
+                wall_hbm.at[plane, rows_at(start, size)], wall.at[plane, rows_at(start, size)], step_sem.at[j]
             )
-            for i, (plane, start, size) in enumerate(areas)
+            for plane, start, size in areas
         ]
-        copies.append(pltpu.make_async_copy(hidden_hbm.at[:, lanes], hidden.at[:, lanes], step_sem.at[3, j]))
-        copies.append(pltpu.make_async_copy(slope_hbm.at[:, lanes], d_up.at[:, lanes], step_sem.at[4, j]))
+        copies.append(pltpu.make_async_copy(hidden_hbm.at[:, lanes], hidden.at[:, lanes], step_sem.at[j]))
+        copies.append(pltpu.make_async_copy(slope_hbm.at[:, lanes], d_up.at[:, lanes], step_sem.at[j]))
         return copies
+
+    def step_wait(j):
+        where = pl.ds(0, 1536 + 2 * UP_A + 2 * UP_B + 2 * 2 * LEN)
+        pltpu.make_async_copy(wall_hbm.at[0, where], wall.at[0, where], step_sem.at[j]).wait()
 
     for load in early + lows:
         load.start()
@@ -1076,8 +1076,7 @@
 
     def feed_step(it, carry):
         j = 11 - it
-        for load in step_loads(j):
-            load.wait()
+        step_wait(j)
         for plane in range(2):
             red.feed(plane, fed(plane, it - 2), fed(plane, it - 1))
         red.push(of_other([fed(p, it - 3) for p in range(2)]), of_other([fed(p, it - 2) for p in range(2)]))
@@ -1432,7 +1431,7 @@
             pltpu.VMEM((2, LEN, 128), F32),
             pltpu.VMEM((2, 64, 128), F32),
             pltpu.VMEM((count_peers, 16, 128), F32),
-            dma((10,)), dma((5, 12)), dma((2,)), dma((2,)), dma((2,)), dma((2,)), dma((count_peers,)), dma((count_peers,)),
+            dma((10,)), dma((12,)), dma((2,)), dma((2,)), dma((2,)), dma((2,)), dma((count_peers,)), dma((count_peers,)),
         ]
         + buffers
         + sems,

time: 235 us -> 234 us (level)
  no operation moved by 1% of the time
where the time goes in v7:
time: 234 us; the launch traced here: 233 us
  Pallas kernels  225 us (96%)
  local copies, waits for them, and re-layouts  4.1 us (2%)
  between operations  2.52 us (1%)
    pallas_call x1, Pallas kernels, backward_pass(): pl.pallas_call(functools.partial(backward_kernel, stages), name='backward...  124 us
    pallas_call x1, Pallas kernels, forward_pass(): pl.pallas_call(functools.partial(forward_kernel, stages), name='gather_fo...  68.3 us
    pallas_call x1, Pallas kernels, adam(): pl.pallas_call(adam_kernel, name='adamw', out_shape=(vector, vector, vect...  33 us

profile of v7, /device:TPU:0, one launch (start us, length us, event | category | flops | bytes accessed | tf_op | source)
XLA Modules:
  0.0 233.2 jit_solution(3251639738976844888)
XLA Ops:
  0.7 0.7 dynamic-slice_bitcast_fusion
  1.4 0.6 pad_add_fusion
  2.0 0.6 sine_convert_fusion
  2.6 0.8 copy.26.features
  3.4 0.9 copy.27.coord_col
  4.2 68.3 %gather_forward.1 = (bf16[2,28672,128]{2,1,0:T(8,128)(2,1)}, bf16[512,768]{1,0:T(8,128)(2,1)}, f32[8,128]{1,0:T(8,128)}, bf16[512,768]{1,0:T(8,128)(2,1)}, bf16[...) custom-call(f32[28160,128]{1,0:T(8,128)} %bitcast.12, ...), custom_call_target="tpu_custom_call" | custom-call | tf_op jit(solution)/shard_map/gather_forward/pallas_call | solution.py:698
  72.5 124.1 %backward_reduce.1 = (bf16[2,256,768]{2,1,0:T(8,128)(2,1)}, bf16[2,256,768]{2,1,0:T(8,128)(2,1)}, bf16[28672,128]{1,0:T(8,128)(2,1)}, f32[16,128]{1,0:T(8,128)}, f32[1,1]{1,0:T(1,128)}) custom-call(bf16[2,28672,128]{2,1,0:T(8,128)(2,1)} %get-tuple-element.29.wall_hbm, bf16[512,768]{1,0:T(8,128)(2,1)} %get-tuple-element.30.cdoc_hbm, ...), custom_call_target="tpu_custom_call" | custom-call | tf_op jit(solution)/shard_map/backward_reduce/pallas_call | solution.py:1411
  196.6 0.0 copy-start.1
  196.6 0.0 copy-start
  196.6 33.0 %adamw.1 = (f32[28160,128]{1,0:T(8,128)}, f32[28160,128]{1,0:T(8,128)}, f32[28160,128]{1,0:T(8,128)}) custom-call(bf16[28672,128]{1,0:T(8,128)(2,1)} %get-tuple-element.46.source_hbm, f32[16,128]{1,0:T(8,128)} %get-tuple-element.47.tables, f32[28160,128]{1,0:T(8,128)} %bitcast.13, f32[28160,128]{1,0:T(8,128)} %bitcast.14, f32[28160,128]{1,0:T(8,128)} %bitcast.15), custom_call_target="tpu_custom_call" | custom-call | tf_op jit(solution)/shard_map/adamw/pallas_call | solution.py:1570
  229.7 0.0 copy-done.1
  229.7 0.9 copy.33
  230.6 0.0 copy-done
  230.6 0.9 copy.34
  (4 shorter events, 0.0 us)
Async XLA Ops:
  196.6 33.1 %copy-start.1 = (bf16[2,256,768]{2,1,0:T(8,128)(2,1)S(1)}, bf16[2,256,768]{2,1,0:T(8,128)(2,1)}, u32[]{:S(2)}) copy-start(bf16[2,256,768]{2,1,0:T(8,128)(2,1)} %get-tuple-element.64) | copy-start | bytes 2359300
  196.6 33.9 %copy-start = (bf16[2,256,768]{2,1,0:T(8,128)(2,1)S(1)}, bf16[2,256,768]{2,1,0:T(8,128)(2,1)}, u32[]{:S(2)}) copy-start(bf16[2,256,768]{2,1,0:T(8,128)(2,1)} %get-tuple-element.65) | copy-start | bytes 2359300
